TPU v7x, 32 devices: a whole 2x2x4 slice. The times are simulated.
32 devices in a mesh: fsdp: 8 (over z, core), cp: 4 (over y, x).
Axes of the slice: x: 2, y: 2, z: 4, core: 2. Of those that a mesh axis runs over, the one named last changes fastest.
Arguments:
- layer_input: bfloat16 [16, 4, 2, 128, 1536], P('fsdp', 'cp'), may hold values from -6 to 6
- cotangent: bfloat16 [16, 4, 2, 128, 1536], P('fsdp', 'cp'), may hold values from -6 to 6
- pairing: int32 [16, 4], P('fsdp'), may hold values from 0 to 3, each once within a row
- routes: int32 [16, 4, 2, 128, 2], P('fsdp', 'cp'), may hold values from 0 to 15, all different within a row; in each aligned block of 256 rows (0 to 255, 256 to 511, ..., all dimensions but the last counted through in order) at most 48 rows name the same one
- first_gain: bfloat16 [1536], P(('fsdp', 'cp')), may hold values from 0.5 to 1.5
- second_gain: bfloat16 [1536], P(('fsdp', 'cp')), may hold values from 0.5 to 1.5
- query_weight: bfloat16 [1536, 1536], P(('fsdp', 'cp')), may hold values from -0.15625 to 0.15625
- key_weight: bfloat16 [1536, 512], P(('fsdp', 'cp')), may hold values from -0.15625 to 0.15625
- value_weight: bfloat16 [1536, 512], P(('fsdp', 'cp')), may hold values from -0.15625 to 0.15625
- out_weight: bfloat16 [1536, 1536], P(('fsdp', 'cp')), may hold values from -1.75 to 1.75
- router_weight: bfloat16 [1536, 16], P(('fsdp', 'cp')), may hold values from -0.109375 to 0.109375
- gate_weight: bfloat16 [16, 1536, 1024], P('cp', 'fsdp'), may hold values from -0.15625 to 0.15625
- up_weight: bfloat16 [16, 1536, 1024], P('cp', 'fsdp'), may hold values from -0.15625 to 0.15625
- down_weight: bfloat16 [16, 1024, 1536], P('cp', 'fsdp'), may hold values from -0.375 to 0.375
Outputs:
- layer_output: bfloat16 [16, 4, 2, 128, 1536], P('fsdp', 'cp')
- input_grad: float32 [16, 4, 2, 128, 1536], P('fsdp', 'cp')
- first_gain_grad: float32 [1536], P(('fsdp', 'cp'))
- second_gain_grad: float32 [1536], P(('fsdp', 'cp'))
- query_grad: float32 [1536, 1536], P(('fsdp', 'cp'))
- key_grad: float32 [1536, 512], P(('fsdp', 'cp'))
- value_grad: float32 [1536, 512], P(('fsdp', 'cp'))
- out_grad: float32 [1536, 1536], P(('fsdp', 'cp'))
- router_grad: float32 [1536, 16], P(('fsdp', 'cp'))
- gate_grad: float32 [16, 1536, 1024], P('cp', 'fsdp')
- up_grad: float32 [16, 1536, 1024], P('cp', 'fsdp')
- down_grad: float32 [16, 1024, 1536], P('cp', 'fsdp')
Inputs may be any that keep to these rules, and one draw needn't show every extreme that they name: Each row is a permutation of the indices of cp; index c of cp holds block pairing[s, c] and block 7 - pairing[s, c] of sequence s. `routes`: the two experts of a token differ. Among the 256 tokens that one index of cp holds of one sequence, no expert is named more than 48 times, a bound that some block reaches.
All inputs are finite; a program needn't handle non-finite values.
Results may differ from a plain program's by a relative error of at most 0.018.
Values may be sent and summed in bfloat16 or wider, within the bound.
A program may use at most 384 MiB of HBM per device.

v0:
```python
import jax
import jax.numpy as jnp
from jax import lax
from jax.sharding import PartitionSpec as P

H = 24
KV = 8
HD = 64
EXPERTS = 16
BLK = 128
CAP = 48


EPS = 1e-05
NEG = -1e30
HIGH = lax.Precision.HIGHEST


def for_sending(x):
    return jax.tree.map(lambda a: a.astype(jnp.bfloat16) if a.dtype == jnp.float32 else a, x)


def rms_forward(rows, gain):
    scale = lax.rsqrt(jnp.mean(rows * rows, axis=-1, keepdims=True) + EPS)
    return (rows * scale * gain, scale)


def rms_backward(rows, scale, gain, grad_norm):
    weighted = grad_norm * gain
    inner = jnp.mean(weighted * rows, axis=-1, keepdims=True)
    grad_rows = scale * weighted - rows * scale * scale * scale * inner
    return (grad_rows, jnp.sum(grad_norm * rows * scale, axis=0))


def positions(pair_row, context, block):
    blocks = jnp.stack([pair_row, 2 * context - 1 - pair_row], axis=1)
    offsets = jnp.arange(block, dtype=jnp.int32)
    return (blocks[:, :, None] * block + offsets[None, None, :]).reshape(-1)


def slot_table(chosen, experts, capacity):
    flat = chosen.reshape(-1)
    onehot = (flat[:, None] == jnp.arange(experts, dtype=jnp.int32)[None, :]).astype(jnp.int32)
    before = jnp.cumsum(onehot, axis=0) - onehot
    return flat * capacity + jnp.sum(before * onehot, axis=1)


def micro_batch(dense, expert_mats, inputs):
    gain_one, gain_two, query_matrix, key_matrix, value_matrix, out_matrix, router_matrix = dense
    gate_matrix, up_matrix, down_matrix = expert_mats
    source, grad_out, pair_row, route_rows = inputs
    context = lax.axis_size("cp")
    here = lax.axis_index("cp")
    width = source.shape[-1]
    rows = 2 * BLK
    seq_len = rows * context
    group = H // KV
    scale = HD ** (-0.5)
    experts_here = gate_matrix.shape[0]
    gain_one = gain_one.astype(jnp.float32)
    gain_two = gain_two.astype(jnp.float32)
    key_places = positions(pair_row, context, BLK)
    query_places = lax.dynamic_slice_in_dim(key_places, here * rows, rows)
    allowed = key_places[None, :] <= query_places[:, None]
    resid = source.reshape(rows, width).astype(jnp.float32)
    normed_one, scale_one = rms_forward(resid, gain_one)
    attn_in = normed_one.astype(jnp.bfloat16)
    queries = jnp.dot(attn_in, query_matrix, preferred_element_type=jnp.float32).astype(
        jnp.bfloat16
    )
    keys = jnp.dot(attn_in, key_matrix, preferred_element_type=jnp.float32).astype(jnp.bfloat16)
    values = jnp.dot(attn_in, value_matrix, preferred_element_type=jnp.float32).astype(jnp.bfloat16)
    keys_all, values_all = (
        lax.all_gather(keys, "cp", axis=0, tiled=True),
        lax.all_gather(values, "cp", axis=0, tiled=True),
    )
    query_groups = queries.reshape(rows, KV, group, HD).transpose(1, 2, 0, 3)
    key_groups = keys_all.reshape(seq_len, KV, HD).transpose(1, 0, 2)
    value_groups = values_all.reshape(seq_len, KV, HD).transpose(1, 0, 2)

    def attend(operands):
        query_g, key_g, value_g = operands
        scores = (
            jnp.einsum("grd,ld->grl", query_g, key_g, preferred_element_type=jnp.float32) * scale
        )
        scores = jnp.where(allowed[None], scores, NEG)
        peak = jnp.max(scores, axis=-1, keepdims=True)
        powers = jnp.exp(scores - peak)
        total = jnp.sum(powers, axis=-1, keepdims=True)
        probs = (powers / total).astype(jnp.bfloat16)
        mixed = jnp.einsum("grl,ld->grd", probs, value_g, preferred_element_type=jnp.float32)
        return (mixed, (peak + jnp.log(total))[..., 0])

    mixed, log_total = lax.map(attend, (query_groups, key_groups, value_groups))
    attn_out = mixed.transpose(2, 0, 1, 3).reshape(rows, H * HD).astype(jnp.bfloat16)
    middle = resid + jnp.dot(attn_out, out_matrix, preferred_element_type=jnp.float32)
    normed_two, scale_two = rms_forward(middle, gain_two)
    moe_in = normed_two.astype(jnp.bfloat16)
    logits = jnp.dot(moe_in, router_matrix, preferred_element_type=jnp.float32)
    chosen = route_rows.reshape(rows, 2)
    picks = (chosen[:, :, None] == jnp.arange(EXPERTS, dtype=jnp.int32)[None, None, :]).astype(
        jnp.float32
    )
    picked = jnp.sum(picks * logits[:, None, :], axis=-1)
    top = jnp.max(picked, axis=-1, keepdims=True)
    powers = jnp.exp(picked - top)
    gates = powers / jnp.sum(powers, axis=-1, keepdims=True)
    slots = slot_table(chosen, EXPERTS, CAP)
    send = (
        jnp.zeros((EXPERTS * CAP, width), jnp.bfloat16).at[slots].set(jnp.repeat(moe_in, 2, axis=0))
    )
    send = send.reshape(context, experts_here, CAP, width)
    arrived = lax.all_to_all(send, "cp", split_axis=0, concat_axis=0, tiled=True)
    gate_pre = jnp.einsum(
        "sjcd,jdf->sjcf", arrived, gate_matrix, preferred_element_type=jnp.float32
    )
    up_pre = jnp.einsum("sjcd,jdf->sjcf", arrived, up_matrix, preferred_element_type=jnp.float32)
    hidden = (gate_pre * jax.nn.sigmoid(gate_pre) * up_pre).astype(jnp.bfloat16)
    produced = jnp.einsum(
        "sjcf,jfd->sjcd", hidden, down_matrix, preferred_element_type=jnp.float32
    ).astype(jnp.bfloat16)
    received, produced, gate_pre, up_pre = (arrived, produced, gate_pre, up_pre)
    returned = lax.all_to_all(produced, "cp", split_axis=0, concat_axis=0, tiled=True)
    back_rows = (
        returned.reshape(EXPERTS * CAP, width)[slots].reshape(rows, 2, width).astype(jnp.float32)
    )
    final = middle + jnp.sum(gates[:, :, None] * back_rows, axis=1)
    output = final.astype(jnp.bfloat16)
    grad_final = grad_out.reshape(rows, width).astype(jnp.float32)
    gate_inner = jnp.sum(back_rows * grad_final[:, None, :], axis=-1)
    pair_grad = gates * (gate_inner - jnp.sum(gates * gate_inner, axis=-1, keepdims=True))
    logit_grad = jnp.sum(picks * pair_grad[:, :, None], axis=1)
    route_grad = (
        (gates[:, :, None] * grad_final[:, None, :]).astype(jnp.bfloat16).reshape(2 * rows, width)
    )
    grad_send = jnp.zeros((EXPERTS * CAP, width), jnp.bfloat16).at[slots].set(route_grad)
    grad_send = grad_send.reshape(context, experts_here, CAP, width)
    grad_arrived = lax.all_to_all(grad_send, "cp", split_axis=0, concat_axis=0, tiled=True)
    sigmoid_gate = jax.nn.sigmoid(gate_pre)
    swish = gate_pre * sigmoid_gate
    hidden = (swish * up_pre).astype(jnp.bfloat16)
    down_part = jnp.einsum(
        "sjcf,sjcd->jfd", hidden, grad_arrived, preferred_element_type=jnp.float32
    )
    hidden_grad = jnp.einsum(
        "sjcd,jfd->sjcf", grad_arrived, down_matrix, preferred_element_type=jnp.float32
    )
    gate_pre_grad = (
        hidden_grad * up_pre * sigmoid_gate * (1.0 + gate_pre * (1.0 - sigmoid_gate))
    ).astype(jnp.bfloat16)
    up_pre_grad = (hidden_grad * swish).astype(jnp.bfloat16)
    gate_part = jnp.einsum(
        "sjcd,sjcf->jdf", received, gate_pre_grad, preferred_element_type=jnp.float32
    )
    up_part = jnp.einsum(
        "sjcd,sjcf->jdf", received, up_pre_grad, preferred_element_type=jnp.float32
    )
    input_part = jnp.einsum(
        "sjcf,jdf->sjcd", gate_pre_grad, gate_matrix, preferred_element_type=jnp.float32
    )
    input_part = input_part + jnp.einsum(
        "sjcf,jdf->sjcd", up_pre_grad, up_matrix, preferred_element_type=jnp.float32
    )
    grad_returned = lax.all_to_all(
        input_part.astype(jnp.bfloat16), "cp", split_axis=0, concat_axis=0, tiled=True
    )
    routed_grad = (
        grad_returned.reshape(EXPERTS * CAP, width)[slots]
        .reshape(rows, 2, width)
        .astype(jnp.float32)
    )
    router_float = router_matrix.astype(jnp.float32)
    moe_in_grad = jnp.sum(routed_grad, axis=1) + jnp.dot(logit_grad, router_float.T, precision=HIGH)
    router_part = jnp.dot(moe_in.astype(jnp.float32).T, logit_grad, precision=HIGH)
    middle_norm_grad, gain_two_grad = rms_backward(middle, scale_two, gain_two, moe_in_grad)
    middle_grad = grad_final + middle_norm_grad
    branch_grad = middle_grad.astype(jnp.bfloat16)
    out_part = jnp.dot(attn_out.T, branch_grad, preferred_element_type=jnp.float32)
    attn_out_grad = jnp.dot(branch_grad, out_matrix.T, preferred_element_type=jnp.float32).astype(
        jnp.bfloat16
    )
    grad_groups = attn_out_grad.reshape(rows, KV, group, HD).transpose(1, 2, 0, 3)

    def attend_back(operands):
        query_g, key_g, value_g, grad_g, total_g = operands
        scores = (
            jnp.einsum("grd,ld->grl", query_g, key_g, preferred_element_type=jnp.float32) * scale
        )
        probs = jnp.where(allowed[None], jnp.exp(scores - total_g[..., None]), 0.0)
        probs_low = probs.astype(jnp.bfloat16)
        value_grad_g = jnp.einsum(
            "grl,grd->ld", probs_low, grad_g, preferred_element_type=jnp.float32
        )
        prob_grad = jnp.einsum("grd,ld->grl", grad_g, value_g, preferred_element_type=jnp.float32)
        inner = jnp.sum(probs * prob_grad, axis=-1, keepdims=True)
        score_grad = (probs * (prob_grad - inner)).astype(jnp.bfloat16)
        query_grad_g = (
            jnp.einsum("grl,ld->grd", score_grad, key_g, preferred_element_type=jnp.float32) * scale
        )
        key_grad_g = (
            jnp.einsum("grl,grd->ld", score_grad, query_g, preferred_element_type=jnp.float32)
            * scale
        )
        return (query_grad_g, key_grad_g, value_grad_g)

    query_grads, key_grads, value_grads = lax.map(
        attend_back, (query_groups, key_groups, value_groups, grad_groups, log_total)
    )
    query_grad = query_grads.transpose(2, 0, 1, 3).reshape(rows, H * HD).astype(jnp.bfloat16)
    key_full = key_grads.transpose(1, 0, 2).reshape(seq_len, KV * HD)
    value_full = value_grads.transpose(1, 0, 2).reshape(seq_len, KV * HD)
    key_grad, value_grad = (
        lax.psum_scatter(
            key_full.astype(jnp.bfloat16), "cp", scatter_dimension=0, tiled=True
        ).astype(jnp.float32),
        lax.psum_scatter(
            value_full.astype(jnp.bfloat16), "cp", scatter_dimension=0, tiled=True
        ).astype(jnp.float32),
    )
    key_grad = key_grad.astype(jnp.bfloat16)
    value_grad = value_grad.astype(jnp.bfloat16)
    query_part = jnp.dot(attn_in.T, query_grad, preferred_element_type=jnp.float32)
    key_part = jnp.dot(attn_in.T, key_grad, preferred_element_type=jnp.float32)
    value_part = jnp.dot(attn_in.T, value_grad, preferred_element_type=jnp.float32)
    attn_in_grad = jnp.dot(query_grad, query_matrix.T, preferred_element_type=jnp.float32)
    attn_in_grad = attn_in_grad + jnp.dot(
        key_grad, key_matrix.T, preferred_element_type=jnp.float32
    )
    attn_in_grad = attn_in_grad + jnp.dot(
        value_grad, value_matrix.T, preferred_element_type=jnp.float32
    )
    resid_norm_grad, gain_one_grad = rms_backward(resid, scale_one, gain_one, attn_in_grad)
    input_grad = middle_grad + resid_norm_grad
    outputs = (output.reshape(source.shape), input_grad.reshape(source.shape))
    grads = (
        (gain_one_grad, gain_two_grad, query_part, key_part, value_part, out_part, router_part),
        (gate_part, up_part, down_part),
    )
    return (outputs, grads)


def local(
    layer_input,
    cotangent,
    pairing,
    routes,
    first_gain,
    second_gain,
    query_weight,
    key_weight,
    value_weight,
    out_weight,
    router_weight,
    gate_weight,
    up_weight,
    down_weight,
):
    spread = lax.axis_size("fsdp") * lax.axis_size("cp")
    owners = lax.axis_size("fsdp")
    small_params = (
        first_gain,
        second_gain,
        query_weight,
        key_weight,
        value_weight,
        out_weight,
        router_weight,
    )
    expert_params = (gate_weight, up_weight, down_weight)
    dense_zero = jax.tree.map(
        lambda leaf: jnp.zeros((leaf.shape[0] * spread,) + leaf.shape[1:], jnp.float32),
        small_params,
    )
    expert_zero = jax.tree.map(
        lambda leaf: jnp.zeros((leaf.shape[0], leaf.shape[1] * owners, leaf.shape[2]), jnp.float32),
        expert_params,
    )
    inputs = (layer_input, cotangent, pairing, routes)

    def step(totals, piece):
        dense = (
            lax.all_gather(small_params[0], ("fsdp", "cp"), axis=0, tiled=True),
            lax.all_gather(small_params[1], ("fsdp", "cp"), axis=0, tiled=True),
            lax.all_gather(small_params[2], ("fsdp", "cp"), axis=0, tiled=True),
            lax.all_gather(small_params[3], ("fsdp", "cp"), axis=0, tiled=True),
            lax.all_gather(small_params[4], ("fsdp", "cp"), axis=0, tiled=True),
            lax.all_gather(small_params[5], ("fsdp", "cp"), axis=0, tiled=True),
            lax.all_gather(small_params[6], ("fsdp", "cp"), axis=0, tiled=True),
        )
        expert_mats = (
            lax.all_gather(expert_params[0], "fsdp", axis=1, tiled=True),
            lax.all_gather(expert_params[1], "fsdp", axis=1, tiled=True),
            lax.all_gather(expert_params[2], "fsdp", axis=1, tiled=True),
        )
        outputs, grads = micro_batch(dense, expert_mats, piece)
        return (jax.tree.map(jnp.add, totals, grads), outputs)

    totals, stacked = lax.scan(step, (dense_zero, expert_zero), inputs)
    layer_output, input_grad = stacked
    dense_sum = lax.psum_scatter(totals[0], ("fsdp", "cp"), scatter_dimension=0, tiled=True)
    expert_sum = jax.tree.map(
        lambda part: part.astype(jnp.float32),
        lax.psum_scatter(for_sending(totals[1]), "fsdp", scatter_dimension=1, tiled=True),
    )
    return (
        layer_output,
        input_grad,
        dense_sum[0],
        dense_sum[1],
        dense_sum[2],
        dense_sum[3],
        dense_sum[4],
        dense_sum[5],
        dense_sum[6],
        expert_sum[0],
        expert_sum[1],
        expert_sum[2],
    )


def solution(mesh):
    in_specs = (
        P("fsdp", "cp", None, None, None),
        P("fsdp", "cp", None, None, None),
        P("fsdp", None),
        P("fsdp", "cp", None, None, None),
        P(("fsdp", "cp")),
        P(("fsdp", "cp")),
        P(("fsdp", "cp"), None),
        P(("fsdp", "cp"), None),
        P(("fsdp", "cp"), None),
        P(("fsdp", "cp"), None),
        P(("fsdp", "cp"), None),
        P("cp", "fsdp", None),
        P("cp", "fsdp", None),
        P("cp", "fsdp", None),
    )
    out_specs = (
        P("fsdp", "cp", None, None, None),
        P("fsdp", "cp", None, None, None),
        P(("fsdp", "cp")),
        P(("fsdp", "cp")),
        P(("fsdp", "cp"), None),
        P(("fsdp", "cp"), None),
        P(("fsdp", "cp"), None),
        P(("fsdp", "cp"), None),
        P(("fsdp", "cp"), None),
        P("cp", "fsdp", None),
        P("cp", "fsdp", None),
        P("cp", "fsdp", None),
    )
    return jax.shard_map(local, mesh=mesh, in_specs=in_specs, out_specs=out_specs, check_vma=False)
```

profile of v0, /device:TPU:0, one launch (start us, length us, event | category | flops | bytes accessed | tf_op | source)
XLA Modules:
  0.0 2879.6 jit_solution(10074297990147923128)
XLA Ops:
  8.1 1877.8 %while.65 = (s32[]{:T(128)}, f32[1536]{0:T(1024)}, f32[1536]{0:T(1024)}, f32[1536,1536]{1,0:T(8,128)}, f32[1536,512]{1,0:T(8,128)}, /*index=5*/f32[1536,512]{1,0...) while((s32[]{:T(128)}, f32[1536]{0:T(1024)}, ...), condition=%wide.region_29.30_spmd.clone, body=%wide.region_0.29_spmd.clone.sunk | while | flops 32387391488 | bytes 928563648 | solution.py:298
  11.7 42.1 %all-reduce.9 = (bf16[1536]{0:T(1024)(128)(2,1)S(1)}, bf16[1536]{0:T(1024)(128)(2,1)S(1)}) all-reduce(bf16[1536]{0:T(1024)(128)(2,1)S(1)} %dynamic-update-slice.6, bf16[1536]{0:T(1024)(128)(2,1)S(1)} %dynamic-update-slice.7), channel_id=1, replica_groups=mesh['fsdp'=8,'cp'=4] {'fsdp','cp'}, use_global_device_ids=true, to_apply=%add | all-reduce | flops 3072 | bytes 12288 | tf_op jit(solution)/shard_map/while
  72.6 54.1 %all-gather.20.cloned.1.call-done = bf16[1536,512]{1,0:T(8,128)(2,1)} async-done(((bf16[48,512]{1,0:T(8,128)(2,1)}), bf16[1536,512]{1,0:T(8,128)(2,1)}) %all-gather.20.cloned.1.call-update) | async-done | bytes 1572880 | tf_op jit(solution)/shard_map/while/body/eval_jaxpr/all_gather | solution.py:286
  133.5 67.8 %all-gather.3 = bf16[32,48,16]{1,2,0:T(8,128)(2,1)S(1)} all-gather(bf16[1,48,16]{1,2,0:T(8,128)(2,1)S(1)} %bitcast.495), channel_id=1, replica_groups=mesh['fsdp'=8,'cp'=4] {'fsdp','cp'}, dimensions={0}, use_global_device_ids=true | all-gather | bytes 50688 | tf_op jit(solution)/shard_map/while/body/eval_jaxpr/all_gather | solution.py:288
  258.9 44.2 %while.66 = (s32[]{:T(128)}, bf16[8,3,256,64]{2,3,1,0:T(8,128)(2,1)}, f32[8,3,256]{2,1,0:T(4,128)S(1)}, bf16[8,3,256,64]{2,3,1,0:T(8,128)(2,1)}, bf16[8,1024,64]...) while((s32[]{:T(128)}, ...), condition=%wide.region_5.5_spmd.clone, body=%wide.region_2.4_spmd.clone.sunk | while | flops 211025152 | bytes 11077729 | solution.py:94
  367.8 65.5 %all-gather.28.cloned.1.call-done = bf16[4,1024,1536]{2,1,0:T(8,128)(2,1)} async-done(((bf16[4,128,1536]{2,1,0:T(8,128)(2,1)}), bf16[4,1024,1536]{2,1,0:T(8,128)(2,1)}) %all-gather.28.cloned.1.call-update) | async-done | bytes 12582928 | tf_op jit(solution)/shard_map/while/body/eval_jaxpr/all_gather | solution.py:293
  444.7 105.2 %all-gather.26.cloned.1.call-done = bf16[4,1536,1024]{2,1,0:T(8,128)(2,1)} async-done(((bf16[4,192,1024]{2,1,0:T(8,128)(2,1)}), bf16[4,1536,1024]{2,1,0:T(8,128)(2,1)}) %all-gather.26.cloned.1.call-update) | async-done | bytes 12582928 | tf_op jit(solution)/shard_map/while/body/eval_jaxpr/all_gather | solution.py:291
  558.7 107.7 %all-gather.30.cloned.1.call-done = bf16[4,1536,1024]{2,1,0:T(8,128)(2,1)} async-done(((bf16[4,192,1024]{2,1,0:T(8,128)(2,1)}), bf16[4,1536,1024]{2,1,0:T(8,128)(2,1)}) %all-gather.30.cloned.1.call-update) | async-done | bytes 12582928 | tf_op jit(solution)/shard_map/while/body/eval_jaxpr/all_gather | solution.py:292
  787.0 83.9 %while.67 = (s32[]{:T(128)}, bf16[8,3,256,64]{2,3,1,0:T(8,128)(2,1)}, bf16[8,1024,64]{1,2,0:T(8,128)(2,1)}, bf16[8,1024,64]{1,2,0:T(8,128)(2,1)}, bf16[8,3,256,6...) while((s32[]{:T(128)}, ...), condition=%wide.region_22.22_spmd.clone, body=%wide.region_20.21_spmd.clone.sunk | while | flops 510770432 | bytes 25650296 | solution.py:206
  943.5 39.6 %all-reduce.9 = (bf16[1536]{0:T(1024)(128)(2,1)S(1)}, bf16[1536]{0:T(1024)(128)(2,1)S(1)}) all-reduce(bf16[1536]{0:T(1024)(128)(2,1)S(1)} %dynamic-update-slice.6, bf16[1536]{0:T(1024)(128)(2,1)S(1)} %dynamic-update-slice.7), channel_id=1, replica_groups=mesh['fsdp'=8,'cp'=4] {'fsdp','cp'}, use_global_device_ids=true, to_apply=%add | all-reduce | flops 3072 | bytes 12288 | tf_op jit(solution)/shard_map/while
  1001.7 54.1 %all-gather.20.cloned.1.call-done = bf16[1536,512]{1,0:T(8,128)(2,1)} async-done(((bf16[48,512]{1,0:T(8,128)(2,1)}), bf16[1536,512]{1,0:T(8,128)(2,1)}) %all-gather.20.cloned.1.call-update) | async-done | bytes 1572880 | tf_op jit(solution)/shard_map/while/body/eval_jaxpr/all_gather | solution.py:286
  1062.2 67.6 %all-gather.3 = bf16[32,48,16]{1,2,0:T(8,128)(2,1)S(1)} all-gather(bf16[1,48,16]{1,2,0:T(8,128)(2,1)S(1)} %bitcast.495), channel_id=1, replica_groups=mesh['fsdp'=8,'cp'=4] {'fsdp','cp'}, dimensions={0}, use_global_device_ids=true | all-gather | bytes 50688 | tf_op jit(solution)/shard_map/while/body/eval_jaxpr/all_gather | solution.py:288
  1187.7 44.2 %while.66 = (s32[]{:T(128)}, bf16[8,3,256,64]{2,3,1,0:T(8,128)(2,1)}, f32[8,3,256]{2,1,0:T(4,128)S(1)}, bf16[8,3,256,64]{2,3,1,0:T(8,128)(2,1)}, bf16[8,1024,64]...) while((s32[]{:T(128)}, ...), condition=%wide.region_5.5_spmd.clone, body=%wide.region_2.4_spmd.clone.sunk | while | flops 211025152 | bytes 11077729 | solution.py:94
  1296.3 65.4 %all-gather.28.cloned.1.call-done = bf16[4,1024,1536]{2,1,0:T(8,128)(2,1)} async-done(((bf16[4,128,1536]{2,1,0:T(8,128)(2,1)}), bf16[4,1024,1536]{2,1,0:T(8,128)(2,1)}) %all-gather.28.cloned.1.call-update) | async-done | bytes 12582928 | tf_op jit(solution)/shard_map/while/body/eval_jaxpr/all_gather | solution.py:293
  1373.2 105.2 %all-gather.26.cloned.1.call-done = bf16[4,1536,1024]{2,1,0:T(8,128)(2,1)} async-done(((bf16[4,192,1024]{2,1,0:T(8,128)(2,1)}), bf16[4,1536,1024]{2,1,0:T(8,128)(2,1)}) %all-gather.26.cloned.1.call-update) | async-done | bytes 12582928 | tf_op jit(solution)/shard_map/while/body/eval_jaxpr/all_gather | solution.py:291
  1487.2 107.6 %all-gather.30.cloned.1.call-done = bf16[4,1536,1024]{2,1,0:T(8,128)(2,1)} async-done(((bf16[4,192,1024]{2,1,0:T(8,128)(2,1)}), bf16[4,1536,1024]{2,1,0:T(8,128)(2,1)}) %all-gather.30.cloned.1.call-update) | async-done | bytes 12582928 | tf_op jit(solution)/shard_map/while/body/eval_jaxpr/all_gather | solution.py:292
  1722.6 83.9 %while.67 = (s32[]{:T(128)}, bf16[8,3,256,64]{2,3,1,0:T(8,128)(2,1)}, bf16[8,1024,64]{1,2,0:T(8,128)(2,1)}, bf16[8,1024,64]{1,2,0:T(8,128)(2,1)}, bf16[8,3,256,6...) while((s32[]{:T(128)}, ...), condition=%wide.region_22.22_spmd.clone, body=%wide.region_20.21_spmd.clone.sunk | while | flops 510770432 | bytes 25650296 | solution.py:206
  1988.0 128.9 %reduce-scatter.21.cloned.1.call-done = bf16[4,192,1024]{2,1,0:T(8,128)(2,1)} async-done(((bf16[4,1536,1024]{2,1,0:T(8,128)(2,1)}), bf16[4,192,1024]{2,1,0:T(8,128)(2,1)}) %reduce-scatter.21.cloned.1.call-update) | async-done | bytes 1572880 | tf_op jit(solution)/shard_map/reduce_scatter | solution.py:303
  2120.3 126.2 %reduce-scatter.23.cloned.1.call-done = bf16[4,192,1024]{2,1,0:T(8,128)(2,1)} async-done(((bf16[4,1536,1024]{2,1,0:T(8,128)(2,1)}), bf16[4,192,1024]{2,1,0:T(8,128)(2,1)}) %reduce-scatter.23.cloned.1.call-update) | async-done | bytes 1572880 | tf_op jit(solution)/shard_map/reduce_scatter | solution.py:303
  2250.0 126.4 %reduce-scatter.25.cloned.1.call-done = bf16[4,128,1536]{2,1,0:T(8,128)(2,1)} async-done(((bf16[4,1024,1536]{2,1,0:T(8,128)(2,1)}), bf16[4,128,1536]{2,1,0:T(8,128)(2,1)}) %reduce-scatter.25.cloned.1.call-update) | async-done | bytes 1572880 | tf_op jit(solution)/shard_map/reduce_scatter | solution.py:303
  2379.9 102.6 %reduce-scatter.15.cloned.1.call-done = f32[48,512]{1,0:T(8,128)} async-done(((f32[1536,512]{1,0:T(8,128)}), f32[48,512]{1,0:T(8,128)}) %reduce-scatter.15.cloned.1.call-update) | async-done | bytes 98320 | tf_op jit(solution)/shard_map/reduce_scatter | solution.py:300
  2482.4 106.6 %reduce-scatter.17.cloned.1.call-done = f32[48,512]{1,0:T(8,128)} async-done(((f32[1536,512]{1,0:T(8,128)}), f32[48,512]{1,0:T(8,128)}) %reduce-scatter.17.cloned.1.call-update) | async-done | bytes 98320 | tf_op jit(solution)/shard_map/reduce_scatter | solution.py:300
  2589.0 141.0 %reduce-scatter.13.cloned.1.call-done = f32[48,1536]{1,0:T(8,128)} async-done(((f32[1536,1536]{1,0:T(8,128)}), f32[48,1536]{1,0:T(8,128)}) %reduce-scatter.13.cloned.1.call-update) | async-done | bytes 294928 | tf_op jit(solution)/shard_map/reduce_scatter | solution.py:300
  2730.0 142.0 %reduce-scatter.19.cloned.1.call-done = f32[48,1536]{1,0:T(8,128)} async-done(((f32[1536,1536]{1,0:T(8,128)}), f32[48,1536]{1,0:T(8,128)}) %reduce-scatter.19.cloned.1.call-update) | async-done | bytes 294928 | tf_op jit(solution)/shard_map/reduce_scatter | solution.py:300
  (690 shorter events, 1102.3 us)
Async XLA Ops:
  9.1 117.6 %all-gather.20.cloned.1.call-start = ((), (), s32[]{:S(2)}) async-start(), calls=%async_computation.25 | async-start | bytes 1622016 | tf_op jit(solution)/shard_map/while/body/eval_jaxpr/all_gather | solution.py:286
  9.9 202.2 %all-gather.18.cloned.1.call-start = ((), (), s32[]{:S(2)}) async-start(), calls=%async_computation.24 | async-start | bytes 1310720 | tf_op jit(solution)/shard_map/while/body/eval_jaxpr/all_gather | solution.py:74
  72.6 141.8 %all-gather.22.cloned.1.call-start = ((), (), s32[]{:S(2)}) async-start(), calls=%async_computation.26 | async-start | bytes 1310720 | tf_op jit(solution)/shard_map/while/body/eval_jaxpr/all_gather | solution.py:75
  129.4 121.3 %all-gather.14.cloned.1.call-start = ((), (), s32[]{:S(2)}) async-start(), calls=%async_computation.22 | async-start | bytes 4866048 | tf_op jit(solution)/shard_map/while/body/eval_jaxpr/all_gather | solution.py:284
  130.0 185.9 %all-gather.24.cloned.1.call-start = ((), (), s32[]{:S(2)}) async-start(), calls=%async_computation.27 | async-start | bytes 4866048 | tf_op jit(solution)/shard_map/while/body/eval_jaxpr/all_gather | solution.py:287
  130.6 302.7 %all-gather.28.cloned.1.call-start = ((), (), s32[]{:S(2)}) async-start(), calls=%async_computation.29 | async-start | bytes 14155776 | tf_op jit(solution)/shard_map/while/body/eval_jaxpr/all_gather | solution.py:293
  131.4 418.5 %all-gather.26.cloned.1.call-start = ((), (), s32[]{:S(2)}) async-start(), calls=%async_computation.28 | async-start | bytes 14155776 | tf_op jit(solution)/shard_map/while/body/eval_jaxpr/all_gather | solution.py:291
  132.1 534.3 %all-gather.30.cloned.1.call-start = ((), (), s32[]{:S(2)}) async-start(), calls=%async_computation.30 | async-start | bytes 14155776 | tf_op jit(solution)/shard_map/while/body/eval_jaxpr/all_gather | solution.py:292
  725.5 188.2 %reduce-scatter.29.cloned.1.call-start = ((), (), s32[]{:S(2)}) async-start(), calls=%async_computation.31 | async-start | bytes 1310720 | tf_op jit(solution)/shard_map/while/body/eval_jaxpr/reduce_scatter | solution.py:213
  941.7 199.0 %all-gather.18.cloned.1.call-start = ((), (), s32[]{:S(2)}) async-start(), calls=%async_computation.24 | async-start | bytes 1310720 | tf_op jit(solution)/shard_map/while/body/eval_jaxpr/all_gather | solution.py:74
  1001.7 141.4 %all-gather.22.cloned.1.call-start = ((), (), s32[]{:S(2)}) async-start(), calls=%async_computation.26 | async-start | bytes 1310720 | tf_op jit(solution)/shard_map/while/body/eval_jaxpr/all_gather | solution.py:75
  1058.5 121.1 %all-gather.14.cloned.1.call-start = ((), (), s32[]{:S(2)}) async-start(), calls=%async_computation.22 | async-start | bytes 4866048 | tf_op jit(solution)/shard_map/while/body/eval_jaxpr/all_gather | solution.py:284
  1059.1 186.1 %all-gather.24.cloned.1.call-start = ((), (), s32[]{:S(2)}) async-start(), calls=%async_computation.27 | async-start | bytes 4866048 | tf_op jit(solution)/shard_map/while/body/eval_jaxpr/all_gather | solution.py:287
  1059.7 302.1 %all-gather.28.cloned.1.call-start = ((), (), s32[]{:S(2)}) async-start(), calls=%async_computation.29 | async-start | bytes 14155776 | tf_op jit(solution)/shard_map/while/body/eval_jaxpr/all_gather | solution.py:293
  1060.3 418.1 %all-gather.26.cloned.1.call-start = ((), (), s32[]{:S(2)}) async-start(), calls=%async_computation.28 | async-start | bytes 14155776 | tf_op jit(solution)/shard_map/while/body/eval_jaxpr/all_gather | solution.py:291
  1061.0 533.7 %all-gather.30.cloned.1.call-start = ((), (), s32[]{:S(2)}) async-start(), calls=%async_computation.30 | async-start | bytes 14155776 | tf_op jit(solution)/shard_map/while/body/eval_jaxpr/all_gather | solution.py:292
  1654.1 213.4 %reduce-scatter.29.cloned.1.call-start = ((), (), s32[]{:S(2)}) async-start(), calls=%async_computation.31 | async-start | bytes 1310720 | tf_op jit(solution)/shard_map/while/body/eval_jaxpr/reduce_scatter | solution.py:213
  1888.1 228.8 %reduce-scatter.21.cloned.1.call-start = ((), (), s32[]{:S(2)}) async-start(), calls=%async_computation.18 | async-start | bytes 14155776 | tf_op jit(solution)/shard_map/reduce_scatter | solution.py:303
  1901.6 345.0 %reduce-scatter.23.cloned.1.call-start = ((), (), s32[]{:S(2)}) async-start(), calls=%async_computation.19 | async-start | bytes 14155776 | tf_op jit(solution)/shard_map/reduce_scatter | solution.py:303
  1915.2 461.2 %reduce-scatter.25.cloned.1.call-start = ((), (), s32[]{:S(2)}) async-start(), calls=%async_computation.20 | async-start | bytes 14155776 | tf_op jit(solution)/shard_map/reduce_scatter | solution.py:303
  1928.7 553.7 %reduce-scatter.15.cloned.1.call-start = ((), (), s32[]{:S(2)}) async-start(), calls=%async_computation.15 | async-start | bytes 3244032 | tf_op jit(solution)/shard_map/reduce_scatter | solution.py:300
  1929.5 659.5 %reduce-scatter.17.cloned.1.call-start = ((), (), s32[]{:S(2)}) async-start(), calls=%async_computation.16 | async-start | bytes 3244032 | tf_op jit(solution)/shard_map/reduce_scatter | solution.py:300
  1930.2 799.7 %reduce-scatter.13.cloned.1.call-start = ((), (), s32[]{:S(2)}) async-start(), calls=%async_computation.14 | async-start | bytes 9732096 | tf_op jit(solution)/shard_map/reduce_scatter | solution.py:300
  1930.8 941.1 %reduce-scatter.19.cloned.1.call-start = ((), (), s32[]{:S(2)}) async-start(), calls=%async_computation.17 | async-start | bytes 9732096 | tf_op jit(solution)/shard_map/reduce_scatter | solution.py:300
  (98 other events, 2901.5 us)
Sparse Core Ops, SparseCore 0:
  12.1 57.7 all-gather.15
  72.8 53.8 all-gather.19
  129.1 25.9 all-gather.17
  157.4 26.9 all-gather.21
  187.1 63.6 all-gather.13
  253.5 62.3 all-gather.23
  317.5 115.7 all-gather.27
  434.9 114.9 all-gather.25
  551.5 114.9 all-gather.29
  871.1 26.3 reduce-scatter.28
  900.7 27.7 reduce-scatter.30
  943.8 55.1 all-gather.15
  1001.8 53.8 all-gather.19
  1058.0 25.8 all-gather.17
  1086.2 26.9 all-gather.21
  1116.0 63.5 all-gather.13
  1182.3 62.7 all-gather.23
  1246.6 115.1 all-gather.27
  1363.4 114.9 all-gather.25
  1479.8 114.9 all-gather.29
  1806.7 26.3 reduce-scatter.28
  1841.9 26.5 reduce-scatter.30
Sparse Core Ops, SparseCore 1:
  1892.1 94.4 reduce-scatter.26
  1988.7 128.1 reduce-scatter.20
  2119.0 127.4 reduce-scatter.22
  2248.9 127.4 reduce-scatter.24
  2382.4 100.0 reduce-scatter.14
  2488.4 100.5 reduce-scatter.16
  2595.3 134.6 reduce-scatter.12
  2737.3 134.6 reduce-scatter.18
where the time goes:
time: 2890 us; the launch traced here: 2880 us
  waiting for transfers between devices  1730 us (60%)
  matrix products  555 us (19%)
  blocking collectives  256 us (9%)
  local copies, waits for them, and re-layouts  145 us (5%)
  other arithmetic  143 us (5%)
  starting transfers between devices  32.1 us (1%)
    reduce_scatter x4, waiting for transfers between devices, local(): lax.psum_scatter(totals[0], ('fsdp', 'cp'), scatter_dimension=0, tiled=True)  492 us
    reduce_scatter x3, waiting for transfers between devices, local(): lax.psum_scatter(for_sending(totals[1]), 'fsdp', scatter_dimension=1, til...  381 us
    all_gather x2, waiting for transfers between devices, step(): lax.all_gather(expert_params[1], 'fsdp', axis=1, tiled=True)  215 us
    all_gather x2, waiting for transfers between devices, step(): lax.all_gather(expert_params[0], 'fsdp', axis=1, tiled=True)  210 us
    all_gather x2, blocking collectives, step(): lax.all_gather(small_params[6], ('fsdp', 'cp'), axis=0, tiled=True)  135 us
    all_gather x2, waiting for transfers between devices, step(): lax.all_gather(expert_params[2], 'fsdp', axis=1, tiled=True)  131 us
    all_gather x2, waiting for transfers between devices, step(): lax.all_gather(small_params[4], ('fsdp', 'cp'), axis=0, tiled=True)  108 us
    while x2, blocking collectives  81.7 us
  transfers between devices with their start and end apart: 38, of which 27 were waited for; matrix products, arithmetic and copies ran while one was open for 19% of the time, Pallas kernels for 0%

commit v1 on v0

v1 whole, which is shorter than its diff:
```python
import functools

import jax
import jax.numpy as jnp
from jax import lax
from jax.experimental import pallas as pl
from jax.experimental.pallas import tpu as pltpu
from jax.sharding import Mesh, PartitionSpec as P

H = 24
KV = 8
HD = 64
EXPERTS = 16
BLK = 128
CAP = 48
EPS = 1e-05
NEG = -1e30
GROUP = H // KV
SCALE = HD ** (-0.5)
PACK = 2
HIGH = lax.Precision.HIGHEST
F32 = jnp.float32
BF16 = jnp.bfloat16
DENSE = ("hi", "ep", "cp")


def dot(a, b, ca=1, cb=0):
    return lax.dot_general(a, b, (((ca,), (cb,)), ((), ())), preferred_element_type=F32)


def sort_blocks(table, seq, src, dst, which, blocks):
    for b in range(blocks):
        at = table[seq, b]
        dst[pl.ds(b * BLK, BLK), :] = src[at // 2, 0, which, pl.ds((at % 2) * BLK, BLK), :]


def stack_heads(rows, first, scale=None):
    parts = [
        rows[half * BLK : (half + 1) * BLK, (first + i) * HD : (first + i + 1) * HD]
        for half in range(2)
        for i in range(GROUP)
    ]
    out = jnp.concatenate(parts, axis=0)
    return out if scale is None else out * jnp.asarray(scale, out.dtype)


def unstack_heads(low, high):
    rows = []
    for pieces in (low, high):
        heads = [p[i * BLK : (i + 1) * BLK] for p in pieces for i in range(GROUP)]
        rows.append(jnp.concatenate(heads, axis=1))
    return jnp.concatenate(rows, axis=0)


def attend_kernel(table, place, q_ref, kv_ref, o_ref, k_s, v_s, low_bias, high_bias):
    seq = pl.program_id(0)
    blocks = 2 * kv_ref.shape[0]
    half = blocks * BLK // 2
    rows = GROUP * BLK
    at = place[seq]

    @pl.when(pl.program_id(1) == 0)
    def _():
        query = lax.broadcasted_iota(jnp.int32, (BLK, half), 0)
        key = lax.broadcasted_iota(jnp.int32, (BLK, half), 1)
        low_bias[...] = jnp.where(key <= query + at * BLK, 0.0, NEG)
        high_bias[...] = jnp.where(key + half <= query + (blocks - 1 - at) * BLK, 0.0, NEG)

    sort_blocks(table, seq, kv_ref, k_s, 0, blocks)
    sort_blocks(table, seq, kv_ref, v_s, 1, blocks)
    q_all = q_ref[...]
    lows, highs = [], []
    for j in range(PACK):
        k = k_s[:, j * HD : (j + 1) * HD]
        v = v_s[:, j * HD : (j + 1) * HD]
        q = stack_heads(q_all, j * GROUP, SCALE)
        s_low = dot(q[:rows], k[:half], 1, 1) + jnp.concatenate([low_bias[...]] * GROUP, axis=0)
        peak = jnp.max(s_low, axis=-1, keepdims=True)
        e_low = jnp.exp(s_low - peak)
        total = jnp.sum(e_low, axis=-1, keepdims=True)
        lows.append((dot(e_low.astype(BF16), v[:half]) / total).astype(BF16))
        s_one = dot(q[rows:], k[:half], 1, 1)
        s_two = dot(q[rows:], k[half:], 1, 1) + jnp.concatenate([high_bias[...]] * GROUP, axis=0)
        peak = jnp.maximum(
            jnp.max(s_one, axis=-1, keepdims=True), jnp.max(s_two, axis=-1, keepdims=True)
        )
        e_one = jnp.exp(s_one - peak)
        e_two = jnp.exp(s_two - peak)
        total = jnp.sum(e_one, axis=-1, keepdims=True) + jnp.sum(e_two, axis=-1, keepdims=True)
        mixed = dot(e_one.astype(BF16), v[:half]) + dot(e_two.astype(BF16), v[half:])
        highs.append((mixed / total).astype(BF16))
    o_ref[...] = unstack_heads(lows, highs)


def attend_back_kernel(
    sizes, kinds, table, inverse, place, q_ref, kv_ref, g_ref, *refs
):
    n = len(kinds)
    ins, dq_ref, dkv_ref, outs = refs[:n], refs[n], refs[n + 1], refs[n + 2 : 2 * n + 2]
    k_s, v_s, low_bias, high_bias, parts = refs[2 * n + 2 : 2 * n + 7]
    post_sems = refs[2 * n + 7 : 2 * n + 10]
    step_send, step_recv, step_here = refs[2 * n + 10 :]
    cp = sizes[2]
    my_cp = lax.axis_index("cp")
    groups = KV // PACK
    step = pl.program_id(0) * groups + pl.program_id(1)
    last = pl.num_programs(0) * groups - 1
    office = PostOffice(sizes, post_sems)

    @pl.when(step == 0)
    def _():
        office.greet(kinds)
        office.begin(kinds, ins, outs)

    def step_copy(at_seq, at_group, at_step, m):
        columns = pl.ds(pl.multiple_of(at_group * PACK * HD, PACK * HD), PACK * HD)
        to = lax.rem(my_cp + m, cp)
        return mesh_copy(
            parts.at[at_step, to],
            dkv_ref.at[my_cp, at_seq, :, :, columns],
            (step_send, step_recv),
            at_step * (cp - 1) + m - 1,
            {"cp": to},
        )

    def own_copy(at_seq, at_group, at_step):
        columns = pl.ds(pl.multiple_of(at_group * PACK * HD, PACK * HD), PACK * HD)
        return pltpu.make_async_copy(
            parts.at[at_step, my_cp], dkv_ref.at[my_cp, at_seq, :, :, columns], step_here.at[at_step]
        )

    seq = pl.program_id(0)
    blocks = 2 * kv_ref.shape[0]
    half = blocks * BLK // 2
    rows = GROUP * BLK
    at = place[seq]

    @pl.when(pl.program_id(1) == 0)
    def _():
        key = lax.broadcasted_iota(jnp.int32, (half, BLK), 0)
        query = lax.broadcasted_iota(jnp.int32, (half, BLK), 1)
        low_bias[...] = jnp.where(key <= query + at * BLK, 0.0, NEG)
        high_bias[...] = jnp.where(key + half <= query + (blocks - 1 - at) * BLK, 0.0, NEG)

    sort_blocks(table, seq, kv_ref, k_s, 0, blocks)
    sort_blocks(table, seq, kv_ref, v_s, 1, blocks)
    q_all = q_ref[...]
    g_all = g_ref[...]
    lows, highs, dks, dvs = [], [], [], []
    for j in range(PACK):
        k = k_s[:, j * HD : (j + 1) * HD]
        v = v_s[:, j * HD : (j + 1) * HD]
        q = stack_heads(q_all, j * GROUP, SCALE)
        g = stack_heads(g_all, j * GROUP)

        def probs(s_parts):
            peak = jnp.max(s_parts[0], axis=0, keepdims=True)
            for s in s_parts[1:]:
                peak = jnp.maximum(peak, jnp.max(s, axis=0, keepdims=True))
            es = [jnp.exp(s - peak) for s in s_parts]
            total = jnp.sum(es[0], axis=0, keepdims=True)
            for e in es[1:]:
                total = total + jnp.sum(e, axis=0, keepdims=True)
            part = 1.0 / total
            return [e * part for e in es]

        def score_grads(ps, dps):
            inner = jnp.sum(ps[0] * dps[0], axis=0, keepdims=True)
            for p, d in zip(ps[1:], dps[1:]):
                inner = inner + jnp.sum(p * d, axis=0, keepdims=True)
            return [(p * (d - inner)).astype(BF16) for p, d in zip(ps, dps)]

        s_low = dot(k[:half], q[:rows], 1, 1) + jnp.concatenate([low_bias[...]] * GROUP, axis=1)
        (p_low,) = probs([s_low])
        (d_low,) = score_grads([p_low], [dot(v[:half], g[:rows], 1, 1)])
        dv_one = dot(p_low.astype(BF16), g[:rows])
        dk_one = dot(d_low, q[:rows])
        lows.append((dot(d_low, k[:half], 0, 0) * SCALE).astype(BF16))

        s_one = dot(k[:half], q[rows:], 1, 1)
        s_two = dot(k[half:], q[rows:], 1, 1) + jnp.concatenate([high_bias[...]] * GROUP, axis=1)
        p_one, p_two = probs([s_one, s_two])
        d_one, d_two = score_grads(
            [p_one, p_two], [dot(v[:half], g[rows:], 1, 1), dot(v[half:], g[rows:], 1, 1)]
        )
        dv_one = dv_one + dot(p_one.astype(BF16), g[rows:])
        dv_two = dot(p_two.astype(BF16), g[rows:])
        dk_one = dk_one + dot(d_one, q[rows:])
        dk_two = dot(d_two, q[rows:])
        highs.append(
            ((dot(d_one, k[:half], 0, 0) + dot(d_two, k[half:], 0, 0)) * SCALE).astype(BF16)
        )
        dks.append(jnp.concatenate([dk_one, dk_two], axis=0).astype(BF16))
        dvs.append(jnp.concatenate([dv_one, dv_two], axis=0).astype(BF16))
    dq_ref[...] = unstack_heads(lows, highs)
    k_s[...] = jnp.concatenate(dks, axis=1)
    v_s[...] = jnp.concatenate(dvs, axis=1)
    for c in range(cp):
        for h in range(2):
            at_b = pl.ds(inverse[seq, 2 * c + h] * BLK, BLK)
            parts[step, c, 0, h * BLK : (h + 1) * BLK, :] = k_s[at_b, :]
            parts[step, c, 1, h * BLK : (h + 1) * BLK, :] = v_s[at_b, :]
    for m in range(1, cp):
        step_copy(seq, pl.program_id(1), step, m).start()
    own_copy(seq, pl.program_id(1), step).start()

    @pl.when(step == last)
    def _():
        @pl.loop(0, last + 1)
        def _(i):
            at_seq, at_group = i // groups, lax.rem(i, groups)
            for m in range(1, cp):
                step_copy(at_seq, at_group, i, m).wait()
            own_copy(at_seq, at_group, i).wait()

        office.end(kinds, ins, outs)


ATTENTION_COST = pl.CostEstimate(flops=2**34, bytes_accessed=2**24, transcendentals=2**24)


def attention_specs(kv):
    cp, n_seq = kv.shape[:2]
    row = pl.BlockSpec((2 * BLK, PACK * GROUP * HD), lambda s, g, *_: (s, g))
    whole = pl.BlockSpec((cp, 1, 2, 2 * BLK, PACK * HD), lambda s, g, *_: (0, s, 0, 0, g))
    return row, whole, (n_seq, KV // PACK), cp * 2 * BLK


def attend(table, place, q, kv):
    row, whole, grid, keys = attention_specs(kv)
    return pl.pallas_call(
        attend_kernel,
        grid_spec=pltpu.PrefetchScalarGridSpec(
            num_scalar_prefetch=2,
            grid=grid,
            in_specs=[row, whole],
            out_specs=row,
            scratch_shapes=[pltpu.VMEM((keys, PACK * HD), BF16)] * 2
            + [pltpu.VMEM((BLK, keys // 2), F32)] * 2,
        ),
        out_shape=jax.ShapeDtypeStruct(q.shape, BF16),
        compiler_params=pltpu.CompilerParams(
            dimension_semantics=("arbitrary", "arbitrary"), vmem_limit_bytes=56 * 2**20
        ),
        cost_estimate=ATTENTION_COST,
    )(table, place, q, kv)


def attend_back(collective_id, table, inverse, place, q, kv, grad, *jobs):
    row, whole, grid, keys = attention_specs(kv)
    sizes = tuple(lax.axis_size(a) for a in DENSE)
    cp = sizes[2]
    steps = grid[0] * grid[1]
    kinds, arrays, shapes = courier_jobs(sizes, jobs)
    smem = pl.BlockSpec(memory_space=pltpu.SMEM)
    hbm = pl.BlockSpec(memory_space=pl.ANY)
    n = jobs_messages(kinds, *sizes)
    return pl.pallas_call(
        functools.partial(attend_back_kernel, sizes, kinds),
        grid=grid,
        in_specs=[smem, smem, smem, row, whole, row] + [hbm] * len(jobs),
        out_specs=[row, hbm] + [hbm] * len(jobs),
        out_shape=[
            jax.ShapeDtypeStruct(q.shape, BF16),
            jax.ShapeDtypeStruct(kv.shape, BF16),
        ]
        + shapes,
        scratch_shapes=[pltpu.VMEM((keys, PACK * HD), BF16)] * 2
        + [pltpu.VMEM((keys // 2, BLK), F32)] * 2
        + [pltpu.VMEM((steps, cp, 2, 2 * BLK, PACK * HD), BF16)]
        + post_scratch(n, len(jobs))
        + [
            pltpu.SemaphoreType.DMA((steps * (cp - 1),)),
            pltpu.SemaphoreType.DMA((steps * (cp - 1),)),
            pltpu.SemaphoreType.DMA((steps,)),
        ],
        compiler_params=pltpu.CompilerParams(
            dimension_semantics=("arbitrary", "arbitrary"),
            vmem_limit_bytes=56 * 2**20,
            collective_id=collective_id,
            has_side_effects=True,
        ),
        cost_estimate=ATTENTION_COST,
    )(table, inverse, place, q, kv, grad, *arrays)


def tie(x, *others):
    return lax.optimization_barrier((x,) + others)[0]


def mesh_copy(src, dst, sems, at, device):
    send, recv = sems
    return pltpu.make_async_remote_copy(
        src_ref=src, dst_ref=dst, send_sem=send.at[at], recv_sem=recv.at[at],
        device_id=device, device_id_type=pl.DeviceIdType.MESH,
    )


def jobs_messages(kinds, hi, ep, cp):
    f, e = hi * ep, ep * cp
    counts = {
        "gather": f // 2 - 1 + (f // 2) * (cp - 1) + (f // 2) * cp,
        "expert": f - 1, "owners": f - 1, "tokens": e - 1, "peers": cp - 1, "quad": ep - 1,
    }
    return sum(counts[k] for k in kinds)


def post_scratch(n, jobs):
    return [
        pltpu.SemaphoreType.DMA((max(n, 1),)),
        pltpu.SemaphoreType.DMA((max(n, 1),)),
        pltpu.SemaphoreType.DMA((max(jobs, 1),)),
    ]


def plus(a, b, size):
    return lax.rem(a + b, size)


def flip(a, bits):
    out = a
    for bit in range(bits.bit_length()):
        if bits >> bit & 1:
            out = out + (1 << bit) - (1 << (bit + 1)) * lax.rem(a // (1 << bit), 2)
    return out


class PostOffice:
    def __init__(self, sizes, sems):
        self.hi, self.ep, self.cp = sizes
        self.fsdp = self.hi * self.ep
        self.send, self.recv, self.here = sems
        self.my_ep, self.my_cp = lax.axis_index("ep"), lax.axis_index("cp")
        self.me = lax.axis_index("hi") * self.ep + self.my_ep
        self.sibling = flip(self.me, 1)

    def at_fsdp(self, f):
        return {"hi": f // self.ep, "ep": lax.rem(f, self.ep)}

    def greet(self, kinds):
        barrier = pltpu.get_barrier_semaphore()
        partners = [self.at_fsdp(plus(self.me, k, self.fsdp)) for k in range(1, self.fsdp)]
        partners += [{"cp": plus(self.my_cp, k, self.cp)} for k in range(1, self.cp)]
        if "tokens" in kinds:
            partners += [
                {"ep": plus(self.my_ep, a, self.ep), "cp": plus(self.my_cp, b, self.cp)}
                for a in range(1, self.ep)
                for b in range(1, self.cp)
            ]
        for p in partners:
            pl.semaphore_signal(barrier, inc=1, device_id=p, device_id_type=pl.DeviceIdType.MESH)
        pl.semaphore_wait(barrier, len(partners))

    def copies(self, kinds, ins, outs):
        me, my_ep, my_cp, ep, cp, fsdp = (
            self.me, self.my_ep, self.my_cp, self.ep, self.cp, self.fsdp
        )
        away, local = [], []

        def post(src, dst, device):
            away.append(mesh_copy(src, dst, (self.send, self.recv), len(away), device))

        def keep(src, dst):
            local.append(pltpu.make_async_copy(src, dst, self.here.at[len(local)]))

        for kind, x, out in zip(kinds, ins, outs):
            if kind == "expert":
                rows = x.shape[1]
                at = pl.ds(pl.multiple_of(me * rows, rows), rows)
                for k in range(1, fsdp):
                    to = plus(me, k, fsdp)
                    post(x.at[lax.rem(to, ep)], out.at[at], self.at_fsdp(to))
                keep(x.at[my_ep], out.at[at])
            elif kind == "owners":
                rows = out.shape[1]
                for k in range(1, fsdp):
                    to = plus(me, k, fsdp)
                    src = x.at[pl.ds(pl.multiple_of(to * rows, rows), rows)]
                    post(src, out.at[me], self.at_fsdp(to))
                keep(x.at[pl.ds(pl.multiple_of(me * rows, rows), rows)], out.at[me])
            elif kind == "quad":
                for k in range(1, ep):
                    to = plus(my_ep, k, ep)
                    post(x.at[to], out.at[my_ep], {"ep": to})
                keep(x.at[my_ep], out.at[my_ep])
            elif kind == "peers":
                for m in range(1, cp):
                    post(x, out.at[my_cp], {"cp": plus(my_cp, m, cp)})
                keep(x, out.at[my_cp])
        return away, local

    def begin(self, *jobs):
        for group in self.copies(*jobs):
            for c in group:
                c.start()

    def end(self, *jobs):
        for group in self.copies(*jobs):
            for c in group:
                c.wait()

    def gather(self, x, out, first, here):
        me, my_cp, cp, fsdp = self.me, self.my_cp, self.cp, self.fsdp
        sent, across = [], []

        def post(src, dst, device):
            c = mesh_copy(src, dst, (self.send, self.recv), first + len(sent), device)
            c.start()
            sent.append(c)
            return c

        def row(f, c):
            return out.at[f * cp + c]

        def share(f, src):
            for m in range(1, cp):
                across.append((f, m, post(src, row(f, my_cp), {"cp": plus(my_cp, m, cp)})))
            mirrored.append(post(src, row(f, my_cp), self.at_fsdp(self.sibling)))

        mirrored = []
        z = post(x, row(me, my_cp), self.at_fsdp(flip(me, 2)))
        own = pltpu.make_async_copy(x, row(me, my_cp), self.here.at[here])
        own.start()
        share(me, x)
        column = [z]
        for k in range(1, fsdp // 2):
            column[-1].wait_recv()
            if k + 1 < fsdp // 2:
                column.append(post(x, row(me, my_cp), self.at_fsdp(flip(me, 2 * k + 2))))
            f = flip(me, 2 * k)
            share(f, row(f, my_cp))
        yield
        for f, m, c in across:
            c.wait_recv()
            got = row(f, plus(my_cp, cp - m, cp))
            mirrored.append(post(got, got, self.at_fsdp(self.sibling)))
        for c in mirrored:
            c.wait_recv()
        for c in sent:
            c.wait_send()
        own.wait()
        yield


def courier_jobs(sizes, jobs):
    hi, ep, cp = sizes
    shapes = []
    for kind, x in jobs:
        if kind == "gather":
            shape = (hi * ep * cp,) + x.shape
        elif kind == "expert":
            shape = (hi * ep * x.shape[1],) + x.shape[2:]
        elif kind == "owners":
            shape = (hi * ep, x.shape[0] // (hi * ep)) + x.shape[1:]
        elif kind == "peers":
            shape = (cp,) + x.shape
        else:
            shape = x.shape
        shapes.append(jax.ShapeDtypeStruct(shape, x.dtype))
    return [k for k, _ in jobs], [x for _, x in jobs], shapes


def courier_kernel(sizes, kinds, *refs):
    n = len(kinds)
    ins, outs = refs[:n], refs[n : 2 * n]
    office = PostOffice(sizes, refs[2 * n :])
    office.greet(kinds)
    first, here, gathers = jobs_messages([k for k in kinds if k != "gather"], *sizes), 0, []
    here = len([k for k in kinds if k != "gather"])
    for kind, x, out in zip(kinds, ins, outs):
        if kind == "gather":
            gathers.append(office.gather(x, out, first, here))
            first, here = first + jobs_messages(["gather"], *sizes), here + 1
            next(gathers[-1])
    office.begin(kinds, ins, outs)
    for g in gathers:
        next(g)
    office.end(kinds, ins, outs)


def courier(collective_id, *jobs):
    sizes = tuple(lax.axis_size(a) for a in DENSE)
    kinds, arrays, shapes = courier_jobs(sizes, jobs)
    hbm = pl.BlockSpec(memory_space=pl.ANY)
    return pl.pallas_call(
        functools.partial(courier_kernel, sizes, kinds),
        out_shape=shapes,
        in_specs=[hbm] * len(jobs),
        out_specs=[hbm] * len(jobs),
        scratch_shapes=post_scratch(jobs_messages(kinds, *sizes), len(jobs)),
        compiler_params=pltpu.CompilerParams(collective_id=collective_id, has_side_effects=True),
    )(*arrays)


def dense_sum_kernel(sizes, kinds, n_parts, *refs):
    n = len(kinds)
    parts, refs = refs[:n_parts], refs[n_parts:]
    widths = [p.shape[2] for p in parts]
    columns = [pl.ds(sum(widths[:j]), w) for j, w in enumerate(widths)]
    ins, out, outs = refs[:n], refs[n], refs[n + 1 : 2 * n + 1]
    mine, from_core, summed, from_peers, rows_out, from_column = refs[2 * n + 1 : 2 * n + 7]
    office = PostOffice(sizes, refs[2 * n + 7 : 2 * n + 10])
    load_sem, core_sems, peer_sems, column_sems = (
        refs[2 * n + 10],
        refs[2 * n + 11 : 2 * n + 13],
        refs[2 * n + 13 : 2 * n + 15],
        refs[2 * n + 15 : 2 * n + 17],
    )
    cp, columns_n = sizes[2], office.fsdp // 2
    me, my_cp = office.me, office.my_cp
    office.greet(kinds)
    core = lax.rem(me, 2)
    targets = [flip(me, 2 * k) for k in range(columns_n - 1, -1, -1)]
    loads, cores = [], []
    for i, f in enumerate(targets):
        other = flip(f, 1)
        for j, (part, where) in enumerate(zip(parts, columns)):
            c = mesh_copy(
                part.at[pl.ds(other * cp, cp)],
                from_core.at[i, :, :, where],
                core_sems,
                i * n_parts + j,
                office.at_fsdp(office.sibling),
            )
            c.start()
            cores.append(c)
            c = pltpu.make_async_copy(
                part.at[pl.ds(f * cp, cp)], mine.at[i, :, :, where], load_sem.at[i * n_parts + j]
            )
            c.start()
            loads.append(c)
    office.begin(kinds, ins, outs)
    peers = []
    for i in range(columns_n):
        for c in loads[i * n_parts : (i + 1) * n_parts] + cores[i * n_parts : (i + 1) * n_parts]:
            c.wait()
        summed[i] = (mine[i].astype(F32) + from_core[i].astype(F32)).astype(BF16)
        row = []
        for m in range(1, cp):
            to = plus(my_cp, m, cp)
            c = mesh_copy(
                summed.at[i, to], from_peers.at[i, m - 1], peer_sems, i * (cp - 1) + m - 1, {"cp": to}
            )
            c.start()
            row.append(c)
        peers.append(row)
    column = []
    total = None
    for i, f in enumerate(targets):
        total = summed[i, my_cp].astype(F32)
        for m, c in enumerate(peers[i], 1):
            c.wait_recv()
            total = total + from_peers[i, m - 1].astype(F32)
        if i < columns_n - 1:
            rows_out[i] = total.astype(BF16)
            c = mesh_copy(
                rows_out.at[i], from_column.at[i], column_sems, i, office.at_fsdp(f)
            )
            c.start()
            column.append(c)
    for i, c in enumerate(column):
        c.wait_recv()
        total = total + from_column[i].astype(F32)
    out[...] = total
    for c in column + [c for row in peers for c in row]:
        c.wait_send()
    office.end(kinds, ins, outs)


def dense_sum(collective_id, parts, *jobs):
    sizes = tuple(lax.axis_size(a) for a in DENSE)
    hi, ep, cp = sizes
    column = hi * ep // 2
    rows = parts[0].shape[0] // (hi * ep * cp)
    width = sum(p.shape[1] for p in parts)
    kinds, arrays, shapes = courier_jobs(sizes, jobs)
    hbm = pl.BlockSpec(memory_space=pl.ANY)
    vmem = pl.BlockSpec(memory_space=pltpu.VMEM)

    def sems(count):
        return [pltpu.SemaphoreType.DMA((count,))] * 2

    return pl.pallas_call(
        functools.partial(dense_sum_kernel, sizes, kinds, len(parts)),
        out_shape=[jax.ShapeDtypeStruct((rows, width), F32)] + shapes,
        in_specs=[hbm] * (len(parts) + len(jobs)),
        out_specs=[vmem] + [hbm] * len(jobs),
        scratch_shapes=[
            pltpu.VMEM((column, cp, rows, width), BF16),
            pltpu.VMEM((column, cp, rows, width), BF16),
            pltpu.VMEM((column, cp, rows, width), BF16),
            pltpu.VMEM((column, cp - 1, rows, width), BF16),
            pltpu.VMEM((column - 1, rows, width), BF16),
            pltpu.VMEM((column - 1, rows, width), BF16),
        ]
        + post_scratch(jobs_messages(kinds, *sizes), len(jobs))
        + [pltpu.SemaphoreType.DMA((column * len(parts),))]
        + sems(column * len(parts))
        + sems(column * (cp - 1))
        + sems(column - 1),
        compiler_params=pltpu.CompilerParams(
            collective_id=collective_id, has_side_effects=True, vmem_limit_bytes=56 * 2**20
        ),
    )(*(p.reshape(-1, rows, p.shape[1]) for p in parts), *arrays)


def quad(x):
    return lax.all_to_all(x, "ep", split_axis=0, concat_axis=0, tiled=True)


def swap(x):
    hi = lax.axis_size("hi")
    xs = x if isinstance(x, list) else [x] * (hi - 1)
    return [
        lax.ppermute(xs[k - 1], "hi", [(i, (i + k) % hi) for i in range(hi)]) for k in range(1, hi)
    ]


def before(k):
    hi = lax.axis_size("hi")
    return lax.rem(lax.axis_index("hi") - k + hi, hi)


def after(k):
    return lax.rem(lax.axis_index("hi") + k, lax.axis_size("hi"))


def place_pieces(mine, pieces):
    rows = mine.shape[0]
    full = jnp.zeros((rows * lax.axis_size("hi"), mine.shape[1]), mine.dtype)
    full = lax.dynamic_update_slice(full, mine, (before(0) * rows, 0))
    for first, arrays in pieces:
        for k, part in enumerate(arrays, 1):
            full = lax.dynamic_update_slice(full, part, (before(k) * rows + first, 0))
    return full


def half_products(left, right):
    width = left.shape[1] // lax.axis_size("hi")
    parts = [
        dot(lax.dynamic_slice_in_dim(left, after(k) * width, width, axis=1), right, 0, 0)
        for k in range(lax.axis_size("hi"))
    ]
    return parts[0], [p.astype(BF16) for p in parts[1:]]


def small_sum(x):
    n = lax.axis_size("hi") * lax.axis_size("ep") * lax.axis_size("cp")
    rows, k = x.shape[0] // n, x.shape[1]
    flat = x.reshape(n, 1, rows * k)
    got = lax.all_to_all(flat, DENSE, split_axis=0, concat_axis=0, tiled=True)
    return jnp.sum(got, axis=(0, 1)).reshape(rows, k)


def rms_backward(rows, scale, gain, grad_norm):
    weighted = grad_norm * gain
    inner = jnp.mean(weighted * rows, axis=-1, keepdims=True)
    grad_rows = scale * weighted - rows * scale * scale * scale * inner
    return grad_rows, jnp.sum(grad_norm * rows * scale, axis=0)


def with_extra(main, *columns):
    rows = main.shape[0]
    columns = [c.reshape(rows, -1).astype(main.dtype) for c in columns]
    used = sum(c.shape[1] for c in columns)
    return jnp.concatenate([main, *columns, jnp.zeros((rows, -used % 128), main.dtype)], axis=1)


def local(
    layer_input,
    cotangent,
    pairing,
    routes,
    first_gain,
    second_gain,
    query_weight,
    key_weight,
    value_weight,
    out_weight,
    router_weight,
    gate_weight,
    up_weight,
    down_weight,
):
    n_seq = layer_input.shape[0]
    width = layer_input.shape[-1]
    rows = 2 * BLK
    tokens = n_seq * rows
    cp = lax.axis_size("cp")
    here = lax.axis_index("cp")
    blocks = 2 * cp
    n_q, n_kv = H * HD, KV * HD
    n_slots = EXPERTS * n_seq * CAP

    first = with_extra(
        jnp.concatenate([query_weight, key_weight, value_weight], axis=1), first_gain
    )
    second = with_extra(out_weight, router_weight, second_gain)
    second = lax.all_gather(second, DENSE, axis=0, tiled=True)
    first, gate_matrix, down = courier(
        0, ("gather", first), ("expert", gate_weight), ("quad", down_weight)
    )
    first = first.reshape(width, -1)
    down = down.reshape(-1, width)
    n_first = n_q + 2 * n_kv

    chosen = routes.reshape(tokens, 2)
    experts = jnp.arange(EXPERTS, dtype=jnp.int32)
    picks = chosen[:, :, None] == experts[None, None, :]
    named = jnp.any(picks, axis=1).astype(BF16)
    token = jnp.arange(tokens, dtype=jnp.int32)
    earlier = (token[None, :] < token[:, None]) & (token[None, :] // rows == token[:, None] // rows)
    before = dot(earlier.astype(BF16), named)
    rank = jnp.sum(jnp.where(picks, before[:, None, :], 0.0), axis=-1).astype(jnp.int32)
    slots = (chosen * n_seq + (token // rows)[:, None]) * CAP + rank
    slot = jnp.arange(n_slots, dtype=jnp.int32)
    at_slot = [slots[:, r][None, :] == slot[:, None] for r in range(2)]
    place_rows = (at_slot[0] | at_slot[1]).astype(BF16)
    take_rows = [(slots[:, r][:, None] == slot[None, :]).astype(BF16) for r in range(2)]

    def exchange(x):
        x = x.reshape(EXPERTS, n_seq * CAP, -1)
        x = lax.all_to_all(x, ("cp", "ep"), split_axis=0, concat_axis=0, tiled=True)
        return x.reshape(n_slots, -1)

    def exchange_scalar(x):
        x = x.reshape(EXPERTS, 1, n_seq * CAP)
        x = lax.all_to_all(x, ("cp", "ep"), split_axis=0, concat_axis=0, tiled=True)
        return x.reshape(n_slots)

    grad_rows = dot(place_rows, cotangent.reshape(tokens, width)).astype(BF16)
    qkv_matrix = first[:, :n_first]
    gain_one = first[:, n_first].astype(F32)
    out_matrix = second[:, :width]
    router_matrix = second[:, width : width + EXPERTS]
    gain_two = second[:, width + EXPERTS].astype(F32)

    resid = layer_input.reshape(tokens, width).astype(F32)
    scale_one = lax.rsqrt(jnp.mean(resid * resid, axis=-1, keepdims=True) + EPS)
    attn_in = (resid * scale_one * gain_one).astype(BF16)
    qkv = dot(attn_in, qkv_matrix).astype(BF16)
    queries = qkv[:, :n_q]
    kv = qkv[:, n_q:].reshape(n_seq, rows, 2, n_kv).transpose(0, 2, 1, 3)
    kv_all, up_matrix = courier(1, ("peers", kv), ("expert", up_weight))
    ids = jnp.stack([pairing, blocks - 1 - pairing], axis=2).reshape(n_seq, blocks)
    order = jnp.arange(blocks, dtype=jnp.int32)
    table = jnp.sum(jnp.where(ids[:, :, None] == order, order[None, :, None], 0), axis=1)
    place = lax.dynamic_index_in_dim(pairing, here, axis=1, keepdims=False)
    grad_rows = exchange(tie(grad_rows, kv_all))
    attn_out = attend(table, place, queries, kv_all)
    attn_out = tie(attn_out, grad_rows)
    middle = resid + dot(attn_out, out_matrix)
    scale_two = lax.rsqrt(jnp.mean(middle * middle, axis=-1, keepdims=True) + EPS)
    moe_in = (middle * scale_two * gain_two).astype(BF16)

    rows_out = dot(place_rows, moe_in).astype(BF16)
    down_piece = swap(down)
    arrived = exchange(rows_out)
    down_matrix = place_pieces(down, [(0, down_piece)])
    gate_pre = dot(arrived, gate_matrix)
    up_pre = dot(arrived, up_matrix)
    sigmoid_gate = jax.nn.sigmoid(gate_pre)
    swish = gate_pre * sigmoid_gate
    hidden = (swish * up_pre).astype(BF16)
    produced = dot(hidden, down_matrix).astype(BF16)
    hidden_grad = dot(grad_rows, down_matrix, 1, 1)
    gate_inner = exchange_scalar(jnp.sum(hidden_grad * hidden.astype(F32), axis=1))
    gate_pre_grad = hidden_grad * up_pre * sigmoid_gate * (1.0 + gate_pre * (1.0 - sigmoid_gate))
    gate_pre_grad = gate_pre_grad.astype(BF16)
    up_pre_grad = (hidden_grad * swish).astype(BF16)
    grad_back = dot(gate_pre_grad, gate_matrix, 1, 1) + dot(up_pre_grad, up_matrix, 1, 1)
    grad_back = grad_back.astype(BF16)

    logits = dot(moe_in, router_matrix)
    pick_f = picks.astype(F32)
    picked = jnp.sum(pick_f * logits[:, None, :], axis=-1)
    powers = jnp.exp(picked - jnp.max(picked, axis=-1, keepdims=True))
    gates = powers / jnp.sum(powers, axis=-1, keepdims=True)
    gate_slot = jnp.sum(
        sum(jnp.where(at_slot[r], gates[:, r][None, :], 0.0) for r in range(2)), axis=1
    )
    gate_slot = exchange_scalar(tie(gate_slot, arrived))[:, None]

    arrived_gated = (arrived.astype(F32) * gate_slot).astype(BF16)
    gate_part = dot(arrived_gated, gate_pre_grad, 0, 0).astype(BF16)
    up_part = dot(arrived_gated, up_pre_grad, 0, 0).astype(BF16)
    down_own, down_sent = half_products(
        hidden, (grad_rows.astype(F32) * gate_slot).astype(BF16)
    )
    down_sent = swap(down_sent)
    grad_returned, gate_part, up_part, down_own = lax.optimization_barrier(
        (exchange(grad_back), gate_part, up_part, down_own)
    )

    returned = exchange(tie(produced, grad_returned))
    back = [dot(take_rows[r], returned) for r in range(2)]
    final = middle + gates[:, :1] * back[0] + gates[:, 1:] * back[1]
    layer_output = final.astype(BF16)
    grad_final = cotangent.reshape(tokens, width).astype(F32)
    gate_inner = jnp.stack(
        [jnp.sum(jnp.where(a, gate_inner[:, None], 0.0), axis=0) for a in at_slot], axis=1
    )
    pair_grad = gates * (gate_inner - jnp.sum(gates * gate_inner, axis=-1, keepdims=True))
    logit_grad = jnp.sum(pick_f * pair_grad[:, :, None], axis=1)
    moe_in_grad = jnp.dot(logit_grad, router_matrix.astype(F32).T, precision=HIGH)
    for r in range(2):
        moe_in_grad = moe_in_grad + gates[:, r : r + 1] * dot(take_rows[r], grad_returned)
    router_part = jnp.dot(moe_in.astype(F32).T, logit_grad, precision=HIGH)
    middle_norm_grad, gain_two_grad = rms_backward(middle, scale_two, gain_two, moe_in_grad)
    middle_grad = grad_final + middle_norm_grad
    branch_grad = middle_grad.astype(BF16)
    out_part = dot(attn_out, branch_grad, 0, 0).astype(BF16)
    router_sum = small_sum(tie(router_part, returned))
    attn_out_grad = dot(branch_grad, out_matrix, 1, 1).astype(BF16)
    attn_out_grad = tie(attn_out_grad, out_part)
    query_grad, kv_grad, gate_parts = attend_back(
        2, table, ids, place, queries, kv_all, attn_out_grad, ("owners", gate_part)
    )
    kv_grad = tie(kv_grad, returned, *down_sent)
    kv_grad = jnp.sum(kv_grad.astype(F32), axis=0).astype(BF16)
    kv_grad = kv_grad.transpose(0, 2, 1, 3).reshape(tokens, 2 * n_kv)
    qkv_grad = jnp.concatenate([query_grad, kv_grad], axis=1)
    first_part = dot(attn_in, qkv_grad, 0, 0).astype(BF16)
    first_sum, up_parts = dense_sum(
        3, [first_part, out_part], ("owners", up_part)
    )
    attn_in_grad = dot(qkv_grad, qkv_matrix, 1, 1)
    resid_norm_grad, gain_one_grad = rms_backward(resid, scale_one, gain_one, attn_in_grad)
    input_grad = middle_grad + resid_norm_grad
    down_sum = tie(down_own, query_grad, returned) + sum(d.astype(F32) for d in down_sent)
    down_sum = quad(down_sum.astype(BF16).reshape(down_weight.shape)).astype(F32)

    def own_sum(parts):
        halves = parts.reshape((-1,) + gate_weight.shape)
        return jnp.sum(halves.astype(F32), axis=0)

    gain_sum = small_sum(jnp.stack([gain_one_grad, gain_two_grad], axis=1))
    return (
        layer_output.reshape(layer_input.shape),
        input_grad.reshape(layer_input.shape),
        gain_sum[:, 0],
        gain_sum[:, 1],
        first_sum[:, :n_q],
        first_sum[:, n_q : n_q + n_kv],
        first_sum[:, n_q + n_kv : n_first],
        first_sum[:, n_first:],
        router_sum,
        own_sum(gate_parts),
        own_sum(up_parts),
        down_sum,
    )


def solution(mesh):
    fsdp, cp = mesh.shape["fsdp"], mesh.shape["cp"]
    ep = EXPERTS // cp
    finer = Mesh(mesh.devices.reshape(fsdp // ep, ep, cp), DENSE)
    rows = ("hi", "ep")
    block = P(rows, "cp", None, None, None)
    dense, vector, expert = P(DENSE, None), P(DENSE), P("cp", rows, None)
    in_specs = (block, block, P(rows, None), block) + (vector,) * 2 + (dense,) * 5 + (expert,) * 3
    out_specs = (block,) * 2 + (vector,) * 2 + (dense,) * 5 + (expert,) * 3
    return jax.shard_map(
        local, mesh=finer, in_specs=in_specs, out_specs=out_specs, check_vma=False
    )
```

time: 2890 us -> 914 us (0.32)
  waiting for transfers between devices: 1730 us -> 153 us
  Pallas kernels: 0 us -> 436 us
  matrix products: 555 us -> 168 us
  blocking collectives: 256 us -> 0 us
  other arithmetic: 143 us -> 31.8 us
  local copies, waits for them, and re-layouts: 145 us -> 34 us
  starting transfers between devices: 32.1 us -> 69.3 us
    reduce_scatter x11 -> x0, waiting for transfers between devices: 884 us -> none  [the longest x4 492 us: local(): lax.psum_scatter(totals[0], ('fsdp', 'cp'), scatter_dimension=0, tiled=True)]
    all_gather x18 -> x1, waiting for transfers between devices: 786 us -> 0.01 us  [local(): second = lax.all_gather(second, DENSE, axis=0, tiled=True)]
    pallas_call x0 -> x5, Pallas kernels: none -> 436 us  [the longest x2 191 us: courier(): pl.pallas_call(functools.partial(courier_kernel, sizes, kinds), out_shape...]
    dot_general x160 -> x26, matrix products: 555 us -> 168 us  [the longest x24 163 us: dot(): lax.dot_general(a, b, (((ca,), (cb,)), ((), ())), preferred_element_type=...]
    all_gather x2 -> x0, blocking collectives: 135 us -> none  [step(): lax.all_gather(small_params[6], ('fsdp', 'cp'), axis=0, tiled=True)]
    ppermute x0 -> x2, waiting for transfers between devices: none -> 88.3 us  [swap(): lax.ppermute(xs[k - 1], 'hi', [(i, (i + k) % hi) for i in range(hi)])]
    while x2 -> x0, blocking collectives: 81.7 us -> none
    convert_element_type x38 -> x6, other arithmetic: 70.3 us -> 8.74 us  [the longest x1 3.48 us: local(): quad(down_sum.astype(BF16).reshape(down_weight.shape)).astype(F32)]
  transfers between devices with their start and end apart: 38 -> 12, of which waited for: 27 -> 5; matrix products, arithmetic and copies ran while one was open for 19% -> 17% of each run, Pallas kernels for 0% -> 48%
where the time goes in v1:
time: 914 us; the launch traced here: 907 us
  Pallas kernels  436 us (48%)
  matrix products  168 us (18%)
  waiting for transfers between devices  153 us (17%)
  starting transfers between devices  69.3 us (8%)
  local copies, waits for them, and re-layouts  34 us (4%)
  other arithmetic  31.8 us (3%)
  between operations  15 us (2%)
    pallas_call x2, Pallas kernels, courier(): pl.pallas_call(functools.partial(courier_kernel, sizes, kinds), out_shape...  191 us
    dot_general x24, matrix products, dot(): lax.dot_general(a, b, (((ca,), (cb,)), ((), ())), preferred_element_type=...  163 us
    pallas_call x1, Pallas kernels, attend_back(): pl.pallas_call(functools.partial(attend_back_kernel, sizes, kinds), grid=...  113 us
    pallas_call x1, Pallas kernels, dense_sum(): pl.pallas_call(functools.partial(dense_sum_kernel, sizes, kinds, len(part...  109 us
    ppermute x2, waiting for transfers between devices, swap(): lax.ppermute(xs[k - 1], 'hi', [(i, (i + k) % hi) for i in range(hi)])  88.3 us
    all_to_all x4, waiting for transfers between devices, exchange(): x = lax.all_to_all(x, ('cp', 'ep'), split_axis=0, concat_axis=0, tiled=True)  54.3 us
    all_to_all x4, starting transfers between devices, exchange(): x = lax.all_to_all(x, ('cp', 'ep'), split_axis=0, concat_axis=0, tiled=True)  37.9 us
    pallas_call x1, Pallas kernels, attend(): pl.pallas_call(attend_kernel, grid_spec=pltpu.PrefetchScalarGridSpec(num_...  22.9 us
  transfers between devices with their start and end apart: 12, of which 5 were waited for; matrix products, arithmetic and copies ran while one was open for 17% of the time, Pallas kernels for 48%

profile of v1, /device:TPU:0, one launch (start us, length us, event | category | flops | bytes accessed | tf_op | source)
XLA Modules:
  0.0 907.5 jit_solution(15897714098489047793)
XLA Ops:
  13.1 123.9 %shard_map.229 = (bf16[32,48,2688]{2,1,0:T(8,128)(2,1)}, bf16[1536,1024]{1,0:T(8,128)(2,1)}, bf16[4,128,1536]{2,1,0:T(8,128)(2,1)}) custom-call(bf16[48,2688]{1,0:T(8,128)(2,1)} %concatenate.13.refs_0_, bf16[4,192,1024]{2,1,0:T(8,128)(2,1)} %refs_1_.2, bf16[4,128,1536]{2,1,0:T(8,128)(2,1)} %refs_2_.1), custom_call_target="tpu_custom_call" | custom-call | tf_op jit(solution)/shard_map/pallas_call | solution.py:485
  139.7 8.3 fusion.5
  151.6 67.2 %shard_map.230 = (bf16[4,2,2,256,512]{4,3,2,1,0:T(8,128)(2,1)}, bf16[1536,1024]{1,0:T(8,128)(2,1)}) custom-call(bf16[2,2,256,512]{3,2,1,0:T(8,128)(2,1)} %bitcast.110, bf16[4,192,1024]{2,1,0:T(8,128)(2,1)} %refs_1_.3), custom_call_target="tpu_custom_call" | custom-call | tf_op jit(solution)/shard_map/pallas_call | solution.py:485
  223.1 20.2 %all-to-all-start = ((bf16[16,96,1536]{2,1,0:T(8,128)(2,1)}), bf16[16,96,1536]{2,1,0:T(8,128)(2,1)}, u32[]{:S(2)}, u32[]{:S(2)}) async-start(bf16[16,96,1536]{2,1,0:T(8,128)(2,1)} %bitcast.108), calls=%async_computation | async-start | bytes 9437184 | tf_op jit(solution)/shard_map/all_to_all | solution.py:723
  246.2 22.9 %shard_map.231 = bf16[512,1536]{1,0:T(8,128)(2,1)} custom-call(s32[2,8]{1,0:T(2,128)} %select_reduce_fusion.5.table, s32[2]{0:T(128)} %fusion.65.place, bf16[512,1536]{1,0:T(8,128)(2,1)} %slice.76.q_ref, bf16[4,2,2,256,512]{4,3,2,1,0:T(8,128)(2,1)} %get-tuple-element.35.kv_ref), custom_call_target="tpu_custom_call" | custom-call | flops 17179869184 | bytes 16777216 | tf_op jit(solution)/shard_map/pallas_call | solution.py:231
  269.1 32.7 %all-to-all-done = bf16[16,96,1536]{2,1,0:T(8,128)(2,1)} async-done(((bf16[16,96,1536]{2,1,0:T(8,128)(2,1)}), bf16[16,96,1536]{2,1,0:T(8,128)(2,1)}, u32[]{:S(2)}, u32[]{:S(2)}) %all-to-all-start) | async-done | bytes 4718624 | tf_op jit(solution)/shard_map/all_to_all | solution.py:723
  323.9 88.3 %collective-permute-done = bf16[512,1536]{1,0:T(8,128)(2,1)} collective-permute-done((bf16[512,1536]{1,0:T(8,128)(2,1)}, bf16[512,1536]{1,0:T(8,128)(2,1)}, u32[]{:S(2)}, u32[]{:S(2)}) %collective-permute-start) | collective-permute-done | bytes 1572896 | tf_op jit(solution)/shard_map/ppermute | solution.py:615
  415.7 8.2 fusion.71
  424.0 7.4 fusion.70
  431.5 12.3 %multiply_reduce_fusion = (f32[1536]{0:T(1024)S(1)}, bf16[1536,1024]{0,1:T(8,128)(2,1)}, bf16[1536,1024]{0,1:T(8,128)(2,1)}, bf16[1536,1024]{0,1:T(8,128)(2,1)}) fusion(f32[1536,1024]{0,1:T(8,128)S(1)} %fusion.71, f32[1536,1024]{0,1:T(8,128)S(1)} %fusion.70, bf16[1536,1536]{1,0:T(8,128)(2,1)} %bitcast.12, bf16[1024,1536]{1,0:T(8,128)(2,1)S(1)} %copy-done.8), kind=kOutput, calls=%fused_computation.14 | convolution fusion | flops 4860148224 | bytes 29890560 | tf_op jit(solution)/shard_map/dot_general | solution.py:28
  451.0 10.0 %fusion.72 = f32[1536,1536]{1,0:T(8,128)} fusion(bf16[1536,1024]{0,1:T(8,128)(2,1)} %get-tuple-element.115, bf16[1536,1024]{1,0:T(8,128)(2,1)} %get-tuple-element.38), kind=kOutput, calls=%fused_computation.136 | convolution fusion | flops 4831838208 | bytes 15728640 | tf_op jit(solution)/shard_map/dot_general | solution.py:28
  470.0 10.6 %add_convert_fusion = bf16[1536,1536]{1,0:T(8,128)(2,1)} fusion(f32[1536,1536]{1,0:T(8,128)} %fusion.72, bf16[1536,1024]{0,1:T(8,128)(2,1)} %get-tuple-element.116, bf16[1536,1024]{1,0:T(8,128)(2,1)} %get-tuple-element.39), kind=kOutput, calls=%fused_computation.3 | convolution fusion | flops 4836556800 | bytes 20447232 | tf_op jit(solution)/shard_map/dot_general | solution.py:28
  486.0 9.2 %convolution_convert_fusion.1 = bf16[1536,1536]{1,0:T(8,128)(2,1)} fusion(bf16[1536,1024]{0,1:T(8,128)(2,1)} %get-tuple-element.114, bf16[1024,1536]{1,0:T(8,128)(2,1)} %copy-done.7), kind=kOutput, calls=%fused_computation.4 | convolution fusion | flops 4834197504 | bytes 11010048 | tf_op jit(solution)/shard_map/dot_general | solution.py:28
  496.0 7.3 fusion.36
  503.3 9.8 %convolution_convert_fusion.6.refs_0_ = bf16[1536,1024]{1,0:T(8,128)(2,1)} fusion(bf16[1536,1024]{0,1:T(8,128)(2,1)S(1)} %copy-done.29, bf16[1536,1536]{1,0:T(8,128)(2,1)} %bitcast.16, f32[1536]{0:T(1024)S(1)} %mul.280), kind=kOutput, calls=%fused_computation.26 | convolution fusion | flops 4840488960 | bytes 11016192 | tf_op jit(solution)/shard_map/dot_general | solution.py:28
  513.1 9.7 %convolution_convert_fusion.5.refs_2_ = bf16[1536,1024]{1,0:T(8,128)(2,1)} fusion(bf16[1536,1024]{0,1:T(8,128)(2,1)S(1)} %copy-done.28, bf16[1536,1536]{1,0:T(8,128)(2,1)} %bitcast.16, f32[1536]{0:T(1024)S(1)} %mul.280), kind=kOutput, calls=%fused_computation.25 | convolution fusion | flops 4840488960 | bytes 11016192 | tf_op jit(solution)/shard_map/dot_general | solution.py:28
  522.8 21.6 %all-to-all-done.2 = bf16[16,96,1536]{2,1,0:T(8,128)(2,1)} async-done(((bf16[16,96,1536]{2,1,0:T(8,128)(2,1)}), bf16[16,96,1536]{2,1,0:T(8,128)(2,1)}, u32[]{:S(2)}, u32[]{:S(2)}) %all-to-all-start.2) | async-done | bytes 4718624 | tf_op jit(solution)/shard_map/all_to_all | solution.py:723
  552.7 6.7 convolution_convert_fusion.7
  582.0 113.0 %shard_map.232 = (bf16[512,1536]{1,0:T(8,128)(2,1)}, bf16[4,2,2,256,512]{4,3,2,1,0:T(8,128)(2,1)}, bf16[8,192,1024]{2,1,0:T(8,128)(2,1)}) custom-call(s32[2,8]{1,0:T(2,128)} %select_reduce_fusion.5.table, s32[2,8]{1,0:T(2,128)} %copy-done.24, s32[2]{0:T(128)} %fusion.65.place, bf16[512,1536]{1,0:T(8,128)(2,1)} %slice.76.q_ref, ...), custom_call_target="tpu_custom_call" | custom-call | flops 17179869184 | bytes 16777216 | tf_op jit(solution)/shard_map/pallas_call | solution.py:258
  701.0 6.6 convolution_multiply_fusion.2
  714.6 9.7 %fusion.20 = (f32[1536]{0:T(1024)S(1)}, f32[512]{0:T(512)S(1)}, f32[512,1536]{1,0:T(8,128)}) fusion(bf16[2,1,2,128,1536]{4,3,2,1,0:T(8,128)(2,1)S(1)} %copy-done.3, f32[512]{0:T(512)S(1)} %bitcast.131, f32[1536]{0:T(1024)S(1)} %copy-done.20, bf16[512,2560]{1,0:T(8,128)(2,1)S(1)} %constant_dynamic-update-slice_fusion, bf16[1536,2688]{1,0:T(8,128)(2,1)} %bitcast.129), kind=kOutput, calls=%fused_computation.41 | convolution fusion | flops 4032034816 | bytes 15220736 | tf_op jit(solution)/shard_map/dot_general | solution.py:28
  724.2 6.5 convolution_convert_fusion
  734.0 8.5 all-to-all-start.6
  742.6 109.2 %shard_map.233 = (f32[48,4096]{1,0:T(8,128)}, bf16[8,192,1024]{2,1,0:T(8,128)(2,1)}) custom-call(bf16[32,48,2560]{2,1,0:T(8,128)(2,1)} %bitcast.103, bf16[32,48,1536]{2,1,0:T(8,128)(2,1)} %bitcast.109, bf16[1536,1024]{1,0:T(8,128)(2,1)} %convolution_convert_fusion.5.refs_2_), custom_call_target="tpu_custom_call" | custom-call | tf_op jit(solution)/shard_map/pallas_call | solution.py:583
  (175 shorter events, 162.4 us)
Async XLA Ops:
  7.2 131.1 %copy-start.2 = (bf16[2,1,2,128,1536]{4,3,2,1,0:T(8,128)(2,1)S(1)}, bf16[2,1,2,128,1536]{4,3,2,1,0:T(8,128)(2,1)}, u32[]{:S(2)}) copy-start(bf16[2,1,2,128,1536]{4,3,2,1,0:T(8,128)(2,1)} %param.14) | copy-start | bytes 4718596
  7.2 294.6 %all-gather.2.cloned.1.call-start = ((), (), s32[]{:S(2)}) async-start(), calls=%async_computation.9 | async-start | bytes 5271552 | tf_op jit(solution)/shard_map/all_gather | solution.py:699
  139.7 8.3 copy-start.12
  139.7 8.3 copy-start.18
  150.4 68.4 %copy-start.15 = (bf16[2,1,2,128,1536]{4,3,2,1,0:T(8,128)(2,1)S(1)}, bf16[2,1,2,128,1536]{4,3,2,1,0:T(8,128)(2,1)}, u32[]{:S(2)}) copy-start(bf16[2,1,2,128,1536]{4,3,2,1,0:T(8,128)(2,1)} %param.15) | copy-start | bytes 4718596
  223.1 20.3 %copy-start.10 = (bf16[512,2560]{1,0:T(8,128)(2,1)S(1)}, bf16[512,2560]{1,0:T(8,128)(2,1)}, u32[]{:S(2)}) copy-start(bf16[512,2560]{1,0:T(8,128)(2,1)} %copy-done.9) | copy-start | bytes 7864324
  223.1 78.7 %all-to-all-start = ((bf16[16,96,1536]{2,1,0:T(8,128)(2,1)}), bf16[16,96,1536]{2,1,0:T(8,128)(2,1)}, u32[]{:S(2)}, u32[]{:S(2)}) async-start(bf16[16,96,1536]{2,1,0:T(8,128)(2,1)} %bitcast.108), calls=%async_computation | async-start | bytes 9437184 | tf_op jit(solution)/shard_map/all_to_all | solution.py:723
  244.8 24.3 %copy-start.24 = (s32[2,8]{1,0:T(2,128)}, s32[2,8]{1,0:T(2,128)S(1)}, u32[]{:S(2)}) copy-start(s32[2,8]{1,0:T(2,128)S(1)} %eq.48.inverse) | copy-start | bytes 196
  313.7 102.0 %all-to-all-start.1 = ((bf16[16,96,1536]{2,1,0:T(8,128)(2,1)}), bf16[16,96,1536]{2,1,0:T(8,128)(2,1)}, u32[]{:S(2)}, u32[]{:S(2)}) async-start(bf16[16,96,1536]{2,1,0:T(8,128)(2,1)} %bitcast.106), calls=%async_computation.1 | async-start | bytes 9437184 | tf_op jit(solution)/shard_map/all_to_all | solution.py:723
  319.9 92.3 %collective-permute-start = (bf16[512,1536]{1,0:T(8,128)(2,1)}, bf16[512,1536]{1,0:T(8,128)(2,1)}, u32[]{:S(2)}, u32[]{:S(2)}) collective-permute-start(bf16[512,1536]{1,0:T(8,128)(2,1)} %bitcast.117), channel_id=1, source_target_pairs={{0,16},{16,0},{1,17},{17,1},{2,18},{18,2},{3,19},{19,3},{4,20},{20... | collective-permute-start | bytes 4718600 | tf_op jit(solution)/shard_map/ppermute | solution.py:615
  323.7 90.0 %copy-start.1 = (bf16[512,1536]{1,0:T(8,128)(2,1)S(1)}, bf16[512,1536]{1,0:T(8,128)(2,1)}, u32[]{:S(2)}) copy-start(bf16[512,1536]{1,0:T(8,128)(2,1)} %copy-done) | copy-start | bytes 4718596
  415.7 8.3 copy-start.25
  444.5 16.5 %all-to-all-start.5 = ((f32[16,1,96]{2,1,0:T(1,128)}), f32[16,1,96]{2,1,0:T(1,128)S(1)}, u32[]{:S(2)}, u32[]{:S(2)}) async-start(f32[16,1,96]{2,1,0:T(1,128)} %reshape.333), calls=%async_computation.5 | async-start | bytes 16384 | tf_op jit(solution)/shard_map/all_to_all | solution.py:728
  464.8 15.8 %all-to-all-start.3 = ((f32[16,1,96]{2,1,0:T(1,128)}), f32[16,1,96]{2,1,0:T(1,128)S(1)}, u32[]{:S(2)}, u32[]{:S(2)}) async-start(f32[16,1,96]{2,1,0:T(1,128)} %reshape.329), calls=%async_computation.3 | async-start | bytes 16384 | tf_op jit(solution)/shard_map/all_to_all | solution.py:728
  480.6 63.9 %all-to-all-start.2 = ((bf16[16,96,1536]{2,1,0:T(8,128)(2,1)}), bf16[16,96,1536]{2,1,0:T(8,128)(2,1)}, u32[]{:S(2)}, u32[]{:S(2)}) async-start(bf16[16,96,1536]{2,1,0:T(8,128)(2,1)} %bitcast.107), calls=%async_computation.2 | async-start | bytes 9437184 | tf_op jit(solution)/shard_map/all_to_all | solution.py:723
  503.3 9.8 %copy-start.28 = (bf16[1536,1024]{0,1:T(8,128)(2,1)S(1)}, bf16[1536,1024]{0,1:T(8,128)(2,1)}, u32[]{:S(2)}) copy-start(bf16[1536,1024]{0,1:T(8,128)(2,1)} %get-tuple-element.116) | copy-start | bytes 9437188
  544.4 156.5 %all-to-all-start.4 = ((bf16[16,96,1536]{2,1,0:T(8,128)(2,1)}), bf16[16,96,1536]{2,1,0:T(8,128)(2,1)}, u32[]{:S(2)}, u32[]{:S(2)}) async-start(bf16[16,96,1536]{2,1,0:T(8,128)(2,1)} %bitcast.105), calls=%async_computation.4 | async-start | bytes 9437184 | tf_op jit(solution)/shard_map/all_to_all | solution.py:723
  559.4 148.2 %collective-permute-start.1 = (bf16[512,1536]{1,0:T(8,128)(2,1)}, bf16[512,1536]{1,0:T(8,128)(2,1)}, u32[]{:S(2)}, u32[]{:S(2)}) collective-permute-start(bf16[512,1536]{1,0:T(8,128)(2,1)} %convolution_convert_fusion.7), channel_id=1, source_target_pairs={{0,16},{16,0},{1,17},{17,1},{2,18},{18,2},{3,19},{19,3},{4,20},{20... | collective-permute-start | bytes 4718600 | tf_op jit(solution)/shard_map/ppermute | solution.py:615
  559.9 9.7 %slice-start = ((s8[5111808]{0:T(1024)(128)(4,1)}), s8[4194304]{0:T(1024)(128)(4,1)S(1)}, s32[]{:S(2)}) async-start(s8[5111808]{0:T(1024)(128)(4,1)} %bitcast.120), calls=%async_computation.10 | async-start | bytes 8388608
  714.6 9.7 %copy-start.13 = (bf16[512,1536]{1,0:T(8,128)(2,1)S(1)}, bf16[512,1536]{1,0:T(8,128)(2,1)}, u32[]{:S(2)}) copy-start(bf16[512,1536]{1,0:T(8,128)(2,1)} %copy-done.12) | copy-start | bytes 4718596
  734.0 126.6 %all-to-all-start.6 = ((f32[32,1,96]{2,1,0:T(1,128)}), f32[32,1,96]{2,1,0:T(1,128)S(1)}, u32[]{:S(2)}, u32[]{:S(2)}) async-start(f32[32,1,96]{2,1,0:T(1,128)} %bitcast.30), calls=%async_computation.6 | async-start | bytes 32768 | tf_op jit(solution)/shard_map/all_to_all | solution.py:651
  742.6 109.2 %copy-start.5 = (f32[512,1536]{1,0:T(8,128)S(1)}, f32[512,1536]{1,0:T(8,128)}, u32[]{:S(2)}) copy-start(f32[512,1536]{1,0:T(8,128)} %fusion.36) | copy-start | bytes 9437188
  860.6 11.9 %all-to-all-start.7 = ((f32[32,1,768]{2,1,0:T(1,128)}), f32[32,1,768]{2,1,0:T(1,128)S(1)}, u32[]{:S(2)}, u32[]{:S(2)}) async-start(f32[32,1,768]{2,1,0:T(1,128)} %reshape.348), calls=%async_computation.7 | async-start | bytes 196608 | tf_op jit(solution)/shard_map/all_to_all | solution.py:651
  872.5 24.5 %all-to-all-start.8 = ((bf16[4,128,1536]{2,1,0:T(8,128)(2,1)}), bf16[4,128,1536]{2,1,0:T(8,128)(2,1)}, u32[]{:S(2)}, u32[]{:S(2)}) async-start(bf16[4,128,1536]{2,1,0:T(8,128)(2,1)} %bitcast.104), calls=%async_computation.8 | async-start | bytes 3145728 | tf_op jit(solution)/shard_map/all_to_all | solution.py:608
  (20 other events, 64.8 us)
Sparse Core Ops, SparseCore 0:
  11.5 118.1 all-gather.1

commit v2 on v1

--- a/solution.py
+++ b/solution.py
@@ -52,35 +52,21 @@
     return jnp.concatenate(rows, axis=0)
 
 
-def attend_kernel(table, place, q_ref, kv_ref, o_ref, k_s, v_s, low_bias, high_bias):
-    seq = pl.program_id(0)
-    blocks = 2 * kv_ref.shape[0]
-    half = blocks * BLK // 2
+def attend_group(q_all, k_all, v_all, low_bias, high_bias):
+    half = k_all.shape[0] // 2
     rows = GROUP * BLK
-    at = place[seq]
-
-    @pl.when(pl.program_id(1) == 0)
-    def _():
-        query = lax.broadcasted_iota(jnp.int32, (BLK, half), 0)
-        key = lax.broadcasted_iota(jnp.int32, (BLK, half), 1)
-        low_bias[...] = jnp.where(key <= query + at * BLK, 0.0, NEG)
-        high_bias[...] = jnp.where(key + half <= query + (blocks - 1 - at) * BLK, 0.0, NEG)
-
-    sort_blocks(table, seq, kv_ref, k_s, 0, blocks)
-    sort_blocks(table, seq, kv_ref, v_s, 1, blocks)
-    q_all = q_ref[...]
     lows, highs = [], []
     for j in range(PACK):
-        k = k_s[:, j * HD : (j + 1) * HD]
-        v = v_s[:, j * HD : (j + 1) * HD]
+        k = k_all[:, j * HD : (j + 1) * HD]
+        v = v_all[:, j * HD : (j + 1) * HD]
         q = stack_heads(q_all, j * GROUP, SCALE)
-        s_low = dot(q[:rows], k[:half], 1, 1) + jnp.concatenate([low_bias[...]] * GROUP, axis=0)
+        s_low = dot(q[:rows], k[:half], 1, 1) + jnp.concatenate([low_bias] * GROUP, axis=0)
         peak = jnp.max(s_low, axis=-1, keepdims=True)
         e_low = jnp.exp(s_low - peak)
         total = jnp.sum(e_low, axis=-1, keepdims=True)
         lows.append((dot(e_low.astype(BF16), v[:half]) / total).astype(BF16))
         s_one = dot(q[rows:], k[:half], 1, 1)
-        s_two = dot(q[rows:], k[half:], 1, 1) + jnp.concatenate([high_bias[...]] * GROUP, axis=0)
+        s_two = dot(q[rows:], k[half:], 1, 1) + jnp.concatenate([high_bias] * GROUP, axis=0)
         peak = jnp.maximum(
             jnp.max(s_one, axis=-1, keepdims=True), jnp.max(s_two, axis=-1, keepdims=True)
         )
@@ -89,7 +75,29 @@
         total = jnp.sum(e_one, axis=-1, keepdims=True) + jnp.sum(e_two, axis=-1, keepdims=True)
         mixed = dot(e_one.astype(BF16), v[:half]) + dot(e_two.astype(BF16), v[half:])
         highs.append((mixed / total).astype(BF16))
-    o_ref[...] = unstack_heads(lows, highs)
+    return unstack_heads(lows, highs)
+
+
+def query_bias(at, blocks):
+    half = blocks * BLK // 2
+    query = lax.broadcasted_iota(jnp.int32, (BLK, half), 0)
+    key = lax.broadcasted_iota(jnp.int32, (BLK, half), 1)
+    low = jnp.where(key <= query + at * BLK, 0.0, NEG)
+    high = jnp.where(key + half <= query + (blocks - 1 - at) * BLK, 0.0, NEG)
+    return low, high
+
+
+def attend_kernel(table, place, q_ref, kv_ref, o_ref, k_s, v_s, low_bias, high_bias):
+    seq = pl.program_id(0)
+    blocks = 2 * kv_ref.shape[0]
+
+    @pl.when(pl.program_id(1) == 0)
+    def _():
+        low_bias[...], high_bias[...] = query_bias(place[seq], blocks)
+
+    sort_blocks(table, seq, kv_ref, k_s, 0, blocks)
+    sort_blocks(table, seq, kv_ref, v_s, 1, blocks)
+    o_ref[...] = attend_group(q_ref[...], k_s[...], v_s[...], low_bias[...], high_bias[...])
 
 
 def attend_back_kernel(
@@ -387,6 +395,17 @@
                 for m in range(1, cp):
                     post(x, out.at[my_cp], {"cp": plus(my_cp, m, cp)})
                 keep(x, out.at[my_cp])
+            elif kind == "tokens":
+                for a in range(ep):
+                    for b in range(cp):
+                        if a or b:
+                            to_ep, to_cp = plus(my_ep, a, ep), plus(my_cp, b, cp)
+                            post(
+                                x.at[to_cp * ep + to_ep],
+                                out.at[my_cp * ep + my_ep],
+                                {"ep": to_ep, "cp": to_cp},
+                            )
+                keep(x.at[my_cp * ep + my_ep], out.at[my_cp * ep + my_ep])
         return away, local
 
     def begin(self, *jobs):
@@ -490,6 +509,136 @@
         scratch_shapes=post_scratch(jobs_messages(kinds, *sizes), len(jobs)),
         compiler_params=pltpu.CompilerParams(collective_id=collective_id, has_side_effects=True),
     )(*arrays)
+
+
+def front_kernel(sizes, kinds, table, place, x_ref, shard_ref, *refs):
+    n = len(kinds)
+    ins = refs[:n]
+    a_ref, q_ref, o_ref, kv_ref, w_ref = refs[n : n + 5]
+    outs = refs[n + 5 : 2 * n + 5]
+    rest = refs[2 * n + 5 :]
+    w_all, kv_mine, k_s, v_s, low_bias, high_bias = rest[:6]
+    office = PostOffice(sizes, rest[6:9])
+    kv_send, kv_recv, kv_here = rest[9:12]
+    kv_bufs = rest[12:]
+    n_seq, cp, my_cp = len(kv_bufs), sizes[2], office.my_cp
+    rows = 2 * BLK
+    wide = KV * HD
+    office.greet(kinds)
+    gather = office.gather(shard_ref, w_all, jobs_messages(kinds, *sizes), n)
+    next(gather)
+    office.begin(kinds, ins, outs)
+    x = x_ref[...].astype(F32)
+    x = x * lax.rsqrt(jnp.mean(x * x, axis=-1, keepdims=True) + EPS)
+    next(gather)
+    depth = x.shape[1]
+    keep_w = pltpu.make_async_copy(w_all, w_ref, kv_here.at[2 * n_seq])
+    keep_w.start()
+    last = pl.ds(H * HD + 2 * wide, 128)
+    gain = w_all[:, :, last].astype(F32).reshape(depth, 128).T[:1]
+    a_ref[...] = (x * gain).astype(BF16)
+
+    def project(first):
+        return dot(a_ref[...], w_all[:, :, pl.ds(first, wide)].reshape(depth, wide)).astype(BF16)
+
+    for part in range(2):
+        piece = project(H * HD + part * wide)
+        for s in range(n_seq):
+            kv_mine[s, part] = piece[s * rows : (s + 1) * rows]
+    copies = []
+    for s in range(n_seq):
+        group = [
+            mesh_copy(
+                kv_mine.at[s],
+                kv_bufs[s].at[my_cp],
+                (kv_send, kv_recv),
+                s * (cp - 1) + m - 1,
+                {"cp": plus(my_cp, m, cp)},
+            )
+            for m in range(1, cp)
+        ]
+        group.append(pltpu.make_async_copy(kv_mine.at[s], kv_bufs[s].at[my_cp], kv_here.at[s]))
+        for c in group:
+            c.start()
+        copies.append(group)
+
+    @pl.loop(0, H * HD // wide)
+    def _(t):
+        first = pl.multiple_of(t * wide, wide)
+        q_ref[:, pl.ds(first, wide)] = project(first)
+
+    keeps = []
+    for s in range(n_seq):
+        for c in copies[s]:
+            c.wait()
+        keep = pltpu.make_async_copy(kv_bufs[s], kv_ref.at[:, s], kv_here.at[n_seq + s])
+        keep.start()
+        keeps.append(keep)
+        for b in range(2 * cp):
+            at = table[s, b]
+            to = pl.ds(b * BLK, BLK)
+            source = pl.ds((at % 2) * BLK, BLK)
+            k_s[to, :] = kv_bufs[s][at // 2, 0, source, :]
+            v_s[to, :] = kv_bufs[s][at // 2, 1, source, :]
+        low_bias[...], high_bias[...] = query_bias(place[s], 2 * cp)
+
+        @pl.loop(0, KV // PACK)
+        def _(g, s=s):
+            head = pl.ds(pl.multiple_of(g * PACK * HD, PACK * HD), PACK * HD)
+            group = PACK * GROUP * HD
+            heads = pl.ds(pl.multiple_of(g * group, group), group)
+            at = pl.ds(s * rows, rows)
+            o_ref[at, heads] = attend_group(
+                q_ref[at, heads], k_s[:, head], v_s[:, head], low_bias[...], high_bias[...]
+            )
+
+    for c in keeps + [keep_w]:
+        c.wait()
+    office.end(kinds, ins, outs)
+
+
+def front(collective_id, table, place, x, shard, *jobs):
+    sizes = tuple(lax.axis_size(a) for a in DENSE)
+    hi, ep, cp = sizes
+    n_seq = table.shape[0]
+    kinds, arrays, shapes = courier_jobs(sizes, jobs)
+    rows, wide = 2 * BLK, KV * HD
+    whole = (hi * ep * cp,) + shard.shape
+    hbm = pl.BlockSpec(memory_space=pl.ANY)
+    vmem = pl.BlockSpec(memory_space=pltpu.VMEM)
+    smem = pl.BlockSpec(memory_space=pltpu.SMEM)
+    keys = cp * rows
+    row_shape = jax.ShapeDtypeStruct(x.shape, BF16)
+    return pl.pallas_call(
+        functools.partial(front_kernel, sizes, kinds),
+        in_specs=[smem, smem, vmem, hbm] + [hbm] * len(jobs),
+        out_specs=[vmem] * 3 + [hbm] * 2 + [hbm] * len(jobs),
+        out_shape=[row_shape] * 3
+        + [
+            jax.ShapeDtypeStruct((cp, n_seq, 2, rows, wide), BF16),
+            jax.ShapeDtypeStruct(whole, BF16),
+        ]
+        + shapes,
+        scratch_shapes=[
+            pltpu.VMEM(whole, BF16),
+            pltpu.VMEM((n_seq, 2, rows, wide), BF16),
+            pltpu.VMEM((keys, wide), BF16),
+            pltpu.VMEM((keys, wide), BF16),
+            pltpu.VMEM((BLK, keys // 2), F32),
+            pltpu.VMEM((BLK, keys // 2), F32),
+        ]
+        + post_scratch(jobs_messages(kinds + ["gather"], *sizes), len(jobs) + 1)
+        + [
+            pltpu.SemaphoreType.DMA((n_seq * (cp - 1),)),
+            pltpu.SemaphoreType.DMA((n_seq * (cp - 1),)),
+            pltpu.SemaphoreType.DMA((2 * n_seq + 1,)),
+        ]
+        + [pltpu.VMEM((cp, 2, rows, wide), BF16)] * n_seq,
+        compiler_params=pltpu.CompilerParams(
+            collective_id=collective_id, has_side_effects=True, vmem_limit_bytes=58 * 2**20
+        ),
+        cost_estimate=ATTENTION_COST,
+    )(table, place, x, shard, *arrays)
 
 
 def dense_sum_kernel(sizes, kinds, n_parts, *refs):
@@ -604,10 +753,6 @@
     )(*(p.reshape(-1, rows, p.shape[1]) for p in parts), *arrays)
 
 
-def quad(x):
-    return lax.all_to_all(x, "ep", split_axis=0, concat_axis=0, tiled=True)
-
-
 def swap(x):
     hi = lax.axis_size("hi")
     xs = x if isinstance(x, list) else [x] * (hi - 1)
@@ -616,40 +761,239 @@
     ]
 
 
-def before(k):
-    hi = lax.axis_size("hi")
-    return lax.rem(lax.axis_index("hi") - k + hi, hi)
-
-
 def after(k):
     return lax.rem(lax.axis_index("hi") + k, lax.axis_size("hi"))
 
 
-def place_pieces(mine, pieces):
-    rows = mine.shape[0]
-    full = jnp.zeros((rows * lax.axis_size("hi"), mine.shape[1]), mine.dtype)
-    full = lax.dynamic_update_slice(full, mine, (before(0) * rows, 0))
-    for first, arrays in pieces:
-        for k, part in enumerate(arrays, 1):
-            full = lax.dynamic_update_slice(full, part, (before(k) * rows + first, 0))
-    return full
-
-
-def half_products(left, right):
-    width = left.shape[1] // lax.axis_size("hi")
+def half_rows(x):
+    rows = x.shape[0] // lax.axis_size("hi")
     parts = [
-        dot(lax.dynamic_slice_in_dim(left, after(k) * width, width, axis=1), right, 0, 0)
+        lax.dynamic_slice_in_dim(x, after(k) * rows, rows, axis=0)
         for k in range(lax.axis_size("hi"))
     ]
-    return parts[0], [p.astype(BF16) for p in parts[1:]]
-
-
-def small_sum(x):
-    n = lax.axis_size("hi") * lax.axis_size("ep") * lax.axis_size("cp")
-    rows, k = x.shape[0] // n, x.shape[1]
-    flat = x.reshape(n, 1, rows * k)
-    got = lax.all_to_all(flat, DENSE, split_axis=0, concat_axis=0, tiled=True)
-    return jnp.sum(got, axis=(0, 1)).reshape(rows, k)
+    return parts[0], parts[1:]
+
+
+def expert_kernel(
+    sizes,
+    group,
+    x_hbm,
+    dy_hbm,
+    gate_hbm,
+    up_hbm,
+    down_hbm,
+    scale_ref,
+    back_ref,
+    inner_ref,
+    e_ref,
+    gate_out,
+    up_out,
+    down_out,
+    x_s,
+    dy_s,
+    gate_w,
+    up_w,
+    down_w,
+    hidden_s,
+    dg_s,
+    du_s,
+    back_s,
+    inner_s,
+    e_s,
+    load_sem,
+    weight_sem,
+    send,
+    recv,
+    out_sem,
+):
+    _, ep, cp = sizes
+    n, cap, width = x_hbm.shape
+    depth = hidden_s.shape[1]
+    me = lax.axis_index("cp") * ep + lax.axis_index("ep")
+
+    def source(k):
+        return lax.rem(me + 1 + k, n)
+
+    def device(at):
+        return {"cp": at // ep, "ep": lax.rem(at, ep)}
+
+    barrier = pltpu.get_barrier_semaphore()
+    for k in range(n - 1):
+        pl.semaphore_signal(
+            barrier, inc=1, device_id=device(source(k)), device_id_type=pl.DeviceIdType.MESH
+        )
+    weights = [
+        pltpu.make_async_copy(src, dst, weight_sem.at[i])
+        for i, (src, dst) in enumerate(
+            ((gate_hbm, gate_w), (up_hbm, up_w), (down_hbm, down_w))
+        )
+    ]
+    loads = []
+    for c in weights[:2]:
+        c.start()
+    for k in range(n):
+        pair = [
+            pltpu.make_async_copy(src.at[source(k)], dst.at[k], load_sem.at[2 * k + i])
+            for i, (src, dst) in enumerate(((x_hbm, x_s), (dy_hbm, dy_s)))
+        ]
+        for c in pair:
+            c.start()
+        loads.append(pair)
+    weights[2].start()
+    for pair in loads:
+        for c in pair:
+            c.wait()
+    for c in weights:
+        c.wait()
+    pl.semaphore_wait(barrier, n - 1)
+
+    def away(k, src, dst, lane):
+        return pltpu.make_async_remote_copy(
+            src_ref=src.at[k],
+            dst_ref=dst.at[me],
+            send_sem=send.at[2 * k + lane],
+            recv_sem=recv.at[2 * k + lane],
+            device_id=device(source(k)),
+            device_id_type=pl.DeviceIdType.MESH,
+        )
+
+    def here(src, dst, lane):
+        return pltpu.make_async_copy(src.at[n - 1], dst.at[me], out_sem.at[lane])
+
+    def keep_e(k):
+        return pltpu.make_async_copy(e_s.at[k], e_ref.at[source(k)], out_sem.at[2 + k])
+
+    tile = group * cap
+    chunk = min(512, depth)
+
+    @pl.loop(0, n // group)
+    def _(t):
+        first = pl.multiple_of(t * tile, tile)
+        at = pl.ds(first, tile)
+        k0 = t * group
+        x = x_s[pl.ds(k0, group)].reshape(tile, width)
+        dy = dy_s[pl.ds(k0, group)].reshape(tile, width)
+        inner = jnp.zeros((tile, 1), F32)
+        for f in range(0, depth, chunk):
+            cols = slice(f, f + chunk)
+            gate_pre = dot(x, gate_w[:, cols])
+            up_pre = dot(x, up_w[:, cols])
+            sigmoid_gate = jax.nn.sigmoid(gate_pre)
+            swish = gate_pre * sigmoid_gate
+            hidden = (swish * up_pre).astype(BF16)
+            hidden_s[at, cols] = hidden
+            hidden_grad = dot(dy, down_w[cols, :], 1, 1)
+            inner = inner + jnp.sum(hidden_grad * hidden.astype(F32), axis=1, keepdims=True)
+            slope = sigmoid_gate * (1.0 + gate_pre * (1.0 - sigmoid_gate))
+            dg_s[at, cols] = (hidden_grad * up_pre * slope).astype(BF16)
+            du_s[at, cols] = (hidden_grad * swish).astype(BF16)
+        high = inner.astype(BF16)
+        rest = inner - high.astype(F32)
+        middle = rest.astype(BF16)
+        low = (rest - middle.astype(F32)).astype(BF16)
+        lane = lax.broadcasted_iota(jnp.int32, (tile, 128), 1)
+        spread = jnp.where(
+            lane == 0,
+            high.astype(F32),
+            jnp.where(lane == 1, middle.astype(F32), jnp.where(lane == 2, low.astype(F32), 0.0)),
+        )
+        inner_s[pl.ds(k0, group)] = spread.astype(BF16).reshape(group, cap, 128)
+        for d in range(0, width, 512):
+            cols = slice(d, d + 512)
+            back = dot(dg_s[at, :], gate_w[cols, :], 1, 1) + dot(du_s[at, :], up_w[cols, :], 1, 1)
+            back_s[pl.ds(k0, group), :, cols] = back.astype(BF16).reshape(group, cap, 512)
+        for i in range(group):
+            k = k0 + i
+
+            @pl.when(k < n - 1)
+            def _():
+                away(k, back_s, back_ref, 0).start()
+                away(k, inner_s, inner_ref, 1).start()
+
+        for d in range(0, width, 512):
+            cols = slice(d, d + 512)
+            e = dot(hidden_s[at, :], down_w[:, cols])
+            e_s[pl.ds(k0, group), :, cols] = e.astype(BF16).reshape(group, cap, 512)
+        for i in range(group):
+            keep_e(k0 + i).start()
+
+    here(back_s, back_ref, 0).start()
+    here(inner_s, inner_ref, 1).start()
+    for k in range(n):
+        gate = scale_ref[source(k)]
+        x_s[k] = (x_s[k].astype(F32) * gate).astype(BF16)
+        dy_s[k] = (dy_s[k].astype(F32) * gate).astype(BF16)
+
+    @pl.loop(0, width // 256)
+    def _(d):
+        cols = pl.ds(pl.multiple_of(d * 256, 256), 256)
+        x = x_s[:, :, cols].reshape(n * cap, 256)
+        gate_out[cols, :] = dot(x, dg_s[...], 0, 0).astype(BF16)
+        up_out[cols, :] = dot(x, du_s[...], 0, 0).astype(BF16)
+
+    @pl.loop(0, depth // 256)
+    def _(f):
+        cols = pl.ds(pl.multiple_of(f * 256, 256), 256)
+        down_out[cols, :] = dot(
+            hidden_s[:, cols], dy_s[...].reshape(n * cap, width), 0, 0
+        ).astype(BF16)
+
+    here(back_s, back_ref, 0).wait()
+    here(inner_s, inner_ref, 1).wait()
+    for k in range(n):
+        keep_e(k).wait()
+    for k in range(n - 1):
+        away(k, back_s, back_ref, 0).wait()
+        away(k, inner_s, inner_ref, 1).wait()
+
+
+def expert(collective_id, x, dy, gate, up, down, scale):
+    sizes = tuple(lax.axis_size(a) for a in DENSE)
+    n, cap, width = x.shape
+    depth = gate.shape[1]
+    hbm = pl.BlockSpec(memory_space=pl.ANY)
+    vmem = pl.BlockSpec(memory_space=pltpu.VMEM)
+    rows = pltpu.VMEM(x.shape, BF16)
+    tall = pltpu.VMEM((n * cap, depth), BF16)
+
+    def sems(count):
+        return pltpu.SemaphoreType.DMA((count,))
+
+    return pl.pallas_call(
+        functools.partial(expert_kernel, sizes, 4),
+        in_specs=[hbm] * 5 + [vmem],
+        out_specs=[hbm] * 3 + [vmem] * 3,
+        out_shape=[
+            jax.ShapeDtypeStruct(x.shape, BF16),
+            jax.ShapeDtypeStruct((n, cap, 128), BF16),
+            jax.ShapeDtypeStruct(x.shape, BF16),
+            jax.ShapeDtypeStruct(gate.shape, BF16),
+            jax.ShapeDtypeStruct(up.shape, BF16),
+            jax.ShapeDtypeStruct(down.shape, BF16),
+        ],
+        scratch_shapes=[
+            rows,
+            rows,
+            pltpu.VMEM(gate.shape, BF16),
+            pltpu.VMEM(up.shape, BF16),
+            pltpu.VMEM(down.shape, BF16),
+            tall,
+            tall,
+            tall,
+            rows,
+            pltpu.VMEM((n, cap, 128), BF16),
+            rows,
+            sems(2 * n),
+            sems(3),
+            sems(2 * n),
+            sems(2 * n),
+            sems(2 + n),
+        ],
+        compiler_params=pltpu.CompilerParams(
+            collective_id=collective_id, has_side_effects=True, vmem_limit_bytes=62 * 2**20
+        ),
+        cost_estimate=ATTENTION_COST,
+    )(x, dy, gate, up, down, scale)
 
 
 def rms_backward(rows, scale, gain, grad_norm):
@@ -697,11 +1041,6 @@
     )
     second = with_extra(out_weight, router_weight, second_gain)
     second = lax.all_gather(second, DENSE, axis=0, tiled=True)
-    first, gate_matrix, down = courier(
-        0, ("gather", first), ("expert", gate_weight), ("quad", down_weight)
-    )
-    first = first.reshape(width, -1)
-    down = down.reshape(-1, width)
     n_first = n_q + 2 * n_kv
 
     chosen = routes.reshape(tokens, 2)
@@ -728,49 +1067,60 @@
         x = lax.all_to_all(x, ("cp", "ep"), split_axis=0, concat_axis=0, tiled=True)
         return x.reshape(n_slots)
 
-    grad_rows = dot(place_rows, cotangent.reshape(tokens, width)).astype(BF16)
-    qkv_matrix = first[:, :n_first]
-    gain_one = first[:, n_first].astype(F32)
     out_matrix = second[:, :width]
     router_matrix = second[:, width : width + EXPERTS]
     gain_two = second[:, width + EXPERTS].astype(F32)
 
+    grad_rows = dot(place_rows, cotangent.reshape(tokens, width)).astype(BF16)
     resid = layer_input.reshape(tokens, width).astype(F32)
     scale_one = lax.rsqrt(jnp.mean(resid * resid, axis=-1, keepdims=True) + EPS)
-    attn_in = (resid * scale_one * gain_one).astype(BF16)
-    qkv = dot(attn_in, qkv_matrix).astype(BF16)
-    queries = qkv[:, :n_q]
-    kv = qkv[:, n_q:].reshape(n_seq, rows, 2, n_kv).transpose(0, 2, 1, 3)
-    kv_all, up_matrix = courier(1, ("peers", kv), ("expert", up_weight))
     ids = jnp.stack([pairing, blocks - 1 - pairing], axis=2).reshape(n_seq, blocks)
     order = jnp.arange(blocks, dtype=jnp.int32)
     table = jnp.sum(jnp.where(ids[:, :, None] == order, order[None, :, None], 0), axis=1)
     place = lax.dynamic_index_in_dim(pairing, here, axis=1, keepdims=False)
-    grad_rows = exchange(tie(grad_rows, kv_all))
-    attn_out = attend(table, place, queries, kv_all)
-    attn_out = tie(attn_out, grad_rows)
+    weights = [("expert", w) for w in (gate_weight, up_weight, down_weight)]
+    if first.shape[0] % 16 == 0:
+        (
+            attn_in,
+            queries,
+            attn_out,
+            kv_all,
+            first,
+            gate_matrix,
+            up_matrix,
+            down_matrix,
+            grad_rows,
+        ) = front(
+            0,
+            table,
+            place,
+            layer_input.reshape(tokens, width),
+            first,
+            *weights,
+            ("tokens", grad_rows.reshape(EXPERTS, n_seq * CAP, width)),
+        )
+        grad_rows = grad_rows.reshape(n_slots, width)
+        first = first.reshape(width, -1)
+        qkv_matrix = first[:, :n_first]
+        gain_one = first[:, n_first].astype(F32)
+    else:
+        first, gate_matrix, down_matrix = courier(0, ("gather", first), weights[0], weights[2])
+        first = first.reshape(width, -1)
+        qkv_matrix = first[:, :n_first]
+        gain_one = first[:, n_first].astype(F32)
+        attn_in = (resid * scale_one * gain_one).astype(BF16)
+        qkv = dot(attn_in, qkv_matrix).astype(BF16)
+        queries = qkv[:, :n_q]
+        kv = qkv[:, n_q:].reshape(n_seq, rows, 2, n_kv).transpose(0, 2, 1, 3)
+        kv_all, up_matrix = courier(1, ("peers", kv), weights[1])
+        grad_rows = exchange(tie(grad_rows, kv_all))
+        attn_out = tie(attend(table, place, queries, kv_all), grad_rows)
     middle = resid + dot(attn_out, out_matrix)
     scale_two = lax.rsqrt(jnp.mean(middle * middle, axis=-1, keepdims=True) + EPS)
     moe_in = (middle * scale_two * gain_two).astype(BF16)
 
     rows_out = dot(place_rows, moe_in).astype(BF16)
-    down_piece = swap(down)
     arrived = exchange(rows_out)
-    down_matrix = place_pieces(down, [(0, down_piece)])
-    gate_pre = dot(arrived, gate_matrix)
-    up_pre = dot(arrived, up_matrix)
-    sigmoid_gate = jax.nn.sigmoid(gate_pre)
-    swish = gate_pre * sigmoid_gate
-    hidden = (swish * up_pre).astype(BF16)
-    produced = dot(hidden, down_matrix).astype(BF16)
-    hidden_grad = dot(grad_rows, down_matrix, 1, 1)
-    gate_inner = exchange_scalar(jnp.sum(hidden_grad * hidden.astype(F32), axis=1))
-    gate_pre_grad = hidden_grad * up_pre * sigmoid_gate * (1.0 + gate_pre * (1.0 - sigmoid_gate))
-    gate_pre_grad = gate_pre_grad.astype(BF16)
-    up_pre_grad = (hidden_grad * swish).astype(BF16)
-    grad_back = dot(gate_pre_grad, gate_matrix, 1, 1) + dot(up_pre_grad, up_matrix, 1, 1)
-    grad_back = grad_back.astype(BF16)
-
     logits = dot(moe_in, router_matrix)
     pick_f = picks.astype(F32)
     picked = jnp.sum(pick_f * logits[:, None, :], axis=-1)
@@ -779,18 +1129,21 @@
     gate_slot = jnp.sum(
         sum(jnp.where(at_slot[r], gates[:, r][None, :], 0.0) for r in range(2)), axis=1
     )
-    gate_slot = exchange_scalar(tie(gate_slot, arrived))[:, None]
-
-    arrived_gated = (arrived.astype(F32) * gate_slot).astype(BF16)
-    gate_part = dot(arrived_gated, gate_pre_grad, 0, 0).astype(BF16)
-    up_part = dot(arrived_gated, up_pre_grad, 0, 0).astype(BF16)
-    down_own, down_sent = half_products(
-        hidden, (grad_rows.astype(F32) * gate_slot).astype(BF16)
+    gate_slot = exchange_scalar(tie(gate_slot, arrived))
+    shape = (EXPERTS, n_seq * CAP, width)
+    grad_returned, inner, produced, gate_part, up_part, down_part = expert(
+        4,
+        arrived.reshape(shape),
+        grad_rows.reshape(shape),
+        gate_matrix,
+        up_matrix,
+        down_matrix,
+        gate_slot.reshape(EXPERTS, -1, 1),
     )
+    grad_returned = grad_returned.reshape(n_slots, width)
+    gate_inner = jnp.sum(inner[:, :, :3].astype(F32), axis=2).reshape(n_slots)
+    down_own, down_sent = half_rows(down_part)
     down_sent = swap(down_sent)
-    grad_returned, gate_part, up_part, down_own = lax.optimization_barrier(
-        (exchange(grad_back), gate_part, up_part, down_own)
-    )
 
     returned = exchange(tie(produced, grad_returned))
     back = [dot(take_rows[r], returned) for r in range(2)]
@@ -810,7 +1163,6 @@
     middle_grad = grad_final + middle_norm_grad
     branch_grad = middle_grad.astype(BF16)
     out_part = dot(attn_out, branch_grad, 0, 0).astype(BF16)
-    router_sum = small_sum(tie(router_part, returned))
     attn_out_grad = dot(branch_grad, out_matrix, 1, 1).astype(BF16)
     attn_out_grad = tie(attn_out_grad, out_part)
     query_grad, kv_grad, gate_parts = attend_back(
@@ -821,33 +1173,37 @@
     kv_grad = kv_grad.transpose(0, 2, 1, 3).reshape(tokens, 2 * n_kv)
     qkv_grad = jnp.concatenate([query_grad, kv_grad], axis=1)
     first_part = dot(attn_in, qkv_grad, 0, 0).astype(BF16)
-    first_sum, up_parts = dense_sum(
-        3, [first_part, out_part], ("owners", up_part)
-    )
     attn_in_grad = dot(qkv_grad, qkv_matrix, 1, 1)
     resid_norm_grad, gain_one_grad = rms_backward(resid, scale_one, gain_one, attn_in_grad)
     input_grad = middle_grad + resid_norm_grad
-    down_sum = tie(down_own, query_grad, returned) + sum(d.astype(F32) for d in down_sent)
-    down_sum = quad(down_sum.astype(BF16).reshape(down_weight.shape)).astype(F32)
+    down_sum = tie(down_own, query_grad, returned).astype(F32) + sum(d.astype(F32) for d in down_sent)
+    down_sum = down_sum.astype(BF16).reshape(down_weight.shape)
 
     def own_sum(parts):
         halves = parts.reshape((-1,) + gate_weight.shape)
         return jnp.sum(halves.astype(F32), axis=0)
 
-    gain_sum = small_sum(jnp.stack([gain_one_grad, gain_two_grad], axis=1))
+    small_part = jnp.concatenate(
+        [router_part, gain_one_grad[:, None], gain_two_grad[:, None]], axis=1
+    ).astype(BF16)
+    small_part = jnp.pad(small_part, ((0, 0), (0, -small_part.shape[1] % 128)))
+    dense, up_parts, down_sum = dense_sum(
+        3, [first_part, out_part, small_part], ("owners", up_part), ("quad", down_sum)
+    )
+    at_small = n_first + width
     return (
         layer_output.reshape(layer_input.shape),
         input_grad.reshape(layer_input.shape),
-        gain_sum[:, 0],
-        gain_sum[:, 1],
-        first_sum[:, :n_q],
-        first_sum[:, n_q : n_q + n_kv],
-        first_sum[:, n_q + n_kv : n_first],
-        first_sum[:, n_first:],
-        router_sum,
+        dense[:, at_small + EXPERTS],
+        dense[:, at_small + EXPERTS + 1],
+        dense[:, :n_q],
+        dense[:, n_q : n_q + n_kv],
+        dense[:, n_q + n_kv : n_first],
+        dense[:, n_first:at_small],
+        dense[:, at_small : at_small + EXPERTS],
         own_sum(gate_parts),
         own_sum(up_parts),
-        down_sum,
+        down_sum.astype(F32),
     )
 
 

time: 914 us -> 837 us (0.916)
  Pallas kernels: 436 us -> 591 us
  waiting for transfers between devices: 153 us -> 58.4 us
  matrix products: 168 us -> 73.5 us
  starting transfers between devices: 69.3 us -> 35 us
    pallas_call x3 -> x2, Pallas kernels: 214 us -> 344 us  [the longest x1 261 us: front(): pl.pallas_call(functools.partial(front_kernel, sizes, kinds), in_specs=[s...]
    dot_general x24 -> x13, matrix products: 163 us -> 69 us  [dot(): lax.dot_general(a, b, (((ca,), (cb,)), ((), ())), preferred_element_type=...]
    ppermute x2 -> x1, waiting for transfers between devices: 88.3 us -> 0.01 us  [swap(): lax.ppermute(xs[k - 1], 'hi', [(i, (i + k) % hi) for i in range(hi)])]
    pallas_call x1, Pallas kernels: 109 us -> 133 us  [dense_sum(): pl.pallas_call(functools.partial(dense_sum_kernel, sizes, kinds, len(part...]
    all_to_all x4 -> x2, starting transfers between devices: 37.9 us -> 15.7 us  [exchange(): x = lax.all_to_all(x, ('cp', 'ep'), split_axis=0, concat_axis=0, tiled=True)]
    all_to_all x3 -> x0, starting transfers between devices: 16.8 us -> none  [the longest x2 12.5 us: small_sum(): got = lax.all_to_all(flat, DENSE, split_axis=0, concat_axis=0, tiled=True)]
    all_to_all x3 -> x0, waiting for transfers between devices: 10.4 us -> none  [the longest x2 6.32 us: small_sum(): got = lax.all_to_all(flat, DENSE, split_axis=0, concat_axis=0, tiled=True)]
    all_to_all x4 -> x2, waiting for transfers between devices: 54.3 us -> 57.1 us  [exchange(): x = lax.all_to_all(x, ('cp', 'ep'), split_axis=0, concat_axis=0, tiled=True)]
  transfers between devices with their start and end apart: 12 -> 5, of which waited for: 5 -> 2; matrix products, arithmetic and copies ran while one was open for 17% -> 6% of each run, Pallas kernels for 48% -> 45%
where the time goes in v2:
time: 837 us; the launch traced here: 828 us
  Pallas kernels  591 us (71%)
  matrix products  73.5 us (9%)
  waiting for transfers between devices  58.4 us (7%)
  starting transfers between devices  35 us (4%)
  other arithmetic  29.2 us (3%)
  local copies, waits for them, and re-layouts  26.1 us (3%)
  between operations  14.7 us (2%)
    pallas_call x1, Pallas kernels, front(): pl.pallas_call(functools.partial(front_kernel, sizes, kinds), in_specs=[s...  261 us
    pallas_call x1, Pallas kernels, dense_sum(): pl.pallas_call(functools.partial(dense_sum_kernel, sizes, kinds, len(part...  133 us
    pallas_call x1, Pallas kernels, attend_back(): pl.pallas_call(functools.partial(attend_back_kernel, sizes, kinds), grid=...  113 us
    pallas_call x1, Pallas kernels, expert(): pl.pallas_call(functools.partial(expert_kernel, sizes, 4), in_specs=[hbm]...  82.8 us
    dot_general x13, matrix products, dot(): lax.dot_general(a, b, (((ca,), (cb,)), ((), ())), preferred_element_type=...  69 us
    all_to_all x2, waiting for transfers between devices, exchange(): x = lax.all_to_all(x, ('cp', 'ep'), split_axis=0, concat_axis=0, tiled=True)  57.1 us
  transfers between devices with their start and end apart: 5, of which 2 were waited for; matrix products, arithmetic and copies ran while one was open for 6% of the time, Pallas kernels for 45%

profile of v2, /device:TPU:0, one launch (start us, length us, event | category | flops | bytes accessed | tf_op | source)
XLA Modules:
  0.0 827.8 jit_solution(17769297492310403609)
XLA Ops:
  19.0 5.6 convolution_convert_fusion.3
  24.6 261.5 %shard_map.229 = (bf16[512,1536]{1,0:T(8,128)(2,1)}, bf16[512,1536]{1,0:T(8,128)(2,1)}, bf16[512,1536]{1,0:T(8,128)(2,1)}, bf16[4,2,2,256,512]{4,3,2,1,0:T(8,128...) custom-call(s32[2,8]{1,0:T(2,128)} %select_reduce_fusion.5.table, ...), custom_call_target="tpu_custom_call" | custom-call | flops 17179869184 | bytes 16777216 | tf_op jit(solution)/shard_map/pallas_call | solution.py:612
  286.1 5.6 multiply_reduce_fusion.3
  297.1 16.5 %all-to-all-start.1 = ((f32[16,1,96]{2,1,0:T(1,128)}), f32[16,1,96]{2,1,0:T(1,128)S(1)}, u32[]{:S(2)}, u32[]{:S(2)}) async-start(f32[16,1,96]{2,1,0:T(1,128)} %reshape.294), calls=%async_computation.1 | async-start | bytes 16384 | tf_op jit(solution)/shard_map/all_to_all | solution.py:1067
  313.6 4.2 convolution_convert_fusion.2
  319.0 4.6 all-to-all-start
  324.8 57.1 %all-to-all-done.x_hbm = bf16[16,96,1536]{2,1,0:T(8,128)(2,1)} async-done(((bf16[16,96,1536]{2,1,0:T(8,128)(2,1)}), bf16[16,96,1536]{2,1,0:T(8,128)(2,1)}, u32[]{:S(2)}, u32[]{:S(2)}) %all-to-all-start) | async-done | bytes 4718624 | tf_op jit(solution)/shard_map/all_to_all | solution.py:1062
  381.9 82.8 %shard_map.230 = (bf16[16,96,1536]{2,1,0:T(8,128)(2,1)}, bf16[16,96,128]{2,1,0:T(8,128)(2,1)}, bf16[16,96,1536]{2,1,0:T(8,128)(2,1)}, bf16[1536,1024]{1,0:T(8,12...) custom-call(bf16[16,96,1536]{2,1,0:T(8,128)(2,1)} %all-to-all-done.x_hbm, ...), custom_call_target="tpu_custom_call" | custom-call | flops 17179869184 | bytes 16777216 | tf_op jit(solution)/shard_map/pallas_call | solution.py:962
  464.7 11.2 %all-to-all-start.2 = ((bf16[16,96,1536]{2,1,0:T(8,128)(2,1)}), bf16[16,96,1536]{2,1,0:T(8,128)(2,1)}, u32[]{:S(2)}, u32[]{:S(2)}) async-start(bf16[16,96,1536]{2,1,0:T(8,128)(2,1)} %get-tuple-element.44), calls=%async_computation.2 | async-start | bytes 9437184 | tf_op jit(solution)/shard_map/all_to_all | solution.py:1062
  478.7 4.7 convolution_multiply_fusion.1
  483.5 4.9 convolution_multiply_fusion
  488.4 3.8 multiply_reduce_fusion
  493.6 4.4 convolution_convert_fusion.1
  498.0 3.8 fusion.21.g_ref
  507.1 113.3 %shard_map.231 = (bf16[512,1536]{1,0:T(8,128)(2,1)}, bf16[4,2,2,256,512]{4,3,2,1,0:T(8,128)(2,1)}, bf16[8,192,1024]{2,1,0:T(8,128)(2,1)}) custom-call(s32[2,8]{1,0:T(2,128)} %select_reduce_fusion.5.table, s32[2,8]{1,0:T(2,128)} %copy-done.20, s32[2]{0:T(128)} %dynamic-slice_reduce_fusion.place, bf16[512,1536]{1,0:T(8,128)(2,1)} %get-tuple-element.46.q_ref, ...), custom_call_target="tpu_custom_call" | custom-call | flops 17179869184 | bytes 16777216 | tf_op jit(solution)/shard_map/pallas_call | solution.py:266
  620.5 4.7 convert_reduce_fusion.1
  626.5 4.1 reduce_sum.187
  633.4 10.3 %fusion.16 = (bf16[1536]{0:T(1024)(128)(2,1)S(1)}, f32[512]{0:T(512)S(1)}, f32[512,1536]{1,0:T(8,128)}) fusion(f32[512]{0:T(512)S(1)} %bitcast.84, bf16[2,1,2,128,1536]{4,3,2,1,0:T(8,128)(2,1)S(1)} %copy-done.7, f32[1536]{0:T(1024)S(1)} %convert_reduce_fusion.4, bf16[512,2560]{1,0:T(8,128)(2,1)S(1)} %constant_dynamic-update-slice_fusion, ...), kind=kOutput, calls=%fused_computation.31 | convolution fusion | flops 4032034816 | bytes 15217664 | tf_op jit(solution)/shard_map/dot_general | solution.py:28
  646.3 9.7 %convolution_convert_fusion = bf16[1536,2560]{1,0:T(8,128)(2,1)} fusion(bf16[512,1536]{1,0:T(8,128)(2,1)} %get-tuple-element.55, bf16[512,2560]{1,0:T(8,128)(2,1)} %copy-done.17), kind=kOutput, calls=%fused_computation | convolution fusion | flops 4030464000 | bytes 12058624 | tf_op jit(solution)/shard_map/dot_general | solution.py:28
  656.0 2.9 add_convert_fusion
  659.0 133.4 %shard_map.232 = (f32[48,4224]{1,0:T(8,128)}, bf16[8,192,1024]{2,1,0:T(8,128)(2,1)}, bf16[4,128,1536]{2,1,0:T(8,128)(2,1)}) custom-call(bf16[32,48,2560]{2,1,0:T(8,128)(2,1)} %bitcast.59, bf16[32,48,1536]{2,1,0:T(8,128)(2,1)} %bitcast.64, bf16[32,48,128]{2,1,0:T(8,128)(2,1)} %bitcast.72, bf16[1536,1024]{1,0:T(8,128)(2,1)} %get-tuple-element.56.refs_3_, ...), custom_call_target="tpu_custom_call" | custom-call | tf_op jit(solution)/shard_map/pallas_call | solution.py:732
  798.2 6.8 convolution_multiply_fusion.2
  811.1 6.9 fusion.20
  818.0 2.8 fusion.13
  (135 shorter events, 47.6 us)
Async XLA Ops:
  7.2 278.9 %all-gather.2.cloned.1.call-start = ((), (), s32[]{:S(2)}) async-start(), calls=%async_computation.3 | async-start | bytes 5271552 | tf_op jit(solution)/shard_map/all_gather | solution.py:1043
  13.4 11.3 %copy-start.20 = (s32[2,8]{1,0:T(2,128)}, s32[2,8]{1,0:T(2,128)S(1)}, u32[]{:S(2)}) copy-start(s32[2,8]{1,0:T(2,128)S(1)} %eq.48.inverse) | copy-start | bytes 196
  19.0 459.7 %copy-start.21 = (s32[512,1]{0,1:T(1,128)}, s32[512,1]{0,1:T(1,128)S(1)}, u32[]{:S(2)}) copy-start(s32[512,1]{0,1:T(1,128)S(1)} %get-tuple-element.126) | copy-start | bytes 6148
  19.0 464.4 %copy-start.23 = (s32[512,1]{0,1:T(1,128)}, s32[512,1]{0,1:T(1,128)S(1)}, u32[]{:S(2)}) copy-start(s32[512,1]{0,1:T(1,128)S(1)} %get-tuple-element.127) | copy-start | bytes 6148
  24.6 261.5 %copy-start.6 = (bf16[2,1,2,128,1536]{4,3,2,1,0:T(8,128)(2,1)S(1)}, bf16[2,1,2,128,1536]{4,3,2,1,0:T(8,128)(2,1)}, u32[]{:S(2)}) copy-start(bf16[2,1,2,128,1536]{4,3,2,1,0:T(8,128)(2,1)} %param.14) | copy-start | bytes 4718596
  293.7 24.1 %copy-start.2 = (bf16[512,1536]{1,0:T(8,128)(2,1)}, bf16[512,1536]{1,0:T(8,128)(2,1)S(1)}, u32[]{:S(2)}) copy-start(bf16[512,1536]{1,0:T(8,128)(2,1)S(1)} %multiply_convert_fusion) | copy-start | bytes 4718596
  295.7 183.0 %copy-start.25 = (f32[512,1]{0,1:T(1,128)}, f32[512,1]{0,1:T(1,128)S(1)}, u32[]{:S(2)}) copy-start(f32[512,1]{0,1:T(1,128)S(1)} %get-tuple-element.124) | copy-start | bytes 6148
  295.7 187.7 %copy-start.27 = (f32[512,1]{0,1:T(1,128)}, f32[512,1]{0,1:T(1,128)S(1)}, u32[]{:S(2)}) copy-start(f32[512,1]{0,1:T(1,128)S(1)} %get-tuple-element.125) | copy-start | bytes 6148
  297.1 21.9 %all-to-all-start.1 = ((f32[16,1,96]{2,1,0:T(1,128)}), f32[16,1,96]{2,1,0:T(1,128)S(1)}, u32[]{:S(2)}, u32[]{:S(2)}) async-start(f32[16,1,96]{2,1,0:T(1,128)} %reshape.294), calls=%async_computation.1 | async-start | bytes 16384 | tf_op jit(solution)/shard_map/all_to_all | solution.py:1067
  319.0 62.9 %all-to-all-start = ((bf16[16,96,1536]{2,1,0:T(8,128)(2,1)}), bf16[16,96,1536]{2,1,0:T(8,128)(2,1)}, u32[]{:S(2)}, u32[]{:S(2)}) async-start(bf16[16,96,1536]{2,1,0:T(8,128)(2,1)} %bitcast.63), calls=%async_computation | async-start | bytes 9437184 | tf_op jit(solution)/shard_map/all_to_all | solution.py:1062
  464.7 12.8 %copy-start.18 = (bf16[16,96,128]{2,1,0:T(8,128)(2,1)S(1)}, bf16[16,96,128]{2,1,0:T(8,128)(2,1)}, u32[]{:S(2)}) copy-start(bf16[16,96,128]{2,1,0:T(8,128)(2,1)} %get-tuple-element.45) | copy-start | bytes 1179652
  464.7 161.7 %all-to-all-start.2 = ((bf16[16,96,1536]{2,1,0:T(8,128)(2,1)}), bf16[16,96,1536]{2,1,0:T(8,128)(2,1)}, u32[]{:S(2)}, u32[]{:S(2)}) async-start(bf16[16,96,1536]{2,1,0:T(8,128)(2,1)} %get-tuple-element.44), calls=%async_computation.2 | async-start | bytes 9437184 | tf_op jit(solution)/shard_map/all_to_all | solution.py:1062
  483.4 4.9 copy-start.1
  492.2 5.8 slice-start
  503.7 122.8 %collective-permute-start = (bf16[512,1536]{1,0:T(8,128)(2,1)}, bf16[512,1536]{1,0:T(8,128)(2,1)}, u32[]{:S(2)}, u32[]{:S(2)}) collective-permute-start(bf16[512,1536]{1,0:T(8,128)(2,1)} %get-tuple-element.119), channel_id=1, source_target_pairs={{0,16},{16,0},{1,17},{17,1},{2,18},{18,2},{3,19},{19,3},{4,20},{20... | collective-permute-start | bytes 4718600 | tf_op jit(solution)/shard_map/ppermute | solution.py:760
  620.5 4.7 copy-start.13
  633.4 10.3 %copy-start.17 = (bf16[512,2560]{1,0:T(8,128)(2,1)}, bf16[512,2560]{1,0:T(8,128)(2,1)S(1)}, u32[]{:S(2)}) copy-start(bf16[512,2560]{1,0:T(8,128)(2,1)S(1)} %constant_dynamic-update-slice_fusion) | copy-start | bytes 7864324
  646.3 9.7 %copy-start.9 = (bf16[512,1536]{1,0:T(8,128)(2,1)S(1)}, bf16[512,1536]{1,0:T(8,128)(2,1)}, u32[]{:S(2)}) copy-start(bf16[512,1536]{1,0:T(8,128)(2,1)} %get-tuple-element.57) | copy-start | bytes 4718596
  659.0 139.2 %copy-start.24 = (s32[512,1]{0,1:T(1,128)S(1)}, s32[512,1]{0,1:T(1,128)}, u32[]{:S(2)}) copy-start(s32[512,1]{0,1:T(1,128)} %copy-done.23) | copy-start | bytes 6148
  659.0 139.2 %copy-start.28 = (f32[512,1]{0,1:T(1,128)S(1)}, f32[512,1]{0,1:T(1,128)}, u32[]{:S(2)}) copy-start(f32[512,1]{0,1:T(1,128)} %copy-done.27) | copy-start | bytes 6148
  798.2 6.8 copy-start.14
  811.1 6.9 copy-start.5
  811.1 6.9 copy-start.8
  811.1 6.9 copy-start.12
  (13 other events, 43.0 us)
Sparse Core Ops, SparseCore 0:
  11.5 113.4 all-gather.1

commit v3 on v2

--- a/solution.py
+++ b/solution.py
@@ -359,19 +359,23 @@
             pl.semaphore_signal(barrier, inc=1, device_id=p, device_id_type=pl.DeviceIdType.MESH)
         pl.semaphore_wait(barrier, len(partners))
 
-    def copies(self, kinds, ins, outs):
+    def copies(self, kinds, ins, outs, only=None):
         me, my_ep, my_cp, ep, cp, fsdp = (
             self.me, self.my_ep, self.my_cp, self.ep, self.cp, self.fsdp
         )
-        away, local = [], []
+        away, local, count = [], [], {"away": 0, "here": 0}
 
         def post(src, dst, device):
-            away.append(mesh_copy(src, dst, (self.send, self.recv), len(away), device))
+            if only is None or job in only:
+                away.append(mesh_copy(src, dst, (self.send, self.recv), count["away"], device))
+            count["away"] += 1
 
         def keep(src, dst):
-            local.append(pltpu.make_async_copy(src, dst, self.here.at[len(local)]))
-
-        for kind, x, out in zip(kinds, ins, outs):
+            if only is None or job in only:
+                local.append(pltpu.make_async_copy(src, dst, self.here.at[count["here"]]))
+            count["here"] += 1
+
+        for job, (kind, x, out) in enumerate(zip(kinds, ins, outs)):
             if kind == "expert":
                 rows = x.shape[1]
                 at = pl.ds(pl.multiple_of(me * rows, rows), rows)
@@ -420,7 +424,7 @@
 
     def gather(self, x, out, first, here):
         me, my_cp, cp, fsdp = self.me, self.my_cp, self.cp, self.fsdp
-        sent, across = [], []
+        sent, across, mirrored = [], [], []
 
         def post(src, dst, device):
             c = mesh_copy(src, dst, (self.send, self.recv), first + len(sent), device)
@@ -436,16 +440,15 @@
                 across.append((f, m, post(src, row(f, my_cp), {"cp": plus(my_cp, m, cp)})))
             mirrored.append(post(src, row(f, my_cp), self.at_fsdp(self.sibling)))
 
-        mirrored = []
         z = post(x, row(me, my_cp), self.at_fsdp(flip(me, 2)))
         own = pltpu.make_async_copy(x, row(me, my_cp), self.here.at[here])
         own.start()
         share(me, x)
-        column = [z]
         for k in range(1, fsdp // 2):
-            column[-1].wait_recv()
+            yield
+            z.wait_recv()
             if k + 1 < fsdp // 2:
-                column.append(post(x, row(me, my_cp), self.at_fsdp(flip(me, 2 * k + 2))))
+                z = post(x, row(me, my_cp), self.at_fsdp(flip(me, 2 * k + 2)))
             f = flip(me, 2 * k)
             share(f, row(f, my_cp))
         yield
@@ -458,7 +461,14 @@
         for c in sent:
             c.wait_send()
         own.wait()
-        yield
+
+    def column_steps(self):
+        return self.fsdp // 2
+
+
+def steps(generator, count):
+    for _ in range(count):
+        next(generator, None)
 
 
 def courier_jobs(sizes, jobs):
@@ -490,10 +500,10 @@
         if kind == "gather":
             gathers.append(office.gather(x, out, first, here))
             first, here = first + jobs_messages(["gather"], *sizes), here + 1
-            next(gathers[-1])
+            steps(gathers[-1], office.column_steps())
     office.begin(kinds, ins, outs)
     for g in gathers:
-        next(g)
+        steps(g, 1)
     office.end(kinds, ins, outs)
 
 
@@ -511,31 +521,56 @@
     )(*arrays)
 
 
-def front_kernel(sizes, kinds, table, place, x_ref, shard_ref, *refs):
+def three_parts(x):
+    high = x.astype(BF16).astype(F32)
+    middle = (x - high).astype(BF16).astype(F32)
+    low = x - high - middle
+    lane = lax.broadcasted_iota(jnp.int32, (x.shape[0], 128), 1)
+    out = jnp.where(lane == 0, high, jnp.where(lane == 1, middle, jnp.where(lane == 2, low, 0.0)))
+    return out.astype(BF16)
+
+
+STAGES = ((0, 3), (), (1, 2), ())
+
+
+def front_kernel(sizes, kinds, table, place, x_ref, routes_ref, slots_ref, shard_ref, shard2_ref, *refs):
     n = len(kinds)
-    ins = refs[:n]
-    a_ref, q_ref, o_ref, kv_ref, w_ref = refs[n : n + 5]
-    outs = refs[n + 5 : 2 * n + 5]
-    rest = refs[2 * n + 5 :]
-    w_all, kv_mine, k_s, v_s, low_bias, high_bias = rest[:6]
-    office = PostOffice(sizes, rest[6:9])
-    kv_send, kv_recv, kv_here = rest[9:12]
-    kv_bufs = rest[12:]
-    n_seq, cp, my_cp = len(kv_bufs), sizes[2], office.my_cp
+    ins, refs = refs[:n], refs[n:]
+    a_ref, q_ref, o_ref, middle_ref, b_ref, gates_ref = refs[:6]
+    kv_ref, w_ref, w2_ref, rows_ref, rows_gate_ref = refs[6:11]
+    outs, rest = refs[11 : n + 11], refs[n + 11 :]
+    w_all, w2_all, kv_mine, k_s, v_s, low_bias, high_bias, send_s, gate_s = rest[:9]
+    office = PostOffice(sizes, rest[9:12])
+    kv_send, kv_recv, kv_here, row_send, row_recv = rest[12:17]
+    kv_bufs = rest[17:]
+    _, ep, cp = sizes
+    n_seq, my_cp = len(kv_bufs), office.my_cp
     rows = 2 * BLK
     wide = KV * HD
     office.greet(kinds)
-    gather = office.gather(shard_ref, w_all, jobs_messages(kinds, *sizes), n)
-    next(gather)
-    office.begin(kinds, ins, outs)
+    base = jobs_messages(kinds, *sizes)
+
+    def begin(stage):
+        if STAGES[stage]:
+            office.begin(kinds, ins, outs, STAGES[stage])
+
+    gather = office.gather(shard_ref, w_all, base, n)
+    gather2 = office.gather(shard2_ref, w2_all, base + jobs_messages(["gather"], *sizes), n + 1)
+    steps(gather, office.column_steps())
+    begin(0)
     x = x_ref[...].astype(F32)
     x = x * lax.rsqrt(jnp.mean(x * x, axis=-1, keepdims=True) + EPS)
-    next(gather)
+    steps(gather, 1)
+    begin(1)
+    steps(gather2, 1)
     depth = x.shape[1]
     keep_w = pltpu.make_async_copy(w_all, w_ref, kv_here.at[2 * n_seq])
     keep_w.start()
-    last = pl.ds(H * HD + 2 * wide, 128)
-    gain = w_all[:, :, last].astype(F32).reshape(depth, 128).T[:1]
+
+    def column(w, first):
+        return w[:, :, pl.ds(first, 128)].reshape(depth, 128)
+
+    gain = column(w_all, H * HD + 2 * wide).astype(F32).T[:1]
     a_ref[...] = (x * gain).astype(BF16)
 
     def project(first):
@@ -561,12 +596,14 @@
         for c in group:
             c.start()
         copies.append(group)
+    steps(gather2, 1)
 
     @pl.loop(0, H * HD // wide)
     def _(t):
         first = pl.multiple_of(t * wide, wide)
         q_ref[:, pl.ds(first, wide)] = project(first)
 
+    steps(gather2, 1)
     keeps = []
     for s in range(n_seq):
         for c in copies[s]:
@@ -580,6 +617,8 @@
             source = pl.ds((at % 2) * BLK, BLK)
             k_s[to, :] = kv_bufs[s][at // 2, 0, source, :]
             v_s[to, :] = kv_bufs[s][at // 2, 1, source, :]
+        if s == n_seq - 1:
+            begin(2)
         low_bias[...], high_bias[...] = query_bias(place[s], 2 * cp)
 
         @pl.loop(0, KV // PACK)
@@ -592,69 +631,157 @@
                 q_ref[at, heads], k_s[:, head], v_s[:, head], low_bias[...], high_bias[...]
             )
 
-    for c in keeps + [keep_w]:
+        steps(gather2, 1)
+
+    begin(3)
+    steps(gather2, office.column_steps())
+    keep_w2 = pltpu.make_async_copy(w2_all, w2_ref, kv_here.at[2 * n_seq + 1])
+    keep_w2.start()
+
+    @pl.loop(0, depth // wide)
+    def _(t):
+        cols = pl.ds(pl.multiple_of(t * wide, wide), wide)
+        out = dot(o_ref[...], w2_all[:, :, cols].reshape(H * HD, wide))
+        middle_ref[:, cols] = x_ref[:, cols].astype(F32) + out
+
+    middle = middle_ref[...]
+    last = column(w2_all, depth)
+    gain = last.astype(F32).T[EXPERTS : EXPERTS + 1]
+    b_ref[...] = (
+        middle * lax.rsqrt(jnp.mean(middle * middle, axis=-1, keepdims=True) + EPS) * gain
+    ).astype(BF16)
+    logits = dot(b_ref[...], last)
+    lane = lax.broadcasted_iota(jnp.int32, logits.shape, 1)
+    picked = [
+        jnp.sum(jnp.where(lane == routes_ref[:, r : r + 1], logits, 0.0), axis=1, keepdims=True)
+        for r in range(2)
+    ]
+    top = jnp.maximum(picked[0], picked[1])
+    powers = [jnp.exp(p - top) for p in picked]
+    gates = [p / (powers[0] + powers[1]) for p in powers]
+    both = jnp.where(lane == 0, gates[0], jnp.where(lane == 1, gates[1], 0.0))
+    gates_ref[...] = both
+    gate_rows = both.T[:2]
+    count = EXPERTS
+    cap = send_s.shape[1]
+    mine = my_cp * ep + office.my_ep
+
+    def away(k, lane):
+        to = lax.rem(mine + 1 + k, count)
+        src, dst = ((send_s, rows_ref), (gate_s, rows_gate_ref))[lane]
+        return mesh_copy(
+            src.at[k],
+            dst.at[mine],
+            (row_send, row_recv),
+            2 * k + lane,
+            {"cp": to // ep, "ep": lax.rem(to, ep)},
+        )
+
+    @pl.loop(0, count)
+    def _(k):
+        first = lax.rem(mine + 1 + k, count) * cap
+        ids = lax.broadcasted_iota(jnp.int32, (cap, slots_ref.shape[1]), 0) + first
+        at = [slots_ref[r : r + 1, :] == ids for r in range(2)]
+        chosen = jnp.where(at[0] | at[1], 1.0, 0.0).astype(BF16)
+        send_s[k] = dot(chosen, b_ref[...]).astype(BF16)
+        gate = sum(jnp.where(at[r], gate_rows[r : r + 1], 0.0) for r in range(2))
+        gate_s[k] = three_parts(jnp.sum(gate, axis=1, keepdims=True))
+
+        @pl.when(k < count - 1)
+        def _():
+            away(k, 0).start()
+            away(k, 1).start()
+
+    own = [
+        pltpu.make_async_copy(src.at[count - 1], dst.at[mine], kv_here.at[2 * n_seq + 2 + i])
+        for i, (src, dst) in enumerate(((send_s, rows_ref), (gate_s, rows_gate_ref)))
+    ]
+    for c in own:
+        c.start()
+    for c in own + keeps + [keep_w, keep_w2]:
         c.wait()
+    for k in range(count - 1):
+        away(k, 0).wait()
+        away(k, 1).wait()
     office.end(kinds, ins, outs)
 
 
-def front(collective_id, table, place, x, shard, *jobs):
+def front(collective_id, table, place, x, routes, slots, shard, shard2, *jobs):
     sizes = tuple(lax.axis_size(a) for a in DENSE)
     hi, ep, cp = sizes
     n_seq = table.shape[0]
     kinds, arrays, shapes = courier_jobs(sizes, jobs)
     rows, wide = 2 * BLK, KV * HD
-    whole = (hi * ep * cp,) + shard.shape
+    whole, whole2 = ((hi * ep * cp,) + s.shape for s in (shard, shard2))
     hbm = pl.BlockSpec(memory_space=pl.ANY)
     vmem = pl.BlockSpec(memory_space=pltpu.VMEM)
     smem = pl.BlockSpec(memory_space=pltpu.SMEM)
     keys = cp * rows
-    row_shape = jax.ShapeDtypeStruct(x.shape, BF16)
+    tokens, width = x.shape
+    sent = (EXPERTS, n_seq * CAP, width)
+    sent_gate = (EXPERTS, n_seq * CAP, 128)
+
+    def sems(count):
+        return pltpu.SemaphoreType.DMA((count,))
+
     return pl.pallas_call(
         functools.partial(front_kernel, sizes, kinds),
-        in_specs=[smem, smem, vmem, hbm] + [hbm] * len(jobs),
-        out_specs=[vmem] * 3 + [hbm] * 2 + [hbm] * len(jobs),
-        out_shape=[row_shape] * 3
+        in_specs=[smem, smem, vmem, vmem, vmem, hbm, hbm] + [hbm] * len(jobs),
+        out_specs=[vmem] * 6 + [hbm] * 5 + [hbm] * len(jobs),
+        out_shape=[jax.ShapeDtypeStruct(x.shape, BF16)] * 3
         + [
+            jax.ShapeDtypeStruct(x.shape, F32),
+            jax.ShapeDtypeStruct(x.shape, BF16),
+            jax.ShapeDtypeStruct((tokens, 128), F32),
             jax.ShapeDtypeStruct((cp, n_seq, 2, rows, wide), BF16),
             jax.ShapeDtypeStruct(whole, BF16),
+            jax.ShapeDtypeStruct(whole2, BF16),
+            jax.ShapeDtypeStruct(sent, BF16),
+            jax.ShapeDtypeStruct(sent_gate, BF16),
         ]
         + shapes,
         scratch_shapes=[
             pltpu.VMEM(whole, BF16),
+            pltpu.VMEM(whole2, BF16),
             pltpu.VMEM((n_seq, 2, rows, wide), BF16),
             pltpu.VMEM((keys, wide), BF16),
             pltpu.VMEM((keys, wide), BF16),
             pltpu.VMEM((BLK, keys // 2), F32),
             pltpu.VMEM((BLK, keys // 2), F32),
+            pltpu.VMEM(sent, BF16),
+            pltpu.VMEM(sent_gate, BF16),
         ]
-        + post_scratch(jobs_messages(kinds + ["gather"], *sizes), len(jobs) + 1)
+        + post_scratch(jobs_messages(kinds + ["gather"] * 2, *sizes), len(jobs) + 2)
         + [
-            pltpu.SemaphoreType.DMA((n_seq * (cp - 1),)),
-            pltpu.SemaphoreType.DMA((n_seq * (cp - 1),)),
-            pltpu.SemaphoreType.DMA((2 * n_seq + 1,)),
+            sems(n_seq * (cp - 1)),
+            sems(n_seq * (cp - 1)),
+            sems(2 * n_seq + 4),
+            sems(2 * EXPERTS),
+            sems(2 * EXPERTS),
         ]
         + [pltpu.VMEM((cp, 2, rows, wide), BF16)] * n_seq,
         compiler_params=pltpu.CompilerParams(
-            collective_id=collective_id, has_side_effects=True, vmem_limit_bytes=58 * 2**20
+            collective_id=collective_id, has_side_effects=True, vmem_limit_bytes=60 * 2**20
         ),
         cost_estimate=ATTENTION_COST,
-    )(table, place, x, shard, *arrays)
-
-
-def dense_sum_kernel(sizes, kinds, n_parts, *refs):
+    )(table, place, x, routes, slots, shard, shard2, *arrays)
+
+
+STAGE_SUM = 0
+
+
+def dense_sum_kernel(sizes, kinds, n_parts, slots_ref, gates_ref, returned_hbm, middle_hbm, *refs):
     n = len(kinds)
     parts, refs = refs[:n_parts], refs[n_parts:]
     widths = [p.shape[2] for p in parts]
     columns = [pl.ds(sum(widths[:j]), w) for j, w in enumerate(widths)]
-    ins, out, outs = refs[:n], refs[n], refs[n + 1 : 2 * n + 1]
-    mine, from_core, summed, from_peers, rows_out, from_column = refs[2 * n + 1 : 2 * n + 7]
-    office = PostOffice(sizes, refs[2 * n + 7 : 2 * n + 10])
-    load_sem, core_sems, peer_sems, column_sems = (
-        refs[2 * n + 10],
-        refs[2 * n + 11 : 2 * n + 13],
-        refs[2 * n + 13 : 2 * n + 15],
-        refs[2 * n + 15 : 2 * n + 17],
+    ins, out, final_ref, outs, rest = (
+        refs[:n], refs[n], refs[n + 1], refs[n + 2 : 2 * n + 2], refs[2 * n + 2 :]
     )
+    mine, from_core, summed, from_peers, rows_out, from_column, returned_s, middle_s = rest[:8]
+    office = PostOffice(sizes, rest[8:11])
+    load_sem, combine_sem = rest[11:13]
+    core_sems, peer_sems, column_sems = rest[13:15], rest[15:17], rest[17:19]
     cp, columns_n = sizes[2], office.fsdp // 2
     me, my_cp = office.me, office.my_cp
     office.greet(kinds)
@@ -678,7 +805,12 @@
             )
             c.start()
             loads.append(c)
-    office.begin(kinds, ins, outs)
+    fetch = [
+        pltpu.make_async_copy(src, dst, combine_sem.at[i])
+        for i, (src, dst) in enumerate(((returned_hbm, returned_s), (middle_hbm, middle_s)))
+    ]
+    for c in fetch:
+        c.start()
     peers = []
     for i in range(columns_n):
         for c in loads[i * n_parts : (i + 1) * n_parts] + cores[i * n_parts : (i + 1) * n_parts]:
@@ -693,6 +825,19 @@
             c.start()
             row.append(c)
         peers.append(row)
+        if i == STAGE_SUM:
+            office.begin(kinds, ins, outs)
+    for c in fetch:
+        c.wait()
+    tokens, width = middle_s.shape
+    slot = lax.broadcasted_iota(jnp.int32, (tokens, returned_s.shape[0]), 1)
+    takes = [(slots_ref[:, r : r + 1] == slot).astype(F32).astype(BF16) for r in range(2)]
+    for d in range(0, width, 512):
+        cols = slice(d, d + 512)
+        final = middle_s[:, cols]
+        for r in range(2):
+            final = final + gates_ref[:, r : r + 1] * dot(takes[r], returned_s[:, cols])
+        final_ref[:, cols] = final.astype(BF16)
     column = []
     total = None
     for i, f in enumerate(targets):
@@ -716,7 +861,7 @@
     office.end(kinds, ins, outs)
 
 
-def dense_sum(collective_id, parts, *jobs):
+def dense_sum(collective_id, parts, slots, gates, returned, middle, *jobs):
     sizes = tuple(lax.axis_size(a) for a in DENSE)
     hi, ep, cp = sizes
     column = hi * ep // 2
@@ -731,9 +876,13 @@
 
     return pl.pallas_call(
         functools.partial(dense_sum_kernel, sizes, kinds, len(parts)),
-        out_shape=[jax.ShapeDtypeStruct((rows, width), F32)] + shapes,
-        in_specs=[hbm] * (len(parts) + len(jobs)),
-        out_specs=[vmem] + [hbm] * len(jobs),
+        out_shape=[
+            jax.ShapeDtypeStruct((rows, width), F32),
+            jax.ShapeDtypeStruct(middle.shape, BF16),
+        ]
+        + shapes,
+        in_specs=[vmem] * 2 + [hbm] * (2 + len(parts) + len(jobs)),
+        out_specs=[vmem] * 2 + [hbm] * len(jobs),
         scratch_shapes=[
             pltpu.VMEM((column, cp, rows, width), BF16),
             pltpu.VMEM((column, cp, rows, width), BF16),
@@ -741,16 +890,18 @@
             pltpu.VMEM((column, cp - 1, rows, width), BF16),
             pltpu.VMEM((column - 1, rows, width), BF16),
             pltpu.VMEM((column - 1, rows, width), BF16),
+            pltpu.VMEM(returned.shape, BF16),
+            pltpu.VMEM(middle.shape, F32),
         ]
         + post_scratch(jobs_messages(kinds, *sizes), len(jobs))
-        + [pltpu.SemaphoreType.DMA((column * len(parts),))]
+        + [pltpu.SemaphoreType.DMA((column * len(parts),)), pltpu.SemaphoreType.DMA((2,))]
         + sems(column * len(parts))
         + sems(column * (cp - 1))
         + sems(column - 1),
         compiler_params=pltpu.CompilerParams(
             collective_id=collective_id, has_side_effects=True, vmem_limit_bytes=56 * 2**20
         ),
-    )(*(p.reshape(-1, rows, p.shape[1]) for p in parts), *arrays)
+    )(slots, gates, returned, middle, *(p.reshape(-1, rows, p.shape[1]) for p in parts), *arrays)
 
 
 def swap(x):
@@ -887,17 +1038,7 @@
             slope = sigmoid_gate * (1.0 + gate_pre * (1.0 - sigmoid_gate))
             dg_s[at, cols] = (hidden_grad * up_pre * slope).astype(BF16)
             du_s[at, cols] = (hidden_grad * swish).astype(BF16)
-        high = inner.astype(BF16)
-        rest = inner - high.astype(F32)
-        middle = rest.astype(BF16)
-        low = (rest - middle.astype(F32)).astype(BF16)
-        lane = lax.broadcasted_iota(jnp.int32, (tile, 128), 1)
-        spread = jnp.where(
-            lane == 0,
-            high.astype(F32),
-            jnp.where(lane == 1, middle.astype(F32), jnp.where(lane == 2, low.astype(F32), 0.0)),
-        )
-        inner_s[pl.ds(k0, group)] = spread.astype(BF16).reshape(group, cap, 128)
+        inner_s[pl.ds(k0, group)] = three_parts(inner).reshape(group, cap, 128)
         for d in range(0, width, 512):
             cols = slice(d, d + 512)
             back = dot(dg_s[at, :], gate_w[cols, :], 1, 1) + dot(du_s[at, :], up_w[cols, :], 1, 1)
@@ -920,7 +1061,10 @@
     here(back_s, back_ref, 0).start()
     here(inner_s, inner_ref, 1).start()
     for k in range(n):
-        gate = scale_ref[source(k)]
+        lanes = lax.broadcasted_iota(jnp.int32, (cap, 128), 1)
+        gate = jnp.sum(
+            jnp.where(lanes < 3, scale_ref[source(k)].astype(F32), 0.0), axis=1, keepdims=True
+        )
         x_s[k] = (x_s[k].astype(F32) * gate).astype(BF16)
         dy_s[k] = (dy_s[k].astype(F32) * gate).astype(BF16)
 
@@ -1040,7 +1184,6 @@
         jnp.concatenate([query_weight, key_weight, value_weight], axis=1), first_gain
     )
     second = with_extra(out_weight, router_weight, second_gain)
-    second = lax.all_gather(second, DENSE, axis=0, tiled=True)
     n_first = n_q + 2 * n_kv
 
     chosen = routes.reshape(tokens, 2)
@@ -1067,10 +1210,6 @@
         x = lax.all_to_all(x, ("cp", "ep"), split_axis=0, concat_axis=0, tiled=True)
         return x.reshape(n_slots)
 
-    out_matrix = second[:, :width]
-    router_matrix = second[:, width : width + EXPERTS]
-    gain_two = second[:, width + EXPERTS].astype(F32)
-
     grad_rows = dot(place_rows, cotangent.reshape(tokens, width)).astype(BF16)
     resid = layer_input.reshape(tokens, width).astype(F32)
     scale_one = lax.rsqrt(jnp.mean(resid * resid, axis=-1, keepdims=True) + EPS)
@@ -1078,14 +1217,21 @@
     order = jnp.arange(blocks, dtype=jnp.int32)
     table = jnp.sum(jnp.where(ids[:, :, None] == order, order[None, :, None], 0), axis=1)
     place = lax.dynamic_index_in_dim(pairing, here, axis=1, keepdims=False)
+    pick_f = picks.astype(F32)
     weights = [("expert", w) for w in (gate_weight, up_weight, down_weight)]
     if first.shape[0] % 16 == 0:
         (
             attn_in,
             queries,
             attn_out,
+            middle,
+            moe_in,
+            gates,
             kv_all,
             first,
+            second,
+            arrived,
+            arrived_gate,
             gate_matrix,
             up_matrix,
             down_matrix,
@@ -1095,41 +1241,50 @@
             table,
             place,
             layer_input.reshape(tokens, width),
+            chosen,
+            slots.T,
             first,
+            second,
             *weights,
             ("tokens", grad_rows.reshape(EXPERTS, n_seq * CAP, width)),
         )
-        grad_rows = grad_rows.reshape(n_slots, width)
+        gates = gates[:, :2]
         first = first.reshape(width, -1)
-        qkv_matrix = first[:, :n_first]
-        gain_one = first[:, n_first].astype(F32)
+        second = second.reshape(n_q, -1)
     else:
+        second = lax.all_gather(second, DENSE, axis=0, tiled=True)
         first, gate_matrix, down_matrix = courier(0, ("gather", first), weights[0], weights[2])
         first = first.reshape(width, -1)
-        qkv_matrix = first[:, :n_first]
-        gain_one = first[:, n_first].astype(F32)
-        attn_in = (resid * scale_one * gain_one).astype(BF16)
-        qkv = dot(attn_in, qkv_matrix).astype(BF16)
+        attn_in = (resid * scale_one * first[:, n_first].astype(F32)).astype(BF16)
+        qkv = dot(attn_in, first[:, :n_first]).astype(BF16)
         queries = qkv[:, :n_q]
         kv = qkv[:, n_q:].reshape(n_seq, rows, 2, n_kv).transpose(0, 2, 1, 3)
         kv_all, up_matrix = courier(1, ("peers", kv), weights[1])
         grad_rows = exchange(tie(grad_rows, kv_all))
         attn_out = tie(attend(table, place, queries, kv_all), grad_rows)
-    middle = resid + dot(attn_out, out_matrix)
+        middle = resid + dot(attn_out, second[:, :width])
+        scale_two = lax.rsqrt(jnp.mean(middle * middle, axis=-1, keepdims=True) + EPS)
+        moe_in = (middle * scale_two * second[:, width + EXPERTS].astype(F32)).astype(BF16)
+        logits = dot(moe_in, second[:, width : width + EXPERTS])
+        picked = jnp.sum(pick_f * logits[:, None, :], axis=-1)
+        powers = jnp.exp(picked - jnp.max(picked, axis=-1, keepdims=True))
+        gates = powers / jnp.sum(powers, axis=-1, keepdims=True)
+        gate_slot = jnp.sum(
+            sum(jnp.where(at_slot[r], gates[:, r][None, :], 0.0) for r in range(2)), axis=1
+        )
+        arrived = exchange(dot(place_rows, moe_in).astype(BF16))
+        rest, lanes = exchange_scalar(tie(gate_slot, arrived)), []
+        for _ in range(3):
+            lanes.append(lax.reduce_precision(rest, 8, 7))
+            rest = rest - lanes[-1]
+        arrived_gate = jnp.pad(jnp.stack(lanes, axis=1).astype(BF16), ((0, 0), (0, 125)))
+    qkv_matrix = first[:, :n_first]
+    gain_one = first[:, n_first].astype(F32)
+    out_matrix = second[:, :width]
+    router_matrix = second[:, width : width + EXPERTS]
+    gain_two = second[:, width + EXPERTS].astype(F32)
     scale_two = lax.rsqrt(jnp.mean(middle * middle, axis=-1, keepdims=True) + EPS)
-    moe_in = (middle * scale_two * gain_two).astype(BF16)
-
-    rows_out = dot(place_rows, moe_in).astype(BF16)
-    arrived = exchange(rows_out)
-    logits = dot(moe_in, router_matrix)
-    pick_f = picks.astype(F32)
-    picked = jnp.sum(pick_f * logits[:, None, :], axis=-1)
-    powers = jnp.exp(picked - jnp.max(picked, axis=-1, keepdims=True))
-    gates = powers / jnp.sum(powers, axis=-1, keepdims=True)
-    gate_slot = jnp.sum(
-        sum(jnp.where(at_slot[r], gates[:, r][None, :], 0.0) for r in range(2)), axis=1
-    )
-    gate_slot = exchange_scalar(tie(gate_slot, arrived))
+
     shape = (EXPERTS, n_seq * CAP, width)
     grad_returned, inner, produced, gate_part, up_part, down_part = expert(
         4,
@@ -1138,7 +1293,7 @@
         gate_matrix,
         up_matrix,
         down_matrix,
-        gate_slot.reshape(EXPERTS, -1, 1),
+        arrived_gate.reshape(EXPERTS, -1, 128),
     )
     grad_returned = grad_returned.reshape(n_slots, width)
     gate_inner = jnp.sum(inner[:, :, :3].astype(F32), axis=2).reshape(n_slots)
@@ -1146,9 +1301,6 @@
     down_sent = swap(down_sent)
 
     returned = exchange(tie(produced, grad_returned))
-    back = [dot(take_rows[r], returned) for r in range(2)]
-    final = middle + gates[:, :1] * back[0] + gates[:, 1:] * back[1]
-    layer_output = final.astype(BF16)
     grad_final = cotangent.reshape(tokens, width).astype(F32)
     gate_inner = jnp.stack(
         [jnp.sum(jnp.where(a, gate_inner[:, None], 0.0), axis=0) for a in at_slot], axis=1
@@ -1187,8 +1339,15 @@
         [router_part, gain_one_grad[:, None], gain_two_grad[:, None]], axis=1
     ).astype(BF16)
     small_part = jnp.pad(small_part, ((0, 0), (0, -small_part.shape[1] % 128)))
-    dense, up_parts, down_sum = dense_sum(
-        3, [first_part, out_part, small_part], ("owners", up_part), ("quad", down_sum)
+    dense, layer_output, up_parts, down_sum = dense_sum(
+        3,
+        [first_part, out_part, small_part],
+        slots,
+        gates,
+        returned,
+        middle,
+        ("owners", up_part),
+        ("quad", down_sum),
     )
     at_small = n_first + width
     return (

time: 837 us -> 769 us (0.919)
  waiting for transfers between devices: 58.4 us -> 0.01 us
  Pallas kernels: 591 us -> 645 us
  matrix products: 73.5 us -> 44.6 us
  starting transfers between devices: 35 us -> 13.9 us
  between operations: 14.7 us -> 1.41 us
    pallas_call x1, Pallas kernels: 261 us -> 345 us  [front(): pl.pallas_call(functools.partial(front_kernel, sizes, kinds), in_specs=[s...]
    all_to_all x2 -> x1, waiting for transfers between devices: 57.1 us -> 0.01 us  [exchange(): x = lax.all_to_all(x, ('cp', 'ep'), split_axis=0, concat_axis=0, tiled=True)]
    dot_general x13 -> x8, matrix products: 69 us -> 40.4 us  [dot(): lax.dot_general(a, b, (((ca,), (cb,)), ((), ())), preferred_element_type=...]
    pallas_call x1, Pallas kernels: 133 us -> 116 us  [dense_sum(): pl.pallas_call(functools.partial(dense_sum_kernel, sizes, kinds, len(part...]
    all_to_all x1 -> x0, starting transfers between devices: 16.5 us -> none  [exchange_scalar(): x = lax.all_to_all(x, ('cp', 'ep'), split_axis=0, concat_axis=0, tiled=True)]
  transfers between devices with their start and end apart: 5 -> 2, of which waited for: 2 -> 0; matrix products, arithmetic and copies ran while one was open for 6% -> 5% of each run, Pallas kernels for 45% -> 14%
where the time goes in v3:
time: 769 us; the launch traced here: 759 us
  Pallas kernels  645 us (84%)
  matrix products  44.6 us (6%)
  local copies, waits for them, and re-layouts  27.8 us (4%)
  other arithmetic  27 us (4%)
  starting transfers between devices  13.9 us (2%)
    pallas_call x1, Pallas kernels, front(): pl.pallas_call(functools.partial(front_kernel, sizes, kinds), in_specs=[s...  345 us
    pallas_call x1, Pallas kernels, dense_sum(): pl.pallas_call(functools.partial(dense_sum_kernel, sizes, kinds, len(part...  116 us
    pallas_call x1, Pallas kernels, attend_back(): pl.pallas_call(functools.partial(attend_back_kernel, sizes, kinds), grid=...  107 us
    pallas_call x1, Pallas kernels, expert(): pl.pallas_call(functools.partial(expert_kernel, sizes, 4), in_specs=[hbm]...  76.8 us
    dot_general x8, matrix products, dot(): lax.dot_general(a, b, (((ca,), (cb,)), ((), ())), preferred_element_type=...  40.4 us
  transfers between devices with their start and end apart: 2, of which 0 were waited for; matrix products, arithmetic and copies ran while one was open for 5% of the time, Pallas kernels for 14%

profile of v3, /device:TPU:0, one launch (start us, length us, event | category | flops | bytes accessed | tf_op | source)
XLA Modules:
  0.0 759.4 jit_solution(14430402813383043615)
XLA Ops:
  5.4 4.2 convolution_convert_fusion.2
  11.2 345.3 %shard_map.229 = (bf16[512,1536]{1,0:T(8,128)(2,1)}, bf16[512,1536]{1,0:T(8,128)(2,1)}, bf16[512,1536]{1,0:T(8,128)(2,1)}, f32[512,1536]{1,0:T(8,128)}, bf16[512...) custom-call(s32[2,8]{1,0:T(2,128)} %select_reduce_fusion.4.table, ...), custom_call_target="tpu_custom_call" | custom-call | flops 17179869184 | bytes 16777216 | tf_op jit(solution)/shard_map/pallas_call | solution.py:727
  356.5 76.8 %shard_map.230 = (bf16[16,96,1536]{2,1,0:T(8,128)(2,1)}, bf16[16,96,128]{2,1,0:T(8,128)(2,1)}, bf16[16,96,1536]{2,1,0:T(8,128)(2,1)}, bf16[1536,1024]{1,0:T(8,12...) custom-call(bf16[16,96,1536]{2,1,0:T(8,128)(2,1)} %get-tuple-element.45.x_hbm, ...), custom_call_target="tpu_custom_call" | custom-call | flops 17179869184 | bytes 16777216 | tf_op jit(solution)/shard_map/pallas_call | solution.py:1106
  433.3 11.7 %all-to-all-start = ((bf16[16,96,1536]{2,1,0:T(8,128)(2,1)}), bf16[16,96,1536]{2,1,0:T(8,128)(2,1)}, u32[]{:S(2)}, u32[]{:S(2)}) async-start(bf16[16,96,1536]{2,1,0:T(8,128)(2,1)} %get-tuple-element.53), calls=%async_computation | async-start | bytes 9437184 | tf_op jit(solution)/shard_map/all_to_all | solution.py:1205
  445.1 1.9 constant_dynamic-slice_fusion
  446.9 2.2 collective-permute-start
  453.0 1.8 slice_multiply_fusion
  455.9 1.9 slice.79
  459.7 4.9 convolution_multiply_fusion.1
  464.6 2.7 convolution_multiply_fusion
  467.4 2.7 multiply_reduce_fusion
  471.5 4.4 convolution_convert_fusion.1
  476.0 3.8 fusion.15.g_ref
  482.9 106.8 %shard_map.231 = (bf16[512,1536]{1,0:T(8,128)(2,1)}, bf16[4,2,2,256,512]{4,3,2,1,0:T(8,128)(2,1)}, bf16[8,192,1024]{2,1,0:T(8,128)(2,1)}) custom-call(s32[2,8]{1,0:T(2,128)} %select_reduce_fusion.4.table, s32[2,8]{1,0:T(2,128)} %copy-done.23, s32[2]{0:T(128)} %dynamic-slice_reduce_fusion.place, bf16[512,1536]{1,0:T(8,128)(2,1)} %get-tuple-element.56.q_ref, ...), custom_call_target="tpu_custom_call" | custom-call | flops 17179869184 | bytes 16777216 | tf_op jit(solution)/shard_map/pallas_call | solution.py:266
  589.6 2.7 constant_dynamic-update-slice_fusion.1
  592.3 3.0 reduce_sum.156
  597.1 10.3 %fusion.12 = (f32[512]{0:T(512)S(1)}, bf16[1536]{0:T(1024)(128)(2,1)S(1)}, f32[512,1536]{1,0:T(8,128)}) fusion(f32[1536]{0:T(1024)S(1)} %convert_reduce_fusion.3, bf16[2,1,2,128,1536]{4,3,2,1,0:T(8,128)(2,1)S(1)} %copy-done.4, f32[512]{0:T(512)S(1)} %bitcast.75, bf16[512,2560]{1,0:T(8,128)(2,1)S(1)} %constant_dynamic-update-slice_fusion, ...), kind=kOutput, calls=%fused_computation.23 | convolution fusion | flops 4032034816 | bytes 15217664 | tf_op jit(solution)/shard_map/dot_general | solution.py:28
  608.6 9.7 %convolution_convert_fusion = bf16[1536,2560]{1,0:T(8,128)(2,1)} fusion(bf16[512,1536]{1,0:T(8,128)(2,1)} %get-tuple-element.55, bf16[512,2560]{1,0:T(8,128)(2,1)} %copy-done.15), kind=kOutput, calls=%fused_computation | convolution fusion | flops 4030464000 | bytes 12058624 | tf_op jit(solution)/shard_map/dot_general | solution.py:28
  618.3 2.9 add_convert_fusion
  621.2 115.9 %shard_map.232 = (f32[48,4224]{1,0:T(8,128)}, bf16[512,1536]{1,0:T(8,128)(2,1)}, bf16[8,192,1024]{2,1,0:T(8,128)(2,1)}, bf16[4,128,1536]{2,1,0:T(8,128)(2,1)}) custom-call(s32[512,2]{1,0:T(8,128)} %copy-done.3, f32[512,2]{1,0:T(8,128)} %get-tuple-element.155.gates_ref, bf16[1536,1536]{1,0:T(8,128)(2,1)} %bitcast.10.returned_hbm, ...), custom_call_target="tpu_custom_call" | custom-call | tf_op jit(solution)/shard_map/pallas_call | solution.py:877
  737.1 1.9 fusion.34
  743.0 3.5 convert_element_type.108
  747.1 8.2 %convert_reduce_fusion = (f32[4,192,1024]{2,1,0:T(8,128)}, f32[4,192,1024]{2,1,0:T(8,128)}) fusion(bf16[2,4,192,1024]{3,2,1,0:T(8,128)(2,1)} %bitcast.61, bf16[2,4,192,1024]{3,2,1,0:T(8,128)(2,1)} %bitcast.59), kind=kLoop, calls=%fused_computation.5 | loop fusion | flops 4718592 | bytes 12582912 | tf_op jit(solution)/shard_map/reduce_sum | solution.py:1336
  755.4 2.7 fusion.11
  (129 shorter events, 26.2 us)
Async XLA Ops:
  0.7 4.6 copy-start.26
  0.7 4.7 copy-start.12
  1.7 8.0 %copy-start.9 = (s32[2,1,2,128,2]{4,3,2,0,1:T(8,128)}, s32[2,1,2,128,2]{4,3,2,0,1:T(8,128)S(1)}, u32[]{:S(2)}) copy-start(s32[2,1,2,128,2]{4,3,2,0,1:T(8,128)S(1)} %copy.88) | copy-start | bytes 12292
  2.5 7.2 copy-start.3
  4.4 5.2 copy-start.23
  5.4 5.1 copy-start.19
  5.4 5.0 copy-start.20
  5.4 5.0 copy-start.21
  433.3 11.7 %copy-start.7 = (bf16[1024,1536]{1,0:T(8,128)(2,1)S(1)}, bf16[1024,1536]{1,0:T(8,128)(2,1)}, u32[]{:S(2)}) copy-start(bf16[1024,1536]{1,0:T(8,128)(2,1)} %get-tuple-element.65) | copy-start | bytes 9437188
  433.3 158.9 %all-to-all-start = ((bf16[16,96,1536]{2,1,0:T(8,128)(2,1)}), bf16[16,96,1536]{2,1,0:T(8,128)(2,1)}, u32[]{:S(2)}, u32[]{:S(2)}) async-start(bf16[16,96,1536]{2,1,0:T(8,128)(2,1)} %get-tuple-element.53), calls=%async_computation | async-start | bytes 9437184 | tf_op jit(solution)/shard_map/all_to_all | solution.py:1205
  445.1 6.0 copy-start.6
  446.9 12.4 %copy-start = (f32[512,1536]{1,0:T(8,128)S(1)}, f32[512,1536]{1,0:T(8,128)}, u32[]{:S(2)}) copy-start(f32[512,1536]{1,0:T(8,128)} %get-tuple-element.54.middle_hbm) | copy-start | bytes 9437188
  446.9 145.3 %collective-permute-start = (bf16[512,1536]{1,0:T(8,128)(2,1)}, bf16[512,1536]{1,0:T(8,128)(2,1)}, u32[]{:S(2)}, u32[]{:S(2)}) collective-permute-start(bf16[512,1536]{1,0:T(8,128)(2,1)} %get-tuple-element.149), channel_id=1, source_target_pairs={{0,16},{16,0},{1,17},{17,1},{2,18},{18,2},{3,19},{19,3},{4,20},{20... | collective-permute-start | bytes 4718600 | tf_op jit(solution)/shard_map/ppermute | solution.py:911
  459.0 8.3 %copy-start.17 = (f32[512,16]{0,1:T(8,128)}, f32[512,16]{0,1:T(8,128)S(1)}, u32[]{:S(2)}) copy-start(f32[512,16]{0,1:T(8,128)S(1)} %select_reduce_fusion.2) | copy-start | bytes 98308
  459.4 5.2 slice-start.2
  459.7 4.9 slice-start.3
  459.7 7.7 %slice-start = ((s8[5111808]{0:T(1024)(128)(4,1)}), s8[4194304]{0:T(1024)(128)(4,1)S(1)}, s32[]{:S(2)}) async-start(s8[5111808]{0:T(1024)(128)(4,1)} %bitcast.68), calls=%async_computation.1 | async-start | bytes 8388608
  471.3 4.7 copy-start.1
  476.0 5.0 copy-start.4
  476.0 5.4 copy-start.10
  597.1 10.3 %copy-start.15 = (bf16[512,2560]{1,0:T(8,128)(2,1)}, bf16[512,2560]{1,0:T(8,128)(2,1)S(1)}, u32[]{:S(2)}) copy-start(bf16[512,2560]{1,0:T(8,128)(2,1)S(1)} %constant_dynamic-update-slice_fusion) | copy-start | bytes 7864324
  608.6 9.7 %copy-start.5 = (bf16[512,1536]{1,0:T(8,128)(2,1)S(1)}, bf16[512,1536]{1,0:T(8,128)(2,1)}, u32[]{:S(2)}) copy-start(bf16[512,1536]{1,0:T(8,128)(2,1)} %get-tuple-element.70) | copy-start | bytes 4718596
  747.1 8.3 %copy-start.2 = (f32[512,1536]{1,0:T(8,128)S(1)}, f32[512,1536]{1,0:T(8,128)}, u32[]{:S(2)}) copy-start(f32[512,1536]{1,0:T(8,128)} %copy-done.1) | copy-start | bytes 9437188
  747.1 8.3 %copy-start.8 = (f32[512,1536]{1,0:T(8,128)S(1)}, f32[512,1536]{1,0:T(8,128)}, u32[]{:S(2)}) copy-start(f32[512,1536]{1,0:T(8,128)} %get-tuple-element.157) | copy-start | bytes 9437188
  (10 other events, 31.5 us)

commit v4 on v3

--- a/solution.py
+++ b/solution.py
@@ -333,6 +333,10 @@
     return out
 
 
+def partner(me, k, n):
+    return lax.rem(me + lax.rem((k + 1) * 5, n), n)
+
+
 class PostOffice:
     def __init__(self, sizes, sems):
         self.hi, self.ep, self.cp = sizes
@@ -400,15 +404,10 @@
                     post(x, out.at[my_cp], {"cp": plus(my_cp, m, cp)})
                 keep(x, out.at[my_cp])
             elif kind == "tokens":
-                for a in range(ep):
-                    for b in range(cp):
-                        if a or b:
-                            to_ep, to_cp = plus(my_ep, a, ep), plus(my_cp, b, cp)
-                            post(
-                                x.at[to_cp * ep + to_ep],
-                                out.at[my_cp * ep + my_ep],
-                                {"ep": to_ep, "cp": to_cp},
-                            )
+                mine = my_cp * ep + my_ep
+                for k in range(ep * cp - 1):
+                    to = partner(mine, k, ep * cp)
+                    post(x.at[to], out.at[mine], {"ep": lax.rem(to, ep), "cp": to // ep})
                 keep(x.at[my_cp * ep + my_ep], out.at[my_cp * ep + my_ep])
         return away, local
 
@@ -667,7 +666,7 @@
     mine = my_cp * ep + office.my_ep
 
     def away(k, lane):
-        to = lax.rem(mine + 1 + k, count)
+        to = partner(mine, k, count)
         src, dst = ((send_s, rows_ref), (gate_s, rows_gate_ref))[lane]
         return mesh_copy(
             src.at[k],
@@ -679,7 +678,7 @@
 
     @pl.loop(0, count)
     def _(k):
-        first = lax.rem(mine + 1 + k, count) * cap
+        first = partner(mine, k, count) * cap
         ids = lax.broadcasted_iota(jnp.int32, (cap, slots_ref.shape[1]), 0) + first
         at = [slots_ref[r : r + 1, :] == ids for r in range(2)]
         chosen = jnp.where(at[0] | at[1], 1.0, 0.0).astype(BF16)
@@ -767,9 +766,6 @@
     )(table, place, x, routes, slots, shard, shard2, *arrays)
 
 
-STAGE_SUM = 0
-
-
 def dense_sum_kernel(sizes, kinds, n_parts, slots_ref, gates_ref, returned_hbm, middle_hbm, *refs):
     n = len(kinds)
     parts, refs = refs[:n_parts], refs[n_parts:]
@@ -811,6 +807,7 @@
     ]
     for c in fetch:
         c.start()
+    office.begin(kinds, ins, outs)
     peers = []
     for i in range(columns_n):
         for c in loads[i * n_parts : (i + 1) * n_parts] + cores[i * n_parts : (i + 1) * n_parts]:
@@ -825,8 +822,6 @@
             c.start()
             row.append(c)
         peers.append(row)
-        if i == STAGE_SUM:
-            office.begin(kinds, ins, outs)
     for c in fetch:
         c.wait()
     tokens, width = middle_s.shape
@@ -963,7 +958,7 @@
     me = lax.axis_index("cp") * ep + lax.axis_index("ep")
 
     def source(k):
-        return lax.rem(me + 1 + k, n)
+        return partner(me, k, n)
 
     def device(at):
         return {"cp": at // ep, "ep": lax.rem(at, ep)}

time: 769 us -> 756 us (0.983)
  no operation moved by 1% of the time
where the time goes in v4:
time: 756 us; the launch traced here: 746 us
  Pallas kernels  638 us (84%)
  matrix products  44.6 us (6%)
  local copies, waits for them, and re-layouts  27.8 us (4%)
  other arithmetic  27 us (4%)
    pallas_call x1, Pallas kernels, front(): pl.pallas_call(functools.partial(front_kernel, sizes, kinds), in_specs=[s...  342 us
    pallas_call x1, Pallas kernels, dense_sum(): pl.pallas_call(functools.partial(dense_sum_kernel, sizes, kinds, len(part...  111 us
    pallas_call x1, Pallas kernels, attend_back(): pl.pallas_call(functools.partial(attend_back_kernel, sizes, kinds), grid=...  107 us
    pallas_call x1, Pallas kernels, expert(): pl.pallas_call(functools.partial(expert_kernel, sizes, 4), in_specs=[hbm]...  77.5 us
    dot_general x8, matrix products, dot(): lax.dot_general(a, b, (((ca,), (cb,)), ((), ())), preferred_element_type=...  40.4 us
  transfers between devices with their start and end apart: 2, of which 0 were waited for; matrix products, arithmetic and copies ran while one was open for 5% of the time, Pallas kernels for 14%

profile of v4, /device:TPU:0, one launch (start us, length us, event | category | flops | bytes accessed | tf_op | source)
XLA Modules:
  0.0 746.2 jit_solution(11082054536524514002)
XLA Ops:
  5.4 4.2 convolution_convert_fusion.2
  11.2 342.1 %shard_map.229 = (bf16[512,1536]{1,0:T(8,128)(2,1)}, bf16[512,1536]{1,0:T(8,128)(2,1)}, bf16[512,1536]{1,0:T(8,128)(2,1)}, f32[512,1536]{1,0:T(8,128)}, bf16[512...) custom-call(s32[2,8]{1,0:T(2,128)} %select_reduce_fusion.4.table, ...), custom_call_target="tpu_custom_call" | custom-call | flops 17179869184 | bytes 16777216 | tf_op jit(solution)/shard_map/pallas_call | solution.py:726
  353.4 77.5 %shard_map.230 = (bf16[16,96,1536]{2,1,0:T(8,128)(2,1)}, bf16[16,96,128]{2,1,0:T(8,128)(2,1)}, bf16[16,96,1536]{2,1,0:T(8,128)(2,1)}, bf16[1536,1024]{1,0:T(8,12...) custom-call(bf16[16,96,1536]{2,1,0:T(8,128)(2,1)} %get-tuple-element.45.x_hbm, ...), custom_call_target="tpu_custom_call" | custom-call | flops 17179869184 | bytes 16777216 | tf_op jit(solution)/shard_map/pallas_call | solution.py:1101
  430.9 5.0 all-to-all-start
  436.0 1.9 constant_dynamic-slice_fusion
  437.8 2.0 collective-permute-start
  443.7 1.8 slice_multiply_fusion
  446.6 1.9 slice.79
  450.4 4.9 convolution_multiply_fusion.1
  455.3 2.7 convolution_multiply_fusion
  458.1 2.7 multiply_reduce_fusion
  462.2 4.4 convolution_convert_fusion.1
  466.7 3.8 fusion.15.g_ref
  473.5 107.5 %shard_map.231 = (bf16[512,1536]{1,0:T(8,128)(2,1)}, bf16[4,2,2,256,512]{4,3,2,1,0:T(8,128)(2,1)}, bf16[8,192,1024]{2,1,0:T(8,128)(2,1)}) custom-call(s32[2,8]{1,0:T(2,128)} %select_reduce_fusion.4.table, s32[2,8]{1,0:T(2,128)} %copy-done.23, s32[2]{0:T(128)} %dynamic-slice_reduce_fusion.place, bf16[512,1536]{1,0:T(8,128)(2,1)} %get-tuple-element.56.q_ref, ...), custom_call_target="tpu_custom_call" | custom-call | flops 17179869184 | bytes 16777216 | tf_op jit(solution)/shard_map/pallas_call | solution.py:266
  581.0 2.7 constant_dynamic-update-slice_fusion.1
  583.7 3.0 reduce_sum.156
  588.5 10.3 %fusion.12 = (f32[512]{0:T(512)S(1)}, bf16[1536]{0:T(1024)(128)(2,1)S(1)}, f32[512,1536]{1,0:T(8,128)}) fusion(f32[1536]{0:T(1024)S(1)} %convert_reduce_fusion.3, bf16[2,1,2,128,1536]{4,3,2,1,0:T(8,128)(2,1)S(1)} %copy-done.4, f32[512]{0:T(512)S(1)} %bitcast.75, bf16[512,2560]{1,0:T(8,128)(2,1)S(1)} %constant_dynamic-update-slice_fusion, ...), kind=kOutput, calls=%fused_computation.23 | convolution fusion | flops 4032034816 | bytes 15217664 | tf_op jit(solution)/shard_map/dot_general | solution.py:28
  600.0 9.7 %convolution_convert_fusion = bf16[1536,2560]{1,0:T(8,128)(2,1)} fusion(bf16[512,1536]{1,0:T(8,128)(2,1)} %get-tuple-element.55, bf16[512,2560]{1,0:T(8,128)(2,1)} %copy-done.15), kind=kOutput, calls=%fused_computation | convolution fusion | flops 4030464000 | bytes 12058624 | tf_op jit(solution)/shard_map/dot_general | solution.py:28
  609.7 2.9 add_convert_fusion
  612.6 111.3 %shard_map.232 = (f32[48,4224]{1,0:T(8,128)}, bf16[512,1536]{1,0:T(8,128)(2,1)}, bf16[8,192,1024]{2,1,0:T(8,128)(2,1)}, bf16[4,128,1536]{2,1,0:T(8,128)(2,1)}) custom-call(s32[512,2]{1,0:T(8,128)} %copy-done.3, f32[512,2]{1,0:T(8,128)} %get-tuple-element.155.gates_ref, bf16[1536,1536]{1,0:T(8,128)(2,1)} %bitcast.10.returned_hbm, ...), custom_call_target="tpu_custom_call" | custom-call | tf_op jit(solution)/shard_map/pallas_call | solution.py:872
  723.9 1.9 fusion.34
  729.8 3.5 convert_element_type.108
  733.9 8.2 %convert_reduce_fusion = (f32[4,192,1024]{2,1,0:T(8,128)}, f32[4,192,1024]{2,1,0:T(8,128)}) fusion(bf16[2,4,192,1024]{3,2,1,0:T(8,128)(2,1)} %bitcast.61, bf16[2,4,192,1024]{3,2,1,0:T(8,128)(2,1)} %bitcast.59), kind=kLoop, calls=%fused_computation.5 | loop fusion | flops 4718592 | bytes 12582912 | tf_op jit(solution)/shard_map/reduce_sum | solution.py:1331
  742.2 2.7 fusion.11
  (129 shorter events, 26.2 us)
Async XLA Ops:
  0.7 4.6 copy-start.26
  0.7 4.7 copy-start.12
  1.7 8.0 %copy-start.9 = (s32[2,1,2,128,2]{4,3,2,0,1:T(8,128)}, s32[2,1,2,128,2]{4,3,2,0,1:T(8,128)S(1)}, u32[]{:S(2)}) copy-start(s32[2,1,2,128,2]{4,3,2,0,1:T(8,128)S(1)} %copy.88) | copy-start | bytes 12292
  2.5 7.2 copy-start.3
  4.4 5.2 copy-start.23
  5.4 5.1 copy-start.19
  5.4 5.0 copy-start.20
  5.4 5.0 copy-start.21
  430.9 5.1 copy-start.7
  430.9 152.8 %all-to-all-start = ((bf16[16,96,1536]{2,1,0:T(8,128)(2,1)}), bf16[16,96,1536]{2,1,0:T(8,128)(2,1)}, u32[]{:S(2)}, u32[]{:S(2)}) async-start(bf16[16,96,1536]{2,1,0:T(8,128)(2,1)} %get-tuple-element.53), calls=%async_computation | async-start | bytes 9437184 | tf_op jit(solution)/shard_map/all_to_all | solution.py:1200
  435.9 5.8 copy-start.6
  437.8 12.2 %copy-start = (f32[512,1536]{1,0:T(8,128)S(1)}, f32[512,1536]{1,0:T(8,128)}, u32[]{:S(2)}) copy-start(f32[512,1536]{1,0:T(8,128)} %get-tuple-element.54.middle_hbm) | copy-start | bytes 9437188
  437.8 145.8 %collective-permute-start = (bf16[512,1536]{1,0:T(8,128)(2,1)}, bf16[512,1536]{1,0:T(8,128)(2,1)}, u32[]{:S(2)}, u32[]{:S(2)}) collective-permute-start(bf16[512,1536]{1,0:T(8,128)(2,1)} %get-tuple-element.149), channel_id=1, source_target_pairs={{0,16},{16,0},{1,17},{17,1},{2,18},{18,2},{3,19},{19,3},{4,20},{20... | collective-permute-start | bytes 4718600 | tf_op jit(solution)/shard_map/ppermute | solution.py:906
  449.7 8.3 %copy-start.17 = (f32[512,16]{0,1:T(8,128)}, f32[512,16]{0,1:T(8,128)S(1)}, u32[]{:S(2)}) copy-start(f32[512,16]{0,1:T(8,128)S(1)} %select_reduce_fusion.2) | copy-start | bytes 98308
  450.0 5.2 slice-start.2
  450.3 4.9 slice-start.3
  450.4 7.7 %slice-start = ((s8[5111808]{0:T(1024)(128)(4,1)}), s8[4194304]{0:T(1024)(128)(4,1)S(1)}, s32[]{:S(2)}) async-start(s8[5111808]{0:T(1024)(128)(4,1)} %bitcast.68), calls=%async_computation.1 | async-start | bytes 8388608
  462.0 4.7 copy-start.1
  466.6 5.0 copy-start.4
  466.7 5.4 copy-start.10
  588.5 10.3 %copy-start.15 = (bf16[512,2560]{1,0:T(8,128)(2,1)}, bf16[512,2560]{1,0:T(8,128)(2,1)S(1)}, u32[]{:S(2)}) copy-start(bf16[512,2560]{1,0:T(8,128)(2,1)S(1)} %constant_dynamic-update-slice_fusion) | copy-start | bytes 7864324
  600.0 9.7 %copy-start.5 = (bf16[512,1536]{1,0:T(8,128)(2,1)S(1)}, bf16[512,1536]{1,0:T(8,128)(2,1)}, u32[]{:S(2)}) copy-start(bf16[512,1536]{1,0:T(8,128)(2,1)} %get-tuple-element.70) | copy-start | bytes 4718596
  733.9 8.3 %copy-start.2 = (f32[512,1536]{1,0:T(8,128)S(1)}, f32[512,1536]{1,0:T(8,128)}, u32[]{:S(2)}) copy-start(f32[512,1536]{1,0:T(8,128)} %copy-done.1) | copy-start | bytes 9437188
  733.9 8.3 %copy-start.8 = (f32[512,1536]{1,0:T(8,128)S(1)}, f32[512,1536]{1,0:T(8,128)}, u32[]{:S(2)}) copy-start(f32[512,1536]{1,0:T(8,128)} %get-tuple-element.157) | copy-start | bytes 9437188
  (10 other events, 31.3 us)

commit v5 on v4

--- a/solution.py
+++ b/solution.py
@@ -384,13 +384,13 @@
                 rows = x.shape[1]
                 at = pl.ds(pl.multiple_of(me * rows, rows), rows)
                 for k in range(1, fsdp):
-                    to = plus(me, k, fsdp)
+                    to = plus(me, 5 * k % fsdp, fsdp)
                     post(x.at[lax.rem(to, ep)], out.at[at], self.at_fsdp(to))
                 keep(x.at[my_ep], out.at[at])
             elif kind == "owners":
                 rows = out.shape[1]
                 for k in range(1, fsdp):
-                    to = plus(me, k, fsdp)
+                    to = plus(me, 5 * k % fsdp, fsdp)
                     src = x.at[pl.ds(pl.multiple_of(to * rows, rows), rows)]
                     post(src, out.at[me], self.at_fsdp(to))
                 keep(x.at[pl.ds(pl.multiple_of(me * rows, rows), rows)], out.at[me])

time: 756 us -> 739 us (0.978)
  Pallas kernels: 638 us -> 617 us
    pallas_call x1, Pallas kernels: 342 us -> 324 us  [front(): pl.pallas_call(functools.partial(front_kernel, sizes, kinds), in_specs=[s...]
  transfers between devices with their start and end apart: 2 -> 2, of which waited for: 0 -> 0; matrix products, arithmetic and copies ran while one was open for 5% -> 5% of each run, Pallas kernels for 14% -> 15%
where the time goes in v5:
time: 739 us; the launch traced here: 730 us
  Pallas kernels  617 us (83%)
  matrix products  44.6 us (6%)
  local copies, waits for them, and re-layouts  27.8 us (4%)
  other arithmetic  27 us (4%)
  starting transfers between devices  11.9 us (2%)
    pallas_call x1, Pallas kernels, front(): pl.pallas_call(functools.partial(front_kernel, sizes, kinds), in_specs=[s...  324 us
    pallas_call x1, Pallas kernels, dense_sum(): pl.pallas_call(functools.partial(dense_sum_kernel, sizes, kinds, len(part...  112 us
    pallas_call x1, Pallas kernels, attend_back(): pl.pallas_call(functools.partial(attend_back_kernel, sizes, kinds), grid=...  107 us
    pallas_call x1, Pallas kernels, expert(): pl.pallas_call(functools.partial(expert_kernel, sizes, 4), in_specs=[hbm]...  73.9 us
    dot_general x8, matrix products, dot(): lax.dot_general(a, b, (((ca,), (cb,)), ((), ())), preferred_element_type=...  40.4 us
  transfers between devices with their start and end apart: 2, of which 0 were waited for; matrix products, arithmetic and copies ran while one was open for 5% of the time, Pallas kernels for 15%

profile of v5, /device:TPU:0, one launch (start us, length us, event | category | flops | bytes accessed | tf_op | source)
XLA Modules:
  0.0 729.6 jit_solution(5564288676979514994)
XLA Ops:
  5.4 4.2 convolution_convert_fusion.2
  11.2 323.6 %shard_map.229 = (bf16[512,1536]{1,0:T(8,128)(2,1)}, bf16[512,1536]{1,0:T(8,128)(2,1)}, bf16[512,1536]{1,0:T(8,128)(2,1)}, f32[512,1536]{1,0:T(8,128)}, bf16[512...) custom-call(s32[2,8]{1,0:T(2,128)} %select_reduce_fusion.4.table, ...), custom_call_target="tpu_custom_call" | custom-call | flops 17179869184 | bytes 16777216 | tf_op jit(solution)/shard_map/pallas_call | solution.py:726
  334.8 73.9 %shard_map.230 = (bf16[16,96,1536]{2,1,0:T(8,128)(2,1)}, bf16[16,96,128]{2,1,0:T(8,128)(2,1)}, bf16[16,96,1536]{2,1,0:T(8,128)(2,1)}, bf16[1536,1024]{1,0:T(8,12...) custom-call(bf16[16,96,1536]{2,1,0:T(8,128)(2,1)} %get-tuple-element.45.x_hbm, ...), custom_call_target="tpu_custom_call" | custom-call | flops 17179869184 | bytes 16777216 | tf_op jit(solution)/shard_map/pallas_call | solution.py:1101
  408.7 9.9 %all-to-all-start = ((bf16[16,96,1536]{2,1,0:T(8,128)(2,1)}), bf16[16,96,1536]{2,1,0:T(8,128)(2,1)}, u32[]{:S(2)}, u32[]{:S(2)}) async-start(bf16[16,96,1536]{2,1,0:T(8,128)(2,1)} %get-tuple-element.53), calls=%async_computation | async-start | bytes 9437184 | tf_op jit(solution)/shard_map/all_to_all | solution.py:1200
  418.7 1.9 constant_dynamic-slice_fusion
  420.5 2.0 collective-permute-start
  426.5 1.8 slice_multiply_fusion
  429.3 1.9 slice.79
  433.1 4.9 convolution_multiply_fusion.1
  438.0 2.7 convolution_multiply_fusion
  440.8 2.7 multiply_reduce_fusion
  445.0 4.4 convolution_convert_fusion.1
  449.4 3.8 fusion.15.g_ref
  456.3 106.9 %shard_map.231 = (bf16[512,1536]{1,0:T(8,128)(2,1)}, bf16[4,2,2,256,512]{4,3,2,1,0:T(8,128)(2,1)}, bf16[8,192,1024]{2,1,0:T(8,128)(2,1)}) custom-call(s32[2,8]{1,0:T(2,128)} %select_reduce_fusion.4.table, s32[2,8]{1,0:T(2,128)} %copy-done.23, s32[2]{0:T(128)} %dynamic-slice_reduce_fusion.place, bf16[512,1536]{1,0:T(8,128)(2,1)} %get-tuple-element.56.q_ref, ...), custom_call_target="tpu_custom_call" | custom-call | flops 17179869184 | bytes 16777216 | tf_op jit(solution)/shard_map/pallas_call | solution.py:266
  563.2 2.7 constant_dynamic-update-slice_fusion.1
  565.9 3.0 reduce_sum.156
  570.7 10.3 %fusion.12 = (f32[512]{0:T(512)S(1)}, bf16[1536]{0:T(1024)(128)(2,1)S(1)}, f32[512,1536]{1,0:T(8,128)}) fusion(f32[1536]{0:T(1024)S(1)} %convert_reduce_fusion.3, bf16[2,1,2,128,1536]{4,3,2,1,0:T(8,128)(2,1)S(1)} %copy-done.4, f32[512]{0:T(512)S(1)} %bitcast.75, bf16[512,2560]{1,0:T(8,128)(2,1)S(1)} %constant_dynamic-update-slice_fusion, ...), kind=kOutput, calls=%fused_computation.23 | convolution fusion | flops 4032034816 | bytes 15217664 | tf_op jit(solution)/shard_map/dot_general | solution.py:28
  582.2 9.7 %convolution_convert_fusion = bf16[1536,2560]{1,0:T(8,128)(2,1)} fusion(bf16[512,1536]{1,0:T(8,128)(2,1)} %get-tuple-element.55, bf16[512,2560]{1,0:T(8,128)(2,1)} %copy-done.15), kind=kOutput, calls=%fused_computation | convolution fusion | flops 4030464000 | bytes 12058624 | tf_op jit(solution)/shard_map/dot_general | solution.py:28
  591.9 2.9 add_convert_fusion
  594.8 112.5 %shard_map.232 = (f32[48,4224]{1,0:T(8,128)}, bf16[512,1536]{1,0:T(8,128)(2,1)}, bf16[8,192,1024]{2,1,0:T(8,128)(2,1)}, bf16[4,128,1536]{2,1,0:T(8,128)(2,1)}) custom-call(s32[512,2]{1,0:T(8,128)} %copy-done.3, f32[512,2]{1,0:T(8,128)} %get-tuple-element.155.gates_ref, bf16[1536,1536]{1,0:T(8,128)(2,1)} %bitcast.10.returned_hbm, ...), custom_call_target="tpu_custom_call" | custom-call | tf_op jit(solution)/shard_map/pallas_call | solution.py:872
  707.3 1.9 fusion.34
  713.2 3.5 convert_element_type.108
  717.3 8.2 %convert_reduce_fusion = (f32[4,192,1024]{2,1,0:T(8,128)}, f32[4,192,1024]{2,1,0:T(8,128)}) fusion(bf16[2,4,192,1024]{3,2,1,0:T(8,128)(2,1)} %bitcast.61, bf16[2,4,192,1024]{3,2,1,0:T(8,128)(2,1)} %bitcast.59), kind=kLoop, calls=%fused_computation.5 | loop fusion | flops 4718592 | bytes 12582912 | tf_op jit(solution)/shard_map/reduce_sum | solution.py:1331
  725.6 2.7 fusion.11
  (129 shorter events, 26.2 us)
Async XLA Ops:
  0.7 4.6 copy-start.26
  0.7 4.7 copy-start.12
  1.7 8.0 %copy-start.9 = (s32[2,1,2,128,2]{4,3,2,0,1:T(8,128)}, s32[2,1,2,128,2]{4,3,2,0,1:T(8,128)S(1)}, u32[]{:S(2)}) copy-start(s32[2,1,2,128,2]{4,3,2,0,1:T(8,128)S(1)} %copy.88) | copy-start | bytes 12292
  2.5 7.2 copy-start.3
  4.4 5.2 copy-start.23
  5.4 5.1 copy-start.19
  5.4 5.0 copy-start.20
  5.4 5.0 copy-start.21
  408.7 10.0 %copy-start.7 = (bf16[1024,1536]{1,0:T(8,128)(2,1)S(1)}, bf16[1024,1536]{1,0:T(8,128)(2,1)}, u32[]{:S(2)}) copy-start(bf16[1024,1536]{1,0:T(8,128)(2,1)} %get-tuple-element.65) | copy-start | bytes 9437188
  408.7 157.2 %all-to-all-start = ((bf16[16,96,1536]{2,1,0:T(8,128)(2,1)}), bf16[16,96,1536]{2,1,0:T(8,128)(2,1)}, u32[]{:S(2)}, u32[]{:S(2)}) async-start(bf16[16,96,1536]{2,1,0:T(8,128)(2,1)} %get-tuple-element.53), calls=%async_computation | async-start | bytes 9437184 | tf_op jit(solution)/shard_map/all_to_all | solution.py:1200
  418.7 5.8 copy-start.6
  420.5 12.2 %copy-start = (f32[512,1536]{1,0:T(8,128)S(1)}, f32[512,1536]{1,0:T(8,128)}, u32[]{:S(2)}) copy-start(f32[512,1536]{1,0:T(8,128)} %get-tuple-element.54.middle_hbm) | copy-start | bytes 9437188
  420.5 145.3 %collective-permute-start = (bf16[512,1536]{1,0:T(8,128)(2,1)}, bf16[512,1536]{1,0:T(8,128)(2,1)}, u32[]{:S(2)}, u32[]{:S(2)}) collective-permute-start(bf16[512,1536]{1,0:T(8,128)(2,1)} %get-tuple-element.149), channel_id=1, source_target_pairs={{0,16},{16,0},{1,17},{17,1},{2,18},{18,2},{3,19},{19,3},{4,20},{20... | collective-permute-start | bytes 4718600 | tf_op jit(solution)/shard_map/ppermute | solution.py:906
  432.4 8.3 %copy-start.17 = (f32[512,16]{0,1:T(8,128)}, f32[512,16]{0,1:T(8,128)S(1)}, u32[]{:S(2)}) copy-start(f32[512,16]{0,1:T(8,128)S(1)} %select_reduce_fusion.2) | copy-start | bytes 98308
  432.8 5.2 slice-start.2
  433.1 4.9 slice-start.3
  433.1 7.7 %slice-start = ((s8[5111808]{0:T(1024)(128)(4,1)}), s8[4194304]{0:T(1024)(128)(4,1)S(1)}, s32[]{:S(2)}) async-start(s8[5111808]{0:T(1024)(128)(4,1)} %bitcast.68), calls=%async_computation.1 | async-start | bytes 8388608
  444.7 4.7 copy-start.1
  449.4 5.0 copy-start.4
  449.4 5.4 copy-start.10
  570.7 10.3 %copy-start.15 = (bf16[512,2560]{1,0:T(8,128)(2,1)}, bf16[512,2560]{1,0:T(8,128)(2,1)S(1)}, u32[]{:S(2)}) copy-start(bf16[512,2560]{1,0:T(8,128)(2,1)S(1)} %constant_dynamic-update-slice_fusion) | copy-start | bytes 7864324
  582.2 9.7 %copy-start.5 = (bf16[512,1536]{1,0:T(8,128)(2,1)S(1)}, bf16[512,1536]{1,0:T(8,128)(2,1)}, u32[]{:S(2)}) copy-start(bf16[512,1536]{1,0:T(8,128)(2,1)} %get-tuple-element.70) | copy-start | bytes 4718596
  717.3 8.3 %copy-start.2 = (f32[512,1536]{1,0:T(8,128)S(1)}, f32[512,1536]{1,0:T(8,128)}, u32[]{:S(2)}) copy-start(f32[512,1536]{1,0:T(8,128)} %copy-done.1) | copy-start | bytes 9437188
  717.3 8.3 %copy-start.8 = (f32[512,1536]{1,0:T(8,128)S(1)}, f32[512,1536]{1,0:T(8,128)}, u32[]{:S(2)}) copy-start(f32[512,1536]{1,0:T(8,128)} %get-tuple-element.157) | copy-start | bytes 9437188
  (10 other events, 31.4 us)
